TPU v7x, 256 devices: a whole 4x4x8 slice. The times are simulated.
256 devices in a mesh: slab: 64 (over x, z, core), sub: 4 (over y).
Axes of the slice: x: 4, y: 4, z: 8, core: 2. Of those that a mesh axis runs over, the one named last changes fastest.
Arguments:
- charge_grid: float32 [512, 256, 512], P('slab', 'sub'), may hold values from -6 to 6
- atom_offset: float32 [3, 4194304], P(None, ('slab', 'sub')), may hold values from 0 to 8
- block_cell: int32 [32768], P(('slab', 'sub')), may hold values from 0 to 511
- block_count: int32 [32768], P(('slab', 'sub')), may hold values from 0 to 128, as said below
Outputs:
- atom_field: float32 [4, 4194304], P(None, ('slab', 'sub'))
Inputs may be any that keep to these rules, and one draw needn't show every extreme that they name: `block_count`: on each device the blocks that hold atoms come first, and its first block holds 128 atoms; a block's atoms fill its lowest slots. Some device has atoms in all 128 blocks and some in only 32.
All inputs are finite; a program needn't handle non-finite values.
Results may differ from a plain program's by a relative error of at most 0.0003.
Values sent between devices are 32-bit elements; how exact they have to be, the bound alone decides.
No kernel may reach another device: no remote copies, remote signals or barrier semaphores. Data moves between devices by JAX's collectives and lax.ppermute only.
A program may use at most 128 MiB of HBM per device.

v0:
```python
import math

import jax
import jax.numpy as jnp
from jax import lax
from jax.sharding import PartitionSpec as P

SLOT = 128
BRICK = 8


TAPS = (0.125, 0.5, 0.75, 0.5, 0.125)
SPANS = (2.0, 8.0, 32.0)
NEAR_WEIGHT = 0.5
HIGH = lax.Precision.HIGHEST


def with_halo(block, sides, width):
    for axis, dim in sides:
        count = lax.axis_size(axis)
        forward = [(i, i + 1) for i in range(count - 1)]
        backward = [(target, source) for source, target in forward]
        low = lax.ppermute(
            lax.slice_in_dim(block, block.shape[dim] - width, None, axis=dim), axis, forward
        )
        high = lax.ppermute(lax.slice_in_dim(block, 0, width, axis=dim), axis, backward)
        block = jnp.concatenate([low, block, high], axis=dim)
    return block


def pad_along(values, axis, width):
    widths = [(0, 0)] * values.ndim
    widths[axis] = (width, width)
    return jnp.pad(values, widths)


def restrict_axis(values, axis, halo_width, margin, coarse_own):
    length = 2 * (coarse_own + 2 * margin - 1) + 1
    total = None
    for offset in range(5):
        start = halo_width - 2 * margin + offset - 2
        term = TAPS[offset] * lax.slice_in_dim(values, start, start + length, 2, axis)
        total = term if total is None else total + term
    return total


def prolong_axis(values, axis, halo_width, margin, coarse_own):
    base = halo_width - margin // 2
    count = coarse_own + margin

    def take(start):
        return lax.slice_in_dim(values, start, start + count, 1, axis)

    even = 0.125 * take(base - 1) + 0.75 * take(base) + 0.125 * take(base + 1)
    odd = 0.5 * take(base) + 0.5 * take(base + 1)
    joined = jnp.stack([even, odd], axis=axis + 1)
    shape = list(even.shape)
    shape[axis] = 2 * count
    return joined.reshape(shape)


def smooth_axis(values, axis, halo_width, margin, own):
    total = None
    for offset in range(5):
        weight = math.exp(-0.5 * (offset - 2) ** 2)
        start = halo_width - margin + offset - 2
        term = weight * lax.slice_in_dim(values, start, start + own + 2 * margin, 1, axis)
        total = term if total is None else total + term
    return total


def gauss_rows(row_index, count, span):
    diff = row_index.astype(jnp.float32)[:, None] - jnp.arange(count).astype(jnp.float32)[None, :]
    return jnp.exp(-((diff / span) ** 2))


def spline(shifted):
    at = jnp.abs(shifted)
    inner = 2.0 / 3.0 - at * at + 0.5 * at * at * at
    outer = jnp.maximum(2.0 - at, 0.0)
    return jnp.where(at < 1.0, inner, outer * outer * outer / 6.0)


def spline_slope(shifted):
    at = jnp.abs(shifted)
    inner = -2.0 * shifted + 1.5 * shifted * at
    outer = jnp.maximum(2.0 - at, 0.0)
    return jnp.where(at < 1.0, inner, -0.5 * outer * outer * jnp.sign(shifted))


def interpolate(patches, offsets, counts):
    grid_index = jnp.arange(patches.shape[1]).astype(offsets.dtype)
    shifted = offsets[:, :, None, :] + 2.0 - grid_index[None, None, :, None]
    weights = spline(shifted)
    slopes = spline_slope(shifted)
    paired = jnp.stack([weights[2], slopes[2]], axis=2)
    inner = jnp.einsum("gkji,gica->gkjca", patches, paired, precision=HIGH)
    base = inner[:, :, :, 0]
    along_x = inner[:, :, :, 1]
    value = jnp.einsum("gkja,gka,gja->ga", base, weights[0], weights[1], precision=HIGH)
    field_z = -jnp.einsum("gkja,gka,gja->ga", base, slopes[0], weights[1], precision=HIGH)
    field_y = -jnp.einsum("gkja,gka,gja->ga", base, weights[0], slopes[1], precision=HIGH)
    field_x = -jnp.einsum("gkja,gka,gja->ga", along_x, weights[0], weights[1], precision=HIGH)
    live = (jnp.arange(offsets.shape[2], dtype=jnp.int32)[None, :] < counts[:, None]).astype(
        offsets.dtype
    )
    return jnp.stack([value, field_z, field_y, field_x]) * live[None]


def brick_windows(values, axis, brick_count, patch_size):
    pieces = [
        lax.slice_in_dim(values, start, start + BRICK * (brick_count - 1) + 1, BRICK, axis)
        for start in range(patch_size)
    ]
    return jnp.stack(pieces, axis=-1)


def on_device(charge_grid, atom_offset, block_cell, block_count):
    depth, rows_own, width_x = charge_grid.shape
    slab_count = lax.axis_size("slab")
    sub_count = lax.axis_size("sub")
    slab_index = lax.axis_index("slab")
    sub_index = lax.axis_index("sub")
    rim_width = 2
    charged = with_halo(charge_grid, (("slab", 0), ("sub", 1)), rim_width)
    charged = pad_along(charged, 2, rim_width)
    coarse = restrict_axis(charged, 0, rim_width, 0, depth // 2)
    coarse = restrict_axis(coarse, 1, rim_width, 0, rows_own // 2)
    coarse = restrict_axis(coarse, 2, rim_width, 0, width_x // 2)
    coarse = with_halo(coarse, (("slab", 0), ("sub", 1)), 2)
    coarse = pad_along(coarse, 2, 2)
    top = restrict_axis(coarse, 0, 2, 0, depth // 4)
    top = restrict_axis(top, 1, 2, 0, rows_own // 4)
    top = restrict_axis(top, 2, 2, 0, width_x // 4)
    planes_top, rows_top, width_top = top.shape
    plane_rows = slab_index * planes_top + jnp.arange(planes_top)
    row_rows = sub_index * rows_top + jnp.arange(rows_top)
    z_kernel = jnp.stack(
        [span ** (-1.5) * gauss_rows(plane_rows, planes_top * slab_count, span) for span in SPANS]
    )
    y_kernel = jnp.stack([gauss_rows(row_rows, rows_top * sub_count, span) for span in SPANS])
    x_kernel = jnp.stack([gauss_rows(jnp.arange(width_top), width_top, span) for span in SPANS])
    gathered = lax.all_gather(top, "sub", axis=1, tiled=True)
    mixed = jnp.einsum(
        "mbj,ijk->mibk",
        y_kernel,
        lax.all_gather(gathered, "slab", axis=0, tiled=True),
        precision=HIGH,
    )
    folded = jnp.einsum("mai,mibk->mabk", z_kernel, mixed, precision=HIGH)
    top_potential = jnp.einsum("mck,mabk->abc", x_kernel, folded, precision=HIGH)
    mid_planes = depth // 2
    mid_rows = rows_own // 2
    widened = with_halo(top_potential, (("slab", 0), ("sub", 1)), 1)
    middle = prolong_axis(widened, 0, 1, 0, planes_top)
    middle = prolong_axis(middle, 1, 1, 0, rows_top)
    middle = prolong_axis(pad_along(middle, 2, 1), 2, 1, 0, width_top)
    middle = with_halo(middle, (("slab", 0), ("sub", 1)), 1)
    fine = prolong_axis(middle, 0, 1, 0, mid_planes)
    fine = prolong_axis(fine, 1, 1, 0, mid_rows)
    fine = prolong_axis(pad_along(fine, 2, 1), 2, 1, 0, width_x // 2)
    near = smooth_axis(charged, 0, rim_width, 0, depth)
    near = smooth_axis(near, 1, rim_width, 0, rows_own)
    near = smooth_axis(near, 2, rim_width, 0, width_x)
    fine = with_halo(fine + NEAR_WEIGHT * near, (("slab", 0), ("sub", 1)), 2)
    fine = pad_along(fine, 2, 2)
    patch_size = BRICK + 4
    bricks_z = depth // BRICK
    bricks_y = rows_own // BRICK
    bricks_x = width_x // BRICK
    table = brick_windows(fine, 0, bricks_z, patch_size)
    table = brick_windows(table, 1, bricks_y, patch_size)
    table = brick_windows(table, 2, bricks_x, patch_size)
    table = table.reshape(bricks_z * bricks_y * bricks_x, patch_size * patch_size * patch_size)
    blocks = block_cell.shape[0]
    group_blocks = min(64, blocks)
    groups = blocks // group_blocks
    offsets = atom_offset.reshape(3, groups, group_blocks, SLOT).transpose(1, 0, 2, 3)

    def one_group(items):
        cell_part, offset_part, count_part = items
        patches = jnp.take(table, cell_part, axis=0).reshape(
            group_blocks, patch_size, patch_size, patch_size
        )
        return interpolate(patches, offset_part, count_part)

    fields = lax.map(
        one_group,
        (
            block_cell.reshape(groups, group_blocks),
            offsets,
            block_count.reshape(groups, group_blocks),
        ),
    )
    return fields.transpose(1, 0, 2, 3).reshape(4, blocks * SLOT)


def solution(mesh):
    placed = (
        P("slab", "sub", None),
        P(None, ("slab", "sub")),
        P(("slab", "sub")),
        P(("slab", "sub")),
    )
    return jax.shard_map(
        on_device, mesh=mesh, in_specs=placed, out_specs=P(None, ("slab", "sub")), check_vma=False
    )
```

profile of v0, /device:TPU:2, one launch (start us, length us, event | category | flops | bytes accessed | tf_op | source)
XLA Modules:
  0.0 617.1 jit_solution(17157237268042803040)
XLA Ops:
  9.6 7.2 %collective-permute-start.1 = (f32[2,64,512]{2,1,0:T(8,128)S(1)}, f32[2,64,512]{2,1,0:T(8,128)S(1)}, u32[]{:S(2)}, u32[]{:S(2)}) collective-permute-start(f32[2,64,512]{2,1,0:T(8,128)S(1)} %get-tuple-element.118), channel_id=1, source_target_pairs={{4,0},{8,4},{12,8},{16,12},{20,16},{24,20},{28,24},{32,28},{36,32}... | collective-permute-start | bytes 786440 | tf_op jit(solution)/shard_map/ppermute | solution.py:26
  20.8 3.5 collective-permute-start.2
  26.0 4.3 collective-permute-done.3
  30.5 3.9 copy.240
  34.4 4.5 pad.19
  38.8 9.6 %slice.415 = f32[4,68,516]{1,0,2:T(4,128)S(1)} slice(f32[12,68,516]{1,0,2:T(8,128)} %pad.19), slice={[0:7:2], [0:68:1], [0:516:1]} | slice | bytes 1122816 | tf_op jit(solution)/shard_map/slice | solution.py:42
  48.4 10.2 %slice.416 = f32[4,68,516]{1,0,2:T(4,128)S(1)} slice(f32[12,68,516]{1,0,2:T(8,128)} %pad.19), slice={[1:8:2], [0:68:1], [0:516:1]} | slice | bytes 1122816 | tf_op jit(solution)/shard_map/slice | solution.py:42
  58.6 11.1 %slice.417 = f32[4,68,516]{1,0,2:T(4,128)} slice(f32[12,68,516]{1,0,2:T(8,128)} %pad.19), slice={[2:9:2], [0:68:1], [0:516:1]} | slice | bytes 1122816 | tf_op jit(solution)/shard_map/slice | solution.py:42
  69.8 11.2 %slice.418 = f32[4,68,516]{1,0,2:T(4,128)} slice(f32[12,68,516]{1,0,2:T(8,128)} %pad.19), slice={[3:10:2], [0:68:1], [0:516:1]} | slice | bytes 1122816 | tf_op jit(solution)/shard_map/slice | solution.py:42
  80.9 11.2 %slice.419 = f32[4,68,516]{1,0,2:T(4,128)} slice(f32[12,68,516]{1,0,2:T(8,128)} %pad.19), slice={[4:11:2], [0:68:1], [0:516:1]} | slice | bytes 1122816 | tf_op jit(solution)/shard_map/slice | solution.py:42
  94.8 11.8 %slice.420 = f32[4,32,516]{1,0,2:T(4,128)S(1)} slice(f32[4,68,516]{1,0,2:T(4,128)S(1)} %multiply_add_fusion.2), slice={[0:4:1], [0:63:2], [0:516:1]} | slice | bytes 528384 | tf_op jit(solution)/shard_map/slice | solution.py:42
  106.6 12.1 %slice.421 = f32[4,32,516]{1,0,2:T(4,128)S(1)} slice(f32[4,68,516]{1,0,2:T(4,128)S(1)} %multiply_add_fusion.2), slice={[0:4:1], [1:64:2], [0:516:1]} | slice | bytes 528384 | tf_op jit(solution)/shard_map/slice | solution.py:42
  118.7 12.2 %slice.422 = f32[4,32,516]{1,0,2:T(4,128)} slice(f32[4,68,516]{1,0,2:T(4,128)S(1)} %multiply_add_fusion.2), slice={[0:4:1], [2:65:2], [0:516:1]} | slice | bytes 528384 | tf_op jit(solution)/shard_map/slice | solution.py:42
  130.9 12.2 %slice.423 = f32[4,32,516]{1,0,2:T(4,128)} slice(f32[4,68,516]{1,0,2:T(4,128)S(1)} %multiply_add_fusion.2), slice={[0:4:1], [3:66:2], [0:516:1]} | slice | bytes 528384 | tf_op jit(solution)/shard_map/slice | solution.py:42
  143.1 12.2 %slice.424 = f32[4,32,516]{1,0,2:T(4,128)} slice(f32[4,68,516]{1,0,2:T(4,128)S(1)} %multiply_add_fusion.2), slice={[0:4:1], [4:67:2], [0:516:1]} | slice | bytes 528384 | tf_op jit(solution)/shard_map/slice | solution.py:42
  160.3 5.8 collective-permute-start.5
  171.1 3.5 collective-permute-start.6
  176.8 3.8 collective-permute-done.7
  186.5 11.9 %all_gather.6 = f32[2,64,128]{2,0,1:T(2,128)S(1)} all-gather(f32[2,16,128]{2,0,1:T(2,128)S(1)} %multiply_add_fusion.6), channel_id=1, replica_groups=mesh['slab'=64,'sub'=4] {'sub'}, dimensions={1}, use_global_device_ids=true | all-gather | bytes 81920 | tf_op jit(solution)/shard_map/all_gather | solution.py:143
  199.4 75.7 %all-gather.2.cloned.1.call-done = f32[128,64,128]{2,1,0:T(8,128)} async-done(((f32[2,64,128]{2,1,0:T(8,128)}), f32[128,64,128]{2,1,0:T(8,128)}) %all-gather.2.cloned.1.call-update) | async-done | bytes 4194320 | tf_op jit(solution)/shard_map/all_gather | solution.py:147
  275.1 9.2 %copy.337 = f32[128,64,128,1]{1,0,3,2:T(8,128)} copy(f32[128,64,128,1]{2,1,0,3:T(8,128)} %bitcast.318) | data formatting | bytes 8388608 | tf_op jit(solution)/shard_map/all_gather | solution.py:147
  284.2 11.7 %convolution_bitcast_fusion = f32[3,128,16,128]{1,2,0,3:T(8,128)S(1)} fusion(f32[128,64,128,1]{1,0,3,2:T(8,128)} %copy.337, f32[1,16,64]{2,1,0:T(8,128)S(1)} %get-tuple-element.146, f32[1,16,64]{2,1,0:T(8,128)S(1)} %get-tuple-element.147, f32[1,16,64]{2,1,0:T(8,128)S(1)} %get-tuple-element.145), kind=kOutput, calls=%fused_computation.90 | convolution fusion | flops 603985920 | bytes 7352320 | tf_op jit(solution)/shard_map/mbj,ijk->mibk/dot_general | solution.py:144
  301.7 5.5 collective-permute-start.9
  308.6 3.4 collective-permute-start.10
  320.0 5.8 collective-permute-start.13
  328.3 3.4 collective-permute-start.14
  333.2 3.6 fusion.28
  346.9 5.8 collective-permute-start.17
  359.6 4.1 collective-permute-start.18
  365.9 3.8 collective-permute-done.19
  388.6 11.3 %slice.518 = f32[1,8,64,12,12]{2,1,4,3,0:T(8,128)} slice(f32[1,8,516,12,12]{2,1,4,3,0:T(8,128)S(1)} %bitcast_dynamic-update-slice_fusion.12), slice={[0:1:1], [0:8:1], [0:505:8], [0:12:1], [0:12:1]} | slice | bytes 589824 | tf_op jit(solution)/shard_map/slice | solution.py:112
  399.8 11.4 %slice.519 = f32[1,8,64,12,12]{2,1,4,3,0:T(8,128)} slice(f32[1,8,516,12,12]{2,1,4,3,0:T(8,128)S(1)} %bitcast_dynamic-update-slice_fusion.12), slice={[0:1:1], [0:8:1], [1:506:8], [0:12:1], [0:12:1]} | slice | bytes 589824 | tf_op jit(solution)/shard_map/slice | solution.py:112
  411.2 11.2 %slice.520 = f32[1,8,64,12,12]{2,1,4,3,0:T(8,128)} slice(f32[1,8,516,12,12]{2,1,4,3,0:T(8,128)S(1)} %bitcast_dynamic-update-slice_fusion.12), slice={[0:1:1], [0:8:1], [2:507:8], [0:12:1], [0:12:1]} | slice | bytes 589824 | tf_op jit(solution)/shard_map/slice | solution.py:112
  422.5 11.4 %slice.521 = f32[1,8,64,12,12]{2,1,4,3,0:T(8,128)} slice(f32[1,8,516,12,12]{2,1,4,3,0:T(8,128)S(1)} %bitcast_dynamic-update-slice_fusion.12), slice={[0:1:1], [0:8:1], [3:508:8], [0:12:1], [0:12:1]} | slice | bytes 589824 | tf_op jit(solution)/shard_map/slice | solution.py:112
  433.8 11.2 %slice.522 = f32[1,8,64,12,12]{2,1,4,3,0:T(8,128)} slice(f32[1,8,516,12,12]{2,1,4,3,0:T(8,128)S(1)} %bitcast_dynamic-update-slice_fusion.12), slice={[0:1:1], [0:8:1], [4:509:8], [0:12:1], [0:12:1]} | slice | bytes 589824 | tf_op jit(solution)/shard_map/slice | solution.py:112
  445.1 11.4 %slice.523 = f32[1,8,64,12,12]{2,1,4,3,0:T(8,128)} slice(f32[1,8,516,12,12]{2,1,4,3,0:T(8,128)S(1)} %bitcast_dynamic-update-slice_fusion.12), slice={[0:1:1], [0:8:1], [5:510:8], [0:12:1], [0:12:1]} | slice | bytes 589824 | tf_op jit(solution)/shard_map/slice | solution.py:112
  456.5 11.2 %slice.524 = f32[1,8,64,12,12]{2,1,4,3,0:T(8,128)} slice(f32[1,8,516,12,12]{2,1,4,3,0:T(8,128)S(1)} %bitcast_dynamic-update-slice_fusion.12), slice={[0:1:1], [0:8:1], [6:511:8], [0:12:1], [0:12:1]} | slice | bytes 589824 | tf_op jit(solution)/shard_map/slice | solution.py:112
  467.7 11.4 %slice.525 = f32[1,8,64,12,12]{2,1,4,3,0:T(8,128)} slice(f32[1,8,516,12,12]{2,1,4,3,0:T(8,128)S(1)} %bitcast_dynamic-update-slice_fusion.12), slice={[0:1:1], [0:8:1], [7:512:8], [0:12:1], [0:12:1]} | slice | bytes 589824 | tf_op jit(solution)/shard_map/slice | solution.py:112
  479.2 11.4 %slice.526 = f32[1,8,64,12,12]{2,1,4,3,0:T(8,128)} slice(f32[1,8,516,12,12]{2,1,4,3,0:T(8,128)S(1)} %bitcast_dynamic-update-slice_fusion.12), slice={[0:1:1], [0:8:1], [8:513:8], [0:12:1], [0:12:1]} | slice | bytes 589824 | tf_op jit(solution)/shard_map/slice | solution.py:112
  490.6 11.3 %slice.527 = f32[1,8,64,12,12]{2,1,4,3,0:T(8,128)} slice(f32[1,8,516,12,12]{2,1,4,3,0:T(8,128)S(1)} %bitcast_dynamic-update-slice_fusion.12), slice={[0:1:1], [0:8:1], [9:514:8], [0:12:1], [0:12:1]} | slice | bytes 589824 | tf_op jit(solution)/shard_map/slice | solution.py:112
  501.9 11.4 %slice.528 = f32[1,8,64,12,12]{2,1,4,3,0:T(8,128)} slice(f32[1,8,516,12,12]{2,1,4,3,0:T(8,128)S(1)} %bitcast_dynamic-update-slice_fusion.12), slice={[0:1:1], [0:8:1], [10:515:8], [0:12:1], [0:12:1]} | slice | bytes 589824 | tf_op jit(solution)/shard_map/slice | solution.py:112
  513.3 10.7 %slice.529 = f32[1,8,64,12,12]{2,1,4,3,0:T(8,128)S(1)} slice(f32[1,8,516,12,12]{2,1,4,3,0:T(8,128)S(1)} %bitcast_dynamic-update-slice_fusion.12), slice={[0:1:1], [0:8:1], [11:516:8], [0:12:1], [0:12:1]} | slice | bytes 589824 | tf_op jit(solution)/shard_map/slice | solution.py:112
  537.7 5.3 reshape.686
  546.1 62.1 %while.10 = (s32[]{:T(128)}, f32[2,4,64,128]{3,2,1,0:T(8,128)}, f32[2,3,64,128]{3,2,0,1:T(8,128)}, s32[2,64]{1,0:T(2,128)S(1)}, f32[512,1728]{1,0:T(8,128)}, /*index=5*/s32[2,64]{1,0:T(2,128)S(1)}, s32[]{:T(128)}) while((s32[]{:T(128)}, f32[2,4,64,128]{3,2,1,0:T(8,128)}, f32[2,3,64,128]{3,2,0,1:T(8,128)}, s32[2,64]{1,0:T(2,128)S(1)}, ...), condition=%wide.region_1.2_spmd, body=%wide.region_0.1_spmd.sunk | while | flops 354858560 | bytes 44882408 | solution.py:187
  553.7 6.1 copy.371
  559.9 12.7 %fusion.137 = f32[64,12,12,2,128]{4,2,3,1,0:T(8,128)S(1)} fusion(f32[64,12,12,12,1]{3,2,4,1,0:T(8,128)} %copy.371, f32[64,12,1,128]{3,1,2,0:T(8,128)S(1)} %get-tuple-element.205, f32[64,12,1,128]{3,1,2,0:T(8,128)S(1)} %get-tuple-element.206), kind=kOutput, calls=%fused_computation.30.clone.1 | convolution fusion | flops 339935232 | bytes 10665984 | tf_op jit(solution)/shard_map/while/body/eval_jaxpr/gkji,gica->gkjca/dot_general | solution.py:97
  584.7 6.1 copy.371
  590.8 12.7 %fusion.137 = f32[64,12,12,2,128]{4,2,3,1,0:T(8,128)S(1)} fusion(f32[64,12,12,12,1]{3,2,4,1,0:T(8,128)} %copy.371, f32[64,12,1,128]{3,1,2,0:T(8,128)S(1)} %get-tuple-element.205, f32[64,12,1,128]{3,1,2,0:T(8,128)S(1)} %get-tuple-element.206), kind=kOutput, calls=%fused_computation.30.clone.1 | convolution fusion | flops 339935232 | bytes 10665984 | tf_op jit(solution)/shard_map/while/body/eval_jaxpr/gkji,gica->gkjca/dot_general | solution.py:97
  (259 shorter events, 129.9 us)
Async XLA Ops:
  6.5 12.4 %copy-start.7 = (f32[8,64,512]{2,1,0:T(8,128)S(1)}, f32[8,64,512]{2,1,0:T(8,128)}, u32[]{:S(2)}) copy-start(f32[8,64,512]{2,1,0:T(8,128)} %param.6) | copy-start | bytes 3145732
  6.5 268.6 %all-gather.2.cloned.1.call-start = ((), (), s32[]{:S(2)}) async-start(), calls=%async_computation | async-start | bytes 4259840 | tf_op jit(solution)/shard_map/all_gather | solution.py:147
  7.7 11.2 %collective-permute-start = (f32[2,64,512]{2,1,0:T(8,128)S(1)}, f32[2,64,512]{2,1,0:T(8,128)S(1)}, u32[]{:S(2)}, u32[]{:S(2)}) collective-permute-start(f32[2,64,512]{2,1,0:T(8,128)S(1)} %get-tuple-element.119), channel_id=1, source_target_pairs={{0,4},{4,8},{8,12},{12,16},{16,20},{20,24},{24,28},{28,32},{32,36}... | collective-permute-start | bytes 786440 | tf_op jit(solution)/shard_map/ppermute | solution.py:23
  9.6 11.1 %collective-permute-start.1 = (f32[2,64,512]{2,1,0:T(8,128)S(1)}, f32[2,64,512]{2,1,0:T(8,128)S(1)}, u32[]{:S(2)}, u32[]{:S(2)}) collective-permute-start(f32[2,64,512]{2,1,0:T(8,128)S(1)} %get-tuple-element.118), channel_id=1, source_target_pairs={{4,0},{8,4},{12,8},{16,12},{20,16},{24,20},{28,24},{32,28},{36,32}... | collective-permute-start | bytes 786440 | tf_op jit(solution)/shard_map/ppermute | solution.py:26
  20.8 5.2 collective-permute-start.2
  24.2 6.0 collective-permute-start.3
  158.4 9.8 %collective-permute-start.4 = (f32[2,32,256]{1,0,2:T(2,128)S(1)}, f32[2,32,256]{1,0,2:T(2,128)S(1)}, u32[]{:S(2)}, u32[]{:S(2)}) collective-permute-start(f32[2,32,256]{1,0,2:T(2,128)S(1)} %get-tuple-element.122), channel_id=1, source_target_pairs={{0,4},{4,8},{8,12},{12,16},{16,20},{20,24},{24,28},{28,32},{32,36}... | collective-permute-start | bytes 196616 | tf_op jit(solution)/shard_map/ppermute | solution.py:23
  160.3 9.6 %collective-permute-start.5 = (f32[2,32,256]{1,0,2:T(2,128)S(1)}, f32[2,32,256]{1,0,2:T(2,128)S(1)}, u32[]{:S(2)}, u32[]{:S(2)}) collective-permute-start(f32[2,32,256]{1,0,2:T(2,128)S(1)} %get-tuple-element.123), channel_id=1, source_target_pairs={{4,0},{8,4},{12,8},{16,12},{20,16},{24,20},{28,24},{32,28},{36,32}... | collective-permute-start | bytes 196616 | tf_op jit(solution)/shard_map/ppermute | solution.py:26
  171.1 5.8 collective-permute-start.6
  175.0 5.6 collective-permute-start.7
  284.2 29.1 %copy-start.5 = (f32[12,68,512]{1,0,2:T(8,128)S(1)}, f32[12,68,512]{1,0,2:T(8,128)}, u32[]{:S(2)}) copy-start(f32[12,68,512]{1,0,2:T(8,128)} %copy.240) | copy-start | bytes 5013508
  299.6 7.7 %collective-permute-start.8 = (f32[1,16,128]{2,1,0:T(8,128)S(1)}, f32[1,16,128]{2,1,0:T(8,128)S(1)}, u32[]{:S(2)}, u32[]{:S(2)}) collective-permute-start(f32[1,16,128]{2,1,0:T(8,128)S(1)} %get-tuple-element.140), channel_id=1, source_target_pairs={{0,4},{4,8},{8,12},{12,16},{16,20},{20,24},{24,28},{28,32},{32,36}... | collective-permute-start | bytes 24584 | tf_op jit(solution)/shard_map/ppermute | solution.py:23
  301.7 6.9 %collective-permute-start.9 = (f32[1,16,128]{2,1,0:T(8,128)S(1)}, f32[1,16,128]{2,1,0:T(8,128)S(1)}, u32[]{:S(2)}, u32[]{:S(2)}) collective-permute-start(f32[1,16,128]{2,1,0:T(8,128)S(1)} %get-tuple-element.141), channel_id=1, source_target_pairs={{4,0},{8,4},{12,8},{16,12},{20,16},{24,20},{28,24},{32,28},{36,32}... | collective-permute-start | bytes 24584 | tf_op jit(solution)/shard_map/ppermute | solution.py:26
  308.6 6.0 collective-permute-start.10
  312.0 5.5 collective-permute-start.11
  317.9 8.4 %collective-permute-start.12 = (f32[1,32,256]{1,2,0:T(8,128)S(1)}, f32[1,32,256]{1,2,0:T(8,128)S(1)}, u32[]{:S(2)}, u32[]{:S(2)}) collective-permute-start(f32[1,32,256]{1,2,0:T(8,128)S(1)} %bitcast.328), channel_id=1, source_target_pairs={{0,4},{4,8},{8,12},{12,16},{16,20},{20,24},{24,28},{28,32},{32,36}... | collective-permute-start | bytes 98312 | tf_op jit(solution)/shard_map/ppermute | solution.py:23
  320.0 8.3 %collective-permute-start.13 = (f32[1,32,256]{1,2,0:T(8,128)S(1)}, f32[1,32,256]{1,2,0:T(8,128)S(1)}, u32[]{:S(2)}, u32[]{:S(2)}) collective-permute-start(f32[1,32,256]{1,2,0:T(8,128)S(1)} %bitcast.329), channel_id=1, source_target_pairs={{4,0},{8,4},{12,8},{16,12},{20,16},{24,20},{28,24},{32,28},{36,32}... | collective-permute-start | bytes 98312 | tf_op jit(solution)/shard_map/ppermute | solution.py:26
  328.3 8.5 %collective-permute-start.14 = (f32[6,1,256]{2,1,0:T(1,128)S(1)}, f32[6,1,256]{2,1,0:T(1,128)S(1)}, u32[]{:S(2)}, u32[]{:S(2)}) collective-permute-start(f32[6,1,256]{2,1,0:T(1,128)S(1)} %get-tuple-element.128), channel_id=1, source_target_pairs={{0,1},{1,2},{2,3},{4,5},{5,6},{6,7},{8,9},{9,10},{10,11},{12,13},{... | collective-permute-start | bytes 18440 | tf_op jit(solution)/shard_map/ppermute | solution.py:23
  331.7 5.5 collective-permute-start.15
  338.4 2.7 copy-start
  343.3 1.3 copy-start.6
  345.0 12.6 %collective-permute-start.16 = (f32[2,64,512]{1,0,2:T(2,128)S(1)}, f32[2,64,512]{1,0,2:T(2,128)S(1)}, u32[]{:S(2)}, u32[]{:S(2)}) collective-permute-start(f32[2,64,512]{1,0,2:T(2,128)S(1)} %get-tuple-element.110), channel_id=1, source_target_pairs={{0,4},{4,8},{8,12},{12,16},{16,20},{20,24},{24,28},{28,32},{32,36}... | collective-permute-start | bytes 786440 | tf_op jit(solution)/shard_map/ppermute | solution.py:23
  346.9 12.4 %collective-permute-start.17 = (f32[2,64,512]{1,0,2:T(2,128)S(1)}, f32[2,64,512]{1,0,2:T(2,128)S(1)}, u32[]{:S(2)}, u32[]{:S(2)}) collective-permute-start(f32[2,64,512]{1,0,2:T(2,128)S(1)} %get-tuple-element.111), channel_id=1, source_target_pairs={{4,0},{8,4},{12,8},{16,12},{20,16},{24,20},{28,24},{32,28},{36,32}... | collective-permute-start | bytes 786440 | tf_op jit(solution)/shard_map/ppermute | solution.py:26
  354.9 10.2 %copy-start.19 = (f32[3,16384]{1,0:T(4,128)S(1)}, f32[3,16384]{1,0:T(4,128)}, u32[]{:S(2)}) copy-start(f32[3,16384]{1,0:T(4,128)} %param.7) | copy-start | bytes 589828
  354.9 10.9 %copy-start.22 = (s32[128]{0:T(128)S(1)}, s32[128]{0:T(128)}, u32[]{:S(2)}) copy-start(s32[128]{0:T(128)} %param.8) | copy-start | bytes 1540
  354.9 10.9 %copy-start.23 = (s32[128]{0:T(128)S(1)}, s32[128]{0:T(128)}, u32[]{:S(2)}) copy-start(s32[128]{0:T(128)} %param.9) | copy-start | bytes 1540
  359.6 6.3 %collective-permute-start.18 = (f32[12,2,512]{2,1,0:T(2,128)S(1)}, f32[12,2,512]{2,1,0:T(2,128)S(1)}, u32[]{:S(2)}, u32[]{:S(2)}) collective-permute-start(f32[12,2,512]{2,1,0:T(2,128)S(1)} %get-tuple-element.112), channel_id=1, source_target_pairs={{0,1},{1,2},{2,3},{4,5},{5,6},{6,7},{8,9},{9,10},{10,11},{12,13},{... | collective-permute-start | bytes 147464 | tf_op jit(solution)/shard_map/ppermute | solution.py:23
  363.7 6.0 collective-permute-start.19
  380.6 7.8 %copy-start.18 = (f32[1,8,516,12]{2,1,3,0:T(8,128)S(1)}, f32[1,8,516,12]{2,1,3,0:T(8,128)}, u32[]{:S(2)}) copy-start(f32[1,8,516,12]{2,1,3,0:T(8,128)} %slice.514) | copy-start | bytes 594436
  380.6 7.8 %copy-start.17 = (f32[1,8,516,12]{2,1,3,0:T(8,128)S(1)}, f32[1,8,516,12]{2,1,3,0:T(8,128)}, u32[]{:S(2)}) copy-start(f32[1,8,516,12]{2,1,3,0:T(8,128)} %slice.515) | copy-start | bytes 594436
  524.0 4.2 copy-start.16
  524.0 5.1 copy-start.15
  524.0 6.0 copy-start.14
  526.2 4.9 copy-start.13
  528.2 3.9 copy-start.12
  529.1 3.9 copy-start.11
  530.1 3.9 copy-start.10
  531.0 3.8 copy-start.9
  532.1 3.7 copy-start.8
  559.9 12.7 %copy-start.3 = (f32[64,128,12]{1,2,0:T(8,128)S(1)}, f32[64,128,12]{1,2,0:T(8,128)}, u32[]{:S(2)}) copy-start(f32[64,128,12]{1,2,0:T(8,128)} %get-tuple-element.208) | copy-start | bytes 1179652 | tf_op jit(solution)/shard_map/while
  559.9 12.8 %copy-start.4 = (f32[64,128,12]{1,2,0:T(8,128)S(1)}, f32[64,128,12]{1,2,0:T(8,128)}, u32[]{:S(2)}) copy-start(f32[64,128,12]{1,2,0:T(8,128)} %get-tuple-element.207) | copy-start | bytes 1179652 | tf_op jit(solution)/shard_map/while
  572.6 3.0 copy-start.1
  572.6 3.0 copy-start.2
  575.6 1.0 copy-start.20
  590.8 12.7 %copy-start.3 = (f32[64,128,12]{1,2,0:T(8,128)S(1)}, f32[64,128,12]{1,2,0:T(8,128)}, u32[]{:S(2)}) copy-start(f32[64,128,12]{1,2,0:T(8,128)} %get-tuple-element.208) | copy-start | bytes 1179652 | tf_op jit(solution)/shard_map/while
  590.8 12.8 %copy-start.4 = (f32[64,128,12]{1,2,0:T(8,128)S(1)}, f32[64,128,12]{1,2,0:T(8,128)}, u32[]{:S(2)}) copy-start(f32[64,128,12]{1,2,0:T(8,128)} %get-tuple-element.207) | copy-start | bytes 1179652 | tf_op jit(solution)/shard_map/while
  603.6 3.0 copy-start.1
  603.6 3.0 copy-start.2
  (3 other events, 2.4 us)
Sparse Core Ops, SparseCore 0:
  199.2 75.8 all-gather.1
where the time goes:
time: 627 us; the launch traced here: 617 us
  local copies, waits for them, and re-layouts  350 us (56%)
  waiting for transfers between devices  106 us (17%)
  starting transfers between devices  64.5 us (10%)
  matrix products  40.8 us (7%)
  other arithmetic  28.2 us (4%)
  between operations  14.6 us (2%)
  blocking collectives  11.9 us (2%)
    slice x24, local copies, waits for them, and re-layouts, brick_windows(): lax.slice_in_dim(values, start, start + BRICK * (brick_count - 1) + 1, BR...  145 us
    slice x20, local copies, waits for them, and re-layouts, restrict_axis(): lax.slice_in_dim(values, start, start + length, 2, axis)  119 us
    all_gather x1, waiting for transfers between devices, on_device(): lax.all_gather(gathered, 'slab', axis=0, tiled=True)  75.7 us
    ppermute x10, starting transfers between devices, with_halo(): lax.ppermute(lax.slice_in_dim(block, 0, width, axis=dim), axis, backward)  36.8 us
    ppermute x10, starting transfers between devices, with_halo(): lax.ppermute(lax.slice_in_dim(block, block.shape[dim] - width, None, axis...  27.7 us
    dot_general x2, matrix products, interpolate(): inner = jnp.einsum('gkji,gica->gkjca', patches, paired, precision=HIGH)  25.5 us
    unnamed x73, local copies, waits for them, and re-layouts  23.7 us
    ppermute x10, waiting for transfers between devices, with_halo(): lax.ppermute(lax.slice_in_dim(block, 0, width, axis=dim), axis, backward)  23.2 us
  transfers between devices with their start and end apart: 21, of which 16 were waited for; matrix products, arithmetic and copies ran while one was open for 2% of the time, Pallas kernels for 0%

commit v1 on v0

v1 whole, which is shorter than its diff:
```python
import math

import jax
import jax.numpy as jnp
import ml_dtypes
import numpy as np
from jax import lax
from jax.experimental import pallas as pl
from jax.experimental.pallas import tpu as pltpu
from jax.sharding import PartitionSpec as P

TAPS = (0.125, 0.5, 0.75, 0.5, 0.125)
SPANS = (2.0, 8.0, 32.0)
NEAR_WEIGHT = 0.5

SLABS, SUBS = 64, 4
CZ, CY, NX = 8, 64, 512
NZ, NY = CZ * SLABS, CY * SUBS
BLOCKS, SLOT = 128, 128

FZ, FY, FX = 16, 72, 640
TZ, TY, TYS = 5, 19, 24
GS = 21
TILE = 40
TILES = 16

F32, BF16 = jnp.float32, jnp.bfloat16


def restriction(n):
    matrix = np.zeros((n // 2, n))
    for target in range(n // 2):
        for offset in range(-2, 3):
            if 0 <= 2 * target + offset < n:
                matrix[target, 2 * target + offset] = TAPS[offset + 2]
    return matrix


def restriction_twice(n):
    return restriction(n // 2) @ restriction(n)


def gauss(n, span):
    index = np.arange(n, dtype=np.float64)
    return np.exp(-(((index[:, None] - index[None, :]) / span) ** 2))


def window(matrix, row0, rows, col0, cols):
    out = np.zeros((rows, cols))
    for r in range(rows):
        for c in range(cols):
            if 0 <= row0 + r < matrix.shape[0] and 0 <= col0 + c < matrix.shape[1]:
                out[r, c] = matrix[row0 + r, col0 + c]
    return out


def halves(matrix):
    whole = np.asarray(matrix, np.float32)
    high = whole.astype(ml_dtypes.bfloat16)
    low = (whole - high.astype(np.float32)).astype(ml_dtypes.bfloat16)
    return high, low


def split(values):
    high = values.astype(BF16)
    return high, (values - high.astype(F32)).astype(BF16)


def dot(left, right):
    return jnp.dot(left, right, preferred_element_type=F32)


def dot3(left_high, left_low, right_high, right_low):
    return dot(left_high, right_high) + (dot(left_low, right_high) + dot(left_high, right_low))


SLAB_KINDS = (0, 1, SLABS - 1)


def make_constants():
    rz, ry, rx = restriction_twice(NZ), restriction_twice(NY), restriction_twice(NX)
    restrict_x = rx.T.astype(ml_dtypes.bfloat16)
    restrict_zy = np.zeros((3, SUBS, CZ, CY, 128))
    for kind, p in enumerate(SLAB_KINDS):
        mz = window(rz, 2 * p - 1, TZ, CZ * p, CZ)
        for q in range(SUBS):
            my = window(ry, 16 * q - 1, TY, CY * q, CY)
            for zt in range(TZ):
                restrict_zy[kind, q, :, :, zt * TYS : zt * TYS + TY] = (
                    mz[zt][:, None, None] * my.T[None, :, :]
                )
    restrict_zy = restrict_zy.reshape(3 * SUBS, CZ * CY, 128).astype(np.float32)

    span_y = np.zeros((SUBS, 128, 3 * 128))
    span_z = np.zeros((TZ, SLABS, 3, 2, SLABS))
    fine_x = np.zeros((SLABS, 8, FX))
    for s, span in enumerate(SPANS):
        gy, gz, gx = gauss(NY // 4, span), gauss(NZ // 4, span), gauss(NX // 4, span)
        for q in range(SUBS):
            part = window(gy, 16 * q - 1, TY, 0, NY // 4).T
            for x in range(2):
                col = s * 128 + (s * 2 + x) * GS
                span_y[q, x * 64 : x * 64 + 64, col : col + TY] = part
        wide = np.zeros((NZ // 4 + 8, NZ // 4))
        wide[1 : 1 + NZ // 4] = gz * span ** (-1.5)
        for k in range(TZ):
            rows = wide[k : k + NZ // 4 : 2]
            span_z[k, :, s] = rows.reshape(SLABS, SLABS, 2).transpose(0, 2, 1)
        px = rx.T @ gx
        for x in range(2):
            fine_x[:, s * 2 + x, 1 : 1 + NX] = px[:, x::2].T
    span_z = span_z.reshape(TZ * SLABS, 3 * 128)
    fine_x = fine_x.reshape(SLABS * 8, FX)

    prolong_y = np.zeros((SUBS, FY, FZ, 128))
    for q in range(SUBS):
        part = window(ry.T, CY * q - 1, CY + 3, 16 * q - 1, TY)
        for zo in range(TZ):
            prolong_y[q, : CY + 3, :, zo * TYS : zo * TYS + TY] = part[:, None, :]
    prolong_y = prolong_y.reshape(SUBS, FY * FZ, 128).astype(ml_dtypes.bfloat16)
    prolong_z = np.zeros((3, 8, FZ, 128))
    for kind, p in enumerate(SLAB_KINDS):
        part = window(rz.T, CZ * p - 1, CZ + 3, 2 * p - 1, TZ)
        for zo in range(TZ):
            prolong_z[kind, :, : CZ + 3, zo * TYS : zo * TYS + TY] = part[None, :, zo, None]
    prolong_z = prolong_z.reshape(3, 8 * FZ, 128).astype(np.float32)
    return dict(
        restrict_x=restrict_x,
        restrict_zy=restrict_zy,
        span_y=halves(span_y),
        span_z=halves(span_z),
        fine_x=halves(fine_x),
        prolong_y=prolong_y,
        prolong_z=prolong_z,
    )


CONSTANTS = make_constants()


def restrict_kernel(place, charge, along_x, along_zy, out):
    values = charge[...].reshape(CZ * CY, NX)
    high, low = split(values)
    narrow = dot(high, along_x[...]) + dot(low, along_x[...])
    narrow_high, narrow_low = split(narrow.T)
    zy_high, zy_low = split(along_zy[0])
    out[...] = dot3(narrow_high, narrow_low, zy_high, zy_low)


def middle_kernel(place, own, one, two, three, y_high, y_low, z_high, z_low, out):
    q = place[1]
    lane = lax.broadcasted_iota(jnp.int32, (SLABS, 128), 1)
    gathered = [None] * TZ
    for back, ref in enumerate((own, one, two, three)):
        source = lax.rem(q + (SUBS - back), SUBS)
        for x in range(2):
            rows = ref[pl.ds(x, SLABS, stride=2), :]
            first = 64 * x - 1 + 16 * source
            inside = (lane >= first) & (lane < first + TY)
            for zt in range(TZ):
                shift = lax.rem(first + (256 - TYS * zt), 128)
                term = jnp.where(inside, pltpu.roll(rows, shift, 1), 0.0)
                gathered[zt] = term if gathered[zt] is None else gathered[zt] + term
    even = gathered[1] + pltpu.roll(gathered[3], 1, 0)
    odd = gathered[2] + pltpu.roll(gathered[4], 1, 0) + pltpu.roll(gathered[0], SLABS - 1, 0)
    top_high, top_low = split(jnp.concatenate([even, odd], axis=0))
    mixed = dot3(top_high, top_low, y_high[0], y_low[0])
    stacked = jnp.concatenate([mixed[:, :128], mixed[:, 128:256], mixed[:, 256:]], axis=0)
    stacked_high, stacked_low = split(stacked)
    folded = dot3(z_high[...], z_low[...], stacked_high, stacked_low)
    for g in range(6):
        total = None
        for k in range(TZ):
            piece = folded[k * SLABS : (k + 1) * SLABS]
            moved = pltpu.roll(piece, (256 + TYS * k - GS * g) % 128, 1)
            term = jnp.where((lane >= TYS * k) & (lane < TYS * k + TY), moved, 0.0)
            total = term if total is None else total + term
        out[pl.ds(g, SLABS, stride=8), :] = total
    for g in range(6, 8):
        out[pl.ds(g, SLABS, stride=8), :] = jnp.zeros((SLABS, 128), F32)


def near_kernel(place, charge, z_low, z_high, y_low, y_high, out, rows, wide):
    p, q = place[0], place[1]
    taps = [math.exp(-0.5 * d * d) for d in range(3)]

    def stencil(at):
        return taps[2] * (at(0) + at(4)) + (taps[1] * (at(1) + at(3)) + at(2))

    def plane(k):
        if k < 3:
            return z_low[k]
        return charge[k - 3] if k < 3 + CZ else z_high[k - 3 - CZ]

    node = lax.broadcasted_iota(jnp.int32, (FY, 128), 0) + (CY * q - 1)
    keep_y = jnp.where((node >= 0) & (node < NY), NEAR_WEIGHT, 0.0)
    keep_y = jnp.concatenate([keep_y] * (NX // 128), axis=1)
    wide[0] = jnp.zeros((FY * FZ, 128), F32)
    wide[1 + NX // 128] = jnp.zeros((FY * FZ, 128), F32)
    for zo in range(CZ + 3):
        rows[8 : 8 + CY] = stencil(lambda d: plane(zo + d))
        rows[4:8] = stencil(lambda d: y_low[zo + d])
        rows[8 + CY : 12 + CY] = stencil(lambda d: y_high[zo + d])
        rows[12 + CY : 24 + CY] = jnp.zeros((12, NX), F32)
        total = stencil(lambda d: rows[5 + d : 5 + d + FY]) * keep_y
        if zo == 0:
            total = total * jnp.where(p > 0, 1.0, 0.0)
        elif zo >= 1 + CZ:
            total = total * jnp.where(p < SLABS - 1, 1.0, 0.0)
        for piece in range(NX // 128):
            at = 128 * piece
            wide[1 + piece, pl.ds(zo, FY, stride=FZ), :] = total[:, at : at + 128]
    for zo in range(CZ + 3, FZ):
        for piece in range(NX // 128):
            wide[1 + piece, pl.ds(zo, FY, stride=FZ), :] = jnp.zeros((FY, 128), F32)
    lane = lax.broadcasted_iota(jnp.int32, (32, FX), 1)
    inside = (lane >= 1) & (lane <= NX)

    def step(i, carry):
        at = pl.ds(pl.multiple_of(32 * i, 32), 32)
        values = jnp.concatenate([wide[c, at, :] for c in range(2 + NX // 128)], axis=1)
        total = stencil(lambda d: pltpu.roll(values, NX + 256 - 125 - d, 1)[:, :FX])
        out[at, :] = jnp.where(inside, total, 0.0)
        return carry

    lax.fori_loop(0, FY * FZ // 32, step, 0)


def spline_pair(distance):
    outer = jnp.maximum(2.0 - jnp.abs(distance), 0.0)
    inner = jnp.maximum(outer - 1.0, 0.0)
    outer_square = outer * outer
    inner_square = 4.0 * (inner * inner)
    value = outer_square * outer - inner_square * inner
    slope = inner_square - outer_square
    return value, jnp.where(distance < 0.0, -slope, slope)


def atoms_kernel(
    place, cell, count, near, arrived, x_high, x_low, along_y, along_z, offset, out, table, top
):
    top_high, top_low = split(arrived[...].T)
    potential = dot3(top_high, top_low, x_high[...], x_low[...])
    high, low = split(potential)
    top[0:128] = high
    top[128:256] = low
    lane = lax.broadcasted_iota(jnp.int32, (128, 128), 1)

    def build(i, carry):
        at = pl.ds(pl.multiple_of(128 * i, 128), 128)
        weight_high, weight_low = split(along_y[0, at, :].astype(F32) * along_z[0])
        fine = near[at, :] + dot3(weight_high, weight_low, top[0:128], top[128:256])
        fine_high = fine.astype(BF16).astype(F32)
        fine_low = fine - fine_high
        for t in range(TILES):
            shift = (FX - 32 * t) % FX
            a = pltpu.roll(fine_high, shift, 1)[:, :128]
            b = pltpu.roll(fine_low, (shift + TILE) % FX, 1)[:, :128]
            c = pltpu.roll(a, 2 * TILE, 1)
            row = jnp.where(lane < TILE, a, jnp.where(lane < 2 * TILE, b, c))
            table[t, at, :] = jnp.where(lane < 3 * TILE, row, 0.0).astype(BF16)
        return carry

    lax.fori_loop(0, FY * FZ // 128, build, 0)

    row16 = lax.broadcasted_iota(jnp.int32, (16, 128), 0).astype(F32) - 1.0
    row40 = lax.broadcasted_iota(jnp.int32, (TILE, 128), 0).astype(F32) - 1.0
    slot = lax.broadcasted_iota(jnp.int32, (1, 128), 1)
    blank = jnp.zeros((8, 256), F32)

    def block(b):
        at = pl.ds(pl.multiple_of(SLOT * b, SLOT), SLOT)
        t = cell[b]
        brick_y = lax.shift_right_logical(t, 6) & 7
        tile = lax.shift_right_logical(t, 2) & 15
        inner = (t & 3) * 8
        here = offset[:, at]
        wz, sz = spline_pair(here[0:1] - row16)
        wy, sy = spline_pair(here[1:2] - row16)
        wx, sx = spline_pair((here[2:3] + inner.astype(F32)) - row40)
        both = jnp.concatenate([wx, sx], axis=1)
        both_high = both.astype(BF16).astype(F32)
        weights = jnp.concatenate([both_high, both_high, both - both_high, blank], axis=0)
        first = pl.multiple_of(128 * brick_y, 128)
        patch = table[tile, pl.ds(first, 11 * FZ), :]
        product = dot(patch, weights.astype(BF16))
        base = along = cross = None
        for j in range(11):
            v = product[FZ * j : FZ * (j + 1), :128]
            d = product[FZ * j : FZ * (j + 1), 128:]
            w, s = wy[j : j + 1], sy[j : j + 1]
            base = v * w if base is None else base + v * w
            along = v * s if along is None else along + v * s
            cross = d * w if cross is None else cross + d * w

        def reduce(values):
            return jnp.sum(values, axis=0, keepdims=True)

        live = jnp.where(slot < count[b], 1.0, 0.0)
        slope = live * (-1.0 / 72.0)
        out[:, at] = jnp.concatenate(
            [
                reduce(base * wz) * (live * (1.0 / 216.0)),
                reduce(base * sz) * slope,
                reduce(along * wz) * slope,
                reduce(cross * wz) * slope,
            ],
            axis=0,
        )

    def step(i, carry):
        for k in range(4):
            block(4 * i + k)
        return carry

    lax.fori_loop(0, BLOCKS // 4, step, 0)


def whole(shape):
    return pl.BlockSpec(shape, lambda i, *_: (0,) * len(shape))


def call(kernel, scalars, in_specs, out_spec, out_shape, scratch, megabytes, flops, moved):
    return pl.pallas_call(
        kernel,
        grid_spec=pltpu.PrefetchScalarGridSpec(
            num_scalar_prefetch=scalars,
            grid=(1,),
            in_specs=in_specs,
            out_specs=out_spec,
            scratch_shapes=scratch,
        ),
        out_shape=jax.ShapeDtypeStruct(out_shape, F32),
        compiler_params=pltpu.CompilerParams(vmem_limit_bytes=megabytes * 2**20),
        cost_estimate=pl.CostEstimate(flops=flops, bytes_accessed=moved, transcendentals=0),
    )


def on_device(charge_grid, atom_offset, block_cell, block_count):
    consts = CONSTANTS
    p, q = lax.axis_index("slab"), lax.axis_index("sub")
    kind = jnp.where(p == 0, 0, jnp.where(p == SLABS - 1, 2, 1))
    place = jnp.stack([p, q, kind, kind * SUBS + q]).astype(jnp.int32)

    up = [(i, i + 1) for i in range(SLABS - 1)]
    down = [(b, a) for a, b in up]
    up_sub = [(i, i + 1) for i in range(SUBS - 1)]
    down_sub = [(b, a) for a, b in up_sub]

    partial = call(
        restrict_kernel,
        1,
        [
            whole((CZ, CY, NX)),
            whole((NX, 128)),
            pl.BlockSpec((1, CZ * CY, 128), lambda i, place: (place[3], 0, 0)),
        ],
        whole((128, 128)),
        (128, 128),
        [],
        32,
        2 * 10**8,
        2 * 10**6,
    )(place, charge_grid, consts["restrict_x"], consts["restrict_zy"])
    pencil = lax.all_to_all(partial, "slab", 0, 0, tiled=True)
    others = [
        lax.ppermute(pencil, "sub", [(i, (i + k) % SUBS) for i in range(SUBS)]) for k in (1, 2, 3)
    ]
    y_high, y_low = consts["span_y"]
    z_high, z_low = consts["span_z"]
    by_sub = pl.BlockSpec((1, 128, 384), lambda i, place: (place[1], 0, 0))
    folded = call(
        middle_kernel,
        1,
        [whole((128, 128))] * 4 + [by_sub, by_sub, whole((320, 384)), whole((320, 384))],
        whole((512, 128)),
        (512, 128),
        [],
        32,
        2 * 10**8,
        2 * 10**6,
    )(place, pencil, *others, y_high, y_low, z_high, z_low)
    arrived = lax.all_to_all(folded, "slab", 0, 0, tiled=True)

    below = lax.ppermute(charge_grid[CZ - 3 :], "slab", up)
    above = lax.ppermute(charge_grid[:4], "slab", down)
    left = jnp.concatenate([below[:, CY - 4 :], charge_grid[:, CY - 4 :], above[:, CY - 4 :]], axis=0)
    right = jnp.concatenate([below[:, :4], charge_grid[:, :4], above[:, :4]], axis=0)
    left = lax.ppermute(left, "sub", up_sub)
    right = lax.ppermute(right, "sub", down_sub)
    near = call(
        near_kernel,
        1,
        [
            whole((CZ, CY, NX)),
            whole((3, CY, NX)),
            whole((4, CY, NX)),
            whole((15, 4, NX)),
            whole((15, 4, NX)),
        ],
        whole((FY * FZ, FX)),
        (FY * FZ, FX),
        [pltpu.VMEM((CY + 24, NX), F32), pltpu.VMEM((2 + NX // 128, FY * FZ, 128), F32)],
        40,
        2 * 10**9,
        16 * 10**6,
    )(place, charge_grid, below, above, left, right)

    x_high, x_low = consts["fine_x"]
    return call(
        atoms_kernel,
        3,
        [
            whole((FY * FZ, FX)),
            whole((512, 128)),
            whole((512, FX)),
            whole((512, FX)),
            pl.BlockSpec((1, FY * FZ, 128), lambda i, place, *_: (place[1], 0, 0)),
            pl.BlockSpec((1, 128, 128), lambda i, place, *_: (place[2], 0, 0)),
            whole((3, BLOCKS * SLOT)),
        ],
        whole((4, BLOCKS * SLOT)),
        (4, BLOCKS * SLOT),
        [pltpu.VMEM((TILES, FY * FZ, 128), BF16), pltpu.VMEM((256, FX), BF16)],
        48,
        10**9,
        8 * 10**6,
    )(
        place,
        block_cell,
        block_count,
        near,
        arrived,
        x_high,
        x_low,
        consts["prolong_y"],
        consts["prolong_z"],
        atom_offset,
    )


def solution(mesh):
    placed = (
        P("slab", "sub", None),
        P(None, ("slab", "sub")),
        P(("slab", "sub")),
        P(("slab", "sub")),
    )
    return jax.shard_map(
        on_device, mesh=mesh, in_specs=placed, out_specs=P(None, ("slab", "sub")), check_vma=False
    )
```

time: 627 us -> 97.1 us (0.15)
  the two profiles are of different devices: /device:TPU:2 before, /device:TPU:1 now
where the time goes in v1:
time: 97.1 us; the launch traced here: 95.5 us
  Pallas kernels  33.4 us (34%)
  starting transfers between devices  32.3 us (33%)
  local copies, waits for them, and re-layouts  15.8 us (16%)
  waiting for transfers between devices  13.5 us (14%)
    pallas_call x1, Pallas kernels, on_device(): call(atoms_kernel, 3, [whole((FY * FZ, FX)), whole((512, 128)), whole((51...  19.5 us
    unnamed x42, local copies, waits for them, and re-layouts  13.1 us
    all_to_all x1, starting transfers between devices, on_device(): pencil = lax.all_to_all(partial, 'slab', 0, 0, tiled=True)  10.7 us
    pallas_call x1, Pallas kernels, on_device(): call(near_kernel, 1, [whole((CZ, CY, NX)), whole((3, CY, NX)), whole((4,...  9.47 us
    all_to_all x1, waiting for transfers between devices, on_device(): pencil = lax.all_to_all(partial, 'slab', 0, 0, tiled=True)  6.58 us
    all_to_all x1, starting transfers between devices, on_device(): arrived = lax.all_to_all(folded, 'slab', 0, 0, tiled=True)  5.87 us
    ppermute x3, starting transfers between devices, on_device(): lax.ppermute(pencil, 'sub', [(i, (i + k) % SUBS) for i in range(SUBS)])  4.99 us
    ppermute x1, starting transfers between devices, on_device(): below = lax.ppermute(charge_grid[CZ - 3:], 'slab', up)  4.92 us
  transfers between devices with their start and end apart: 9, of which 5 were waited for; matrix products, arithmetic and copies ran while one was open for 1% of the time, Pallas kernels for 15%

profile of v1, /device:TPU:1, one launch (start us, length us, event | category | flops | bytes accessed | tf_op | source)
XLA Modules:
  0.0 95.5 jit_solution(4980569075700190277)
XLA Ops:
  0.0 1.9 %slice.24 = f32[3,64,512]{2,1,0:T(8,128)} slice(f32[8,64,512]{2,1,0:T(8,128)} %charge.3), slice={[5:8], [0:64], [0:512]} | slice | bytes 786432 | tf_op jit(solution)/shard_map/slice | solution.py:385
  1.9 4.9 %collective-permute-start = (f32[3,64,512]{2,1,0:T(8,128)}, f32[3,64,512]{2,1,0:T(8,128)S(1)}, u32[]{:S(2)}, u32[]{:S(2)}) collective-permute-start(f32[3,64,512]{2,1,0:T(8,128)} %slice.24), channel_id=1, source_target_pairs={{0,4},{4,8},{8,12},{12,16},{16,20},{20,24},{24,28},{28,32},{32,36}... | collective-permute-start | bytes 1179656 | tf_op jit(solution)/shard_map/ppermute | solution.py:385
  6.8 0.1 pad_add_fusion.place
  6.9 1.2 %copy-done = f32[8,64,512]{2,1,0:T(8,128)S(1)} copy-done((f32[8,64,512]{2,1,0:T(8,128)S(1)}, f32[8,64,512]{2,1,0:T(8,128)}, u32[]{:S(2)}) %copy-start) | copy-done | bytes 1048600
  8.1 1.9 %copy-done.2 = f32[12,512,128]{2,1,0:T(8,128)S(1)} copy-done((f32[12,512,128]{2,1,0:T(8,128)S(1)}, f32[12,512,128]{2,1,0:T(8,128)}, u32[]{:S(2)}) %copy-start.2) | copy-done | bytes 3145752
  10.0 0.9 copy-done.14
  10.9 2.0 %shard_map.137 = f32[128,128]{1,0:T(8,128)} custom-call(s32[4]{0:T(128)S(1)} %pad_add_fusion.place, f32[8,64,512]{2,1,0:T(8,128)S(1)} %copy-done, bf16[512,128]{1,0:T(8,128)(2,1)S(1)} %copy-done.14, f32[12,512,128]{2,1,0:T(8,128)S(1)} %copy-done.2), custom_call_target="tpu_custom_call" | custom-call | flops 200000000 | bytes 2000000 | tf_op jit(solution)/shard_map/pallas_call | solution.py:350
  12.9 10.7 %all-to-all-start = ((f32[64,2,128]{2,1,0:T(2,128)}), f32[64,2,128]{2,1,0:T(2,128)S(1)}, u32[]{:S(2)}, u32[]{:S(2)}) async-start(f32[64,2,128]{2,1,0:T(2,128)} %bitcast.4), calls=%async_computation | async-start | bytes 131072 | tf_op jit(solution)/shard_map/all_to_all | solution.py:365
  23.6 0.0 copy-done.1
  23.6 0.8 slice.25
  24.5 2.4 %collective-permute-start.1 = (f32[4,64,512]{2,1,0:T(8,128)}, f32[4,64,512]{2,1,0:T(8,128)S(1)}, u32[]{:S(2)}, u32[]{:S(2)}) collective-permute-start(f32[4,64,512]{2,1,0:T(8,128)} %slice.25), channel_id=1, source_target_pairs={{4,0},{8,4},{12,8},{16,12},{20,16},{24,20},{28,24},{32,28},{36,32}... | collective-permute-start | bytes 1572872 | tf_op jit(solution)/shard_map/ppermute | solution.py:386
  26.8 6.6 %all-to-all-done = f32[64,2,128]{2,1,0:T(2,128)S(1)} async-done(((f32[64,2,128]{2,1,0:T(2,128)}), f32[64,2,128]{2,1,0:T(2,128)S(1)}, u32[]{:S(2)}, u32[]{:S(2)}) %all-to-all-start) | async-done | bytes 65568 | tf_op jit(solution)/shard_map/all_to_all | solution.py:365
  33.4 1.3 %collective-permute-start.4 = (f32[128,128]{1,0:T(8,128)S(1)}, f32[128,128]{1,0:T(8,128)S(1)}, u32[]{:S(2)}, u32[]{:S(2)}) collective-permute-start(f32[128,128]{1,0:T(8,128)S(1)} %bitcast.9), channel_id=1, source_target_pairs={{0,1},{1,2},{2,3},{3,0},{4,5},{5,6},{6,7},{7,4},{8,9},{9,10},{10,1... | collective-permute-start | bytes 196616 | tf_op jit(solution)/shard_map/ppermute | solution.py:367
  34.7 2.6 %collective-permute-start.5 = (f32[128,128]{1,0:T(8,128)S(1)}, f32[128,128]{1,0:T(8,128)S(1)}, u32[]{:S(2)}, u32[]{:S(2)}) collective-permute-start(f32[128,128]{1,0:T(8,128)S(1)} %bitcast.10), channel_id=1, source_target_pairs={{0,2},{1,3},{2,0},{3,1},{4,6},{5,7},{6,4},{7,5},{8,10},{9,11},{10,... | collective-permute-start | bytes 196616 | tf_op jit(solution)/shard_map/ppermute | solution.py:367
  37.3 1.1 %collective-permute-start.6 = (f32[128,128]{1,0:T(8,128)S(1)}, f32[128,128]{1,0:T(8,128)S(1)}, u32[]{:S(2)}, u32[]{:S(2)}) collective-permute-start(f32[128,128]{1,0:T(8,128)S(1)} %bitcast.11), channel_id=1, source_target_pairs={{0,3},{1,0},{2,1},{3,2},{4,7},{5,4},{6,5},{7,6},{8,11},{9,8},{10,9... | collective-permute-start | bytes 196616 | tf_op jit(solution)/shard_map/ppermute | solution.py:367
  38.4 0.0 collective-permute-done.4.one
  38.4 1.8 %collective-permute-done.5.two = f32[128,128]{1,0:T(8,128)S(1)} collective-permute-done((f32[128,128]{1,0:T(8,128)S(1)}, f32[128,128]{1,0:T(8,128)S(1)}, u32[]{:S(2)}, u32[]{:S(2)}) %collective-permute-start.5) | collective-permute-done | bytes 65568 | tf_op jit(solution)/shard_map/ppermute | solution.py:367
  40.3 0.5 collective-permute-done.6.three
  40.7 0.0 copy-done.8
  40.7 0.0 copy-done.9
  40.8 0.0 copy-done.11
  40.8 2.5 %shard_map.138 = f32[512,128]{1,0:T(8,128)} custom-call(s32[4]{0:T(128)S(1)} %pad_add_fusion.place, f32[128,128]{1,0:T(8,128)S(1)} %bitcast.12, f32[128,128]{1,0:T(8,128)S(1)} %collective-permute-done.4.one, f32[128,128]{1,0:T(8,128)S(1)} %collective-permute-done.5.two, f32[128,128]{1,0:T(8,128)S(1)} %collective-permute-done.6.three, ...), custom_call_target="tpu_custom_call" | custom-call | flops 200000000 | bytes 2000000 | tf_op jit(solution)/shard_map/pallas_call | solution.py:372
  43.2 5.9 %all-to-all-start.1 = ((f32[64,8,128]{2,1,0:T(8,128)}), f32[64,8,128]{2,1,0:T(8,128)S(1)}, u32[]{:S(2)}, u32[]{:S(2)}) async-start(f32[64,8,128]{2,1,0:T(8,128)} %bitcast.6), calls=%async_computation.1 | async-start | bytes 524288 | tf_op jit(solution)/shard_map/all_to_all | solution.py:383
  49.1 0.0 collective-permute-done.z_low
  49.1 0.0 copy-start.17
  49.1 0.8 copy-done.17
  49.9 0.0 collective-permute-done.1.z_high
  49.9 0.0 copy-start.15
  49.9 0.8 copy-done.15
  50.7 2.1 %collective-permute-start.2 = (f32[15,4,512]{2,1,0:T(4,128)S(1)}, f32[15,4,512]{2,1,0:T(4,128)S(1)}, u32[]{:S(2)}, u32[]{:S(2)}) collective-permute-start(f32[15,4,512]{2,1,0:T(4,128)S(1)} %pad_maximum_fusion), channel_id=1, source_target_pairs={{0,1},{1,2},{2,3},{4,5},{5,6},{6,7},{8,9},{9,10},{10,11},{12,13},{... | collective-permute-start | bytes 368648 | tf_op jit(solution)/shard_map/ppermute | solution.py:389
  52.8 0.0 copy-start.19
  52.8 0.0 copy-start.20
  52.9 0.0 copy-start.5
  52.9 0.0 copy-start.6
  52.9 0.0 copy-start.10
  52.9 1.4 %collective-permute-start.3 = (f32[15,4,512]{2,1,0:T(4,128)S(1)}, f32[15,4,512]{2,1,0:T(4,128)S(1)}, u32[]{:S(2)}, u32[]{:S(2)}) collective-permute-start(f32[15,4,512]{2,1,0:T(4,128)S(1)} %pad_maximum_fusion.1), channel_id=1, source_target_pairs={{1,0},{2,1},{3,2},{5,4},{6,5},{7,6},{9,8},{10,9},{11,10},{13,12},{... | collective-permute-start | bytes 368648 | tf_op jit(solution)/shard_map/ppermute | solution.py:390
  54.4 0.6 collective-permute-done.2.y_low
  54.9 4.1 %collective-permute-done.3.y_high = f32[15,4,512]{2,1,0:T(4,128)S(1)} collective-permute-done((f32[15,4,512]{2,1,0:T(4,128)S(1)}, f32[15,4,512]{2,1,0:T(4,128)S(1)}, u32[]{:S(2)}, u32[]{:S(2)}) %collective-permute-start.3) | collective-permute-done | bytes 122912 | tf_op jit(solution)/shard_map/ppermute | solution.py:390
  59.0 1.0 %copy-done.16 = f32[4,64,512]{2,1,0:T(8,128)S(1)} copy-done((f32[4,64,512]{2,1,0:T(8,128)S(1)}, f32[4,64,512]{2,1,0:T(8,128)}, u32[]{:S(2)}) %copy-start.16) | copy-done | bytes 524312
  60.0 1.0 %copy-done.18 = f32[3,64,512]{2,1,0:T(8,128)S(1)} copy-done((f32[3,64,512]{2,1,0:T(8,128)S(1)}, f32[3,64,512]{2,1,0:T(8,128)}, u32[]{:S(2)}) %copy-start.18) | copy-done | bytes 393240
  61.0 9.5 %shard_map.136.near = f32[1152,640]{1,0:T(8,128)S(1)} custom-call(s32[4]{0:T(128)S(1)} %pad_add_fusion.place, f32[8,64,512]{2,1,0:T(8,128)S(1)} %copy-done.1, f32[3,64,512]{2,1,0:T(8,128)S(1)} %copy-done.18, f32[4,64,512]{2,1,0:T(8,128)S(1)} %copy-done.16, f32[15,4,512]{2,1,0:T(4,128)S(1)} %collective-permute-done.2.y_low, ...), custom_call_target="tpu_custom_call" | custom-call | flops 2000000000 | bytes 16000000 | tf_op jit(solution)/shard_map/pallas_call | solution.py:391
  70.5 1.6 %copy-done.3 = f32[1152,640]{1,0:T(8,128)} copy-done((f32[1152,640]{1,0:T(8,128)}, f32[1152,640]{1,0:T(8,128)S(1)}, u32[]{:S(2)}) %copy-start.3) | copy-done | bytes 2949144
  72.1 0.0 all-to-all-done.1
  72.1 0.0 copy-done.20
  72.1 1.8 %copy-done.4 = f32[1152,640]{1,0:T(8,128)S(1)} copy-done((f32[1152,640]{1,0:T(8,128)S(1)}, f32[1152,640]{1,0:T(8,128)}, u32[]{:S(2)}) %copy-start.4) | copy-done | bytes 2949144
  74.0 1.1 %copy-done.7 = bf16[512,640]{1,0:T(8,128)(2,1)S(1)} copy-done((bf16[512,640]{1,0:T(8,128)(2,1)S(1)}, bf16[512,640]{1,0:T(8,128)(2,1)}, u32[]{:S(2)}) %copy-start.7) | copy-done | bytes 655384
  75.1 0.9 copy-done.13
  76.0 19.5 %shard_map.139 = f32[4,16384]{1,0:T(4,128)} custom-call(s32[4]{0:T(128)S(1)} %pad_add_fusion.place, s32[128]{0:T(128)S(1)} %copy-done.19, s32[128]{0:T(128)S(1)} %copy-done.20, f32[1152,640]{1,0:T(8,128)S(1)} %copy-done.4, f32[512,128]{1,0:T(8,128)S(1)} %bitcast.8, bf16[512,640]{1,0:T(8,128)(2,1)S(1)} %copy-done.6, bf16[512,640]{1,0:T(8,128)(2,1)S(1)} %copy-done.7, ...), custom_call_target="tpu_custom_call" | custom-call | flops 1000000000 | bytes 8000000 | tf_op jit(solution)/shard_map/pallas_call | solution.py:410
  (24 shorter events, 0.1 us)
Async XLA Ops:
  0.0 40.7 %copy-start.8 = (bf16[4,128,384]{2,1,0:T(8,128)(2,1)S(1)}, bf16[4,128,384]{2,1,0:T(8,128)(2,1)}, u32[]{:S(2)}) copy-start(bf16[4,128,384]{2,1,0:T(8,128)(2,1)} %constant.41.clone.y_high) | copy-start | bytes 1179652
  0.0 40.7 %copy-start.9 = (bf16[4,128,384]{2,1,0:T(8,128)(2,1)S(1)}, bf16[4,128,384]{2,1,0:T(8,128)(2,1)}, u32[]{:S(2)}) copy-start(bf16[4,128,384]{2,1,0:T(8,128)(2,1)} %constant.42.clone.y_low) | copy-start | bytes 1179652
  1.9 47.2 %collective-permute-start = (f32[3,64,512]{2,1,0:T(8,128)}, f32[3,64,512]{2,1,0:T(8,128)S(1)}, u32[]{:S(2)}, u32[]{:S(2)}) collective-permute-start(f32[3,64,512]{2,1,0:T(8,128)} %slice.24), channel_id=1, source_target_pairs={{0,4},{4,8},{8,12},{12,16},{16,20},{20,24},{24,28},{28,32},{32,36}... | collective-permute-start | bytes 1179656 | tf_op jit(solution)/shard_map/ppermute | solution.py:385
  6.9 1.2 %copy-start = (f32[8,64,512]{2,1,0:T(8,128)S(1)}, f32[8,64,512]{2,1,0:T(8,128)}, u32[]{:S(2)}) copy-start(f32[8,64,512]{2,1,0:T(8,128)} %charge.3) | copy-start | bytes 3145732
  8.1 1.9 %copy-start.2 = (f32[12,512,128]{2,1,0:T(8,128)S(1)}, f32[12,512,128]{2,1,0:T(8,128)}, u32[]{:S(2)}) copy-start(f32[12,512,128]{2,1,0:T(8,128)} %constant.40.clone.along_zy) | copy-start | bytes 9437188
  10.0 0.9 copy-start.14
  10.9 12.7 %copy-start.1 = (f32[8,64,512]{2,1,0:T(8,128)S(1)}, f32[8,64,512]{2,1,0:T(8,128)}, u32[]{:S(2)}) copy-start(f32[8,64,512]{2,1,0:T(8,128)} %charge.3) | copy-start | bytes 3145732
  10.9 29.9 %copy-start.11 = (bf16[320,384]{1,0:T(8,128)(2,1)S(1)}, bf16[320,384]{1,0:T(8,128)(2,1)}, u32[]{:S(2)}) copy-start(bf16[320,384]{1,0:T(8,128)(2,1)} %constant.43.clone.z_high) | copy-start | bytes 737284
  10.9 29.9 %copy-start.12 = (bf16[320,384]{1,0:T(8,128)(2,1)S(1)}, bf16[320,384]{1,0:T(8,128)(2,1)}, u32[]{:S(2)}) copy-start(bf16[320,384]{1,0:T(8,128)(2,1)} %constant.44.clone.z_low) | copy-start | bytes 737284
  12.9 20.5 %all-to-all-start = ((f32[64,2,128]{2,1,0:T(2,128)}), f32[64,2,128]{2,1,0:T(2,128)S(1)}, u32[]{:S(2)}, u32[]{:S(2)}) async-start(f32[64,2,128]{2,1,0:T(2,128)} %bitcast.4), calls=%async_computation | async-start | bytes 131072 | tf_op jit(solution)/shard_map/all_to_all | solution.py:365
  24.5 25.4 %collective-permute-start.1 = (f32[4,64,512]{2,1,0:T(8,128)}, f32[4,64,512]{2,1,0:T(8,128)S(1)}, u32[]{:S(2)}, u32[]{:S(2)}) collective-permute-start(f32[4,64,512]{2,1,0:T(8,128)} %slice.25), channel_id=1, source_target_pairs={{4,0},{8,4},{12,8},{16,12},{20,16},{24,20},{28,24},{32,28},{36,32}... | collective-permute-start | bytes 1572872 | tf_op jit(solution)/shard_map/ppermute | solution.py:386
  33.4 5.0 %collective-permute-start.4 = (f32[128,128]{1,0:T(8,128)S(1)}, f32[128,128]{1,0:T(8,128)S(1)}, u32[]{:S(2)}, u32[]{:S(2)}) collective-permute-start(f32[128,128]{1,0:T(8,128)S(1)} %bitcast.9), channel_id=1, source_target_pairs={{0,1},{1,2},{2,3},{3,0},{4,5},{5,6},{6,7},{7,4},{8,9},{9,10},{10,1... | collective-permute-start | bytes 196616 | tf_op jit(solution)/shard_map/ppermute | solution.py:367
  34.7 5.5 %collective-permute-start.5 = (f32[128,128]{1,0:T(8,128)S(1)}, f32[128,128]{1,0:T(8,128)S(1)}, u32[]{:S(2)}, u32[]{:S(2)}) collective-permute-start(f32[128,128]{1,0:T(8,128)S(1)} %bitcast.10), channel_id=1, source_target_pairs={{0,2},{1,3},{2,0},{3,1},{4,6},{5,7},{6,4},{7,5},{8,10},{9,11},{10,... | collective-permute-start | bytes 196616 | tf_op jit(solution)/shard_map/ppermute | solution.py:367
  37.3 3.4 %collective-permute-start.6 = (f32[128,128]{1,0:T(8,128)S(1)}, f32[128,128]{1,0:T(8,128)S(1)}, u32[]{:S(2)}, u32[]{:S(2)}) collective-permute-start(f32[128,128]{1,0:T(8,128)S(1)} %bitcast.11), channel_id=1, source_target_pairs={{0,3},{1,0},{2,1},{3,2},{4,7},{5,4},{6,5},{7,6},{8,11},{9,8},{10,9... | collective-permute-start | bytes 196616 | tf_op jit(solution)/shard_map/ppermute | solution.py:367
  43.2 28.9 %all-to-all-start.1 = ((f32[64,8,128]{2,1,0:T(8,128)}), f32[64,8,128]{2,1,0:T(8,128)S(1)}, u32[]{:S(2)}, u32[]{:S(2)}) async-start(f32[64,8,128]{2,1,0:T(8,128)} %bitcast.6), calls=%async_computation.1 | async-start | bytes 524288 | tf_op jit(solution)/shard_map/all_to_all | solution.py:383
  49.1 0.8 copy-start.17
  49.9 0.8 copy-start.15
  50.7 4.2 %collective-permute-start.2 = (f32[15,4,512]{2,1,0:T(4,128)S(1)}, f32[15,4,512]{2,1,0:T(4,128)S(1)}, u32[]{:S(2)}, u32[]{:S(2)}) collective-permute-start(f32[15,4,512]{2,1,0:T(4,128)S(1)} %pad_maximum_fusion), channel_id=1, source_target_pairs={{0,1},{1,2},{2,3},{4,5},{5,6},{6,7},{8,9},{9,10},{10,11},{12,13},{... | collective-permute-start | bytes 368648 | tf_op jit(solution)/shard_map/ppermute | solution.py:389
  52.8 19.3 %copy-start.19 = (s32[128]{0:T(128)S(1)}, s32[128]{0:T(128)}, u32[]{:S(2)}) copy-start(s32[128]{0:T(128)} %cell.1) | copy-start | bytes 1540
  52.8 19.3 %copy-start.20 = (s32[128]{0:T(128)S(1)}, s32[128]{0:T(128)}, u32[]{:S(2)}) copy-start(s32[128]{0:T(128)} %count.1) | copy-start | bytes 1540
  52.9 19.2 %copy-start.5 = (bf16[4,1152,128]{2,1,0:T(8,128)(2,1)S(1)}, bf16[4,1152,128]{2,1,0:T(8,128)(2,1)}, u32[]{:S(2)}) copy-start(bf16[4,1152,128]{2,1,0:T(8,128)(2,1)} %constant.47.clone.along_y) | copy-start | bytes 3538948
  52.9 19.2 %copy-start.6 = (bf16[512,640]{1,0:T(8,128)(2,1)S(1)}, bf16[512,640]{1,0:T(8,128)(2,1)}, u32[]{:S(2)}) copy-start(bf16[512,640]{1,0:T(8,128)(2,1)} %constant.45.clone.x_high) | copy-start | bytes 1966084
  52.9 19.2 %copy-start.10 = (f32[3,16384]{1,0:T(4,128)S(1)}, f32[3,16384]{1,0:T(4,128)}, u32[]{:S(2)}) copy-start(f32[3,16384]{1,0:T(4,128)} %offset.1) | copy-start | bytes 589828
  52.9 6.1 %collective-permute-start.3 = (f32[15,4,512]{2,1,0:T(4,128)S(1)}, f32[15,4,512]{2,1,0:T(4,128)S(1)}, u32[]{:S(2)}, u32[]{:S(2)}) collective-permute-start(f32[15,4,512]{2,1,0:T(4,128)S(1)} %pad_maximum_fusion.1), channel_id=1, source_target_pairs={{1,0},{2,1},{3,2},{5,4},{6,5},{7,6},{9,8},{10,9},{11,10},{13,12},{... | collective-permute-start | bytes 368648 | tf_op jit(solution)/shard_map/ppermute | solution.py:390
  59.0 1.0 %copy-start.16 = (f32[4,64,512]{2,1,0:T(8,128)S(1)}, f32[4,64,512]{2,1,0:T(8,128)}, u32[]{:S(2)}) copy-start(f32[4,64,512]{2,1,0:T(8,128)} %copy-done.15) | copy-start | bytes 1572868
  60.0 1.0 %copy-start.18 = (f32[3,64,512]{2,1,0:T(8,128)S(1)}, f32[3,64,512]{2,1,0:T(8,128)}, u32[]{:S(2)}) copy-start(f32[3,64,512]{2,1,0:T(8,128)} %copy-done.17) | copy-start | bytes 1179652
  70.5 1.6 %copy-start.3 = (f32[1152,640]{1,0:T(8,128)}, f32[1152,640]{1,0:T(8,128)S(1)}, u32[]{:S(2)}) copy-start(f32[1152,640]{1,0:T(8,128)S(1)} %shard_map.136.near) | copy-start | bytes 8847364
  72.1 1.8 %copy-start.4 = (f32[1152,640]{1,0:T(8,128)S(1)}, f32[1152,640]{1,0:T(8,128)}, u32[]{:S(2)}) copy-start(f32[1152,640]{1,0:T(8,128)} %copy-done.3) | copy-start | bytes 8847364
  74.0 1.1 %copy-start.7 = (bf16[512,640]{1,0:T(8,128)(2,1)S(1)}, bf16[512,640]{1,0:T(8,128)(2,1)}, u32[]{:S(2)}) copy-start(bf16[512,640]{1,0:T(8,128)(2,1)} %constant.46.clone.x_low) | copy-start | bytes 1966084
  75.1 0.9 copy-start.13

commit v2 on v1

--- a/solution.py
+++ b/solution.py
@@ -11,6 +11,7 @@
 
 TAPS = (0.125, 0.5, 0.75, 0.5, 0.125)
 SPANS = (2.0, 8.0, 32.0)
+NEAR = [math.exp(-0.5 * d * d) for d in range(3)]
 NEAR_WEIGHT = 0.5
 
 SLABS, SUBS = 64, 4
@@ -124,7 +125,13 @@
         for zo in range(TZ):
             prolong_z[kind, :, : CZ + 3, zo * TYS : zo * TYS + TY] = part[None, :, zo, None]
     prolong_z = prolong_z.reshape(3, 8 * FZ, 128).astype(np.float32)
+    near_x = np.zeros((NX, FX))
+    for node in range(NX):
+        for offset in range(-2, 3):
+            if 0 <= node + offset < NX:
+                near_x[node + offset, node + 1] = NEAR_WEIGHT * NEAR[abs(offset)]
     return dict(
+        near_x=halves(near_x),
         restrict_x=restrict_x,
         restrict_zy=restrict_zy,
         span_y=halves(span_y),
@@ -138,7 +145,9 @@
 CONSTANTS = make_constants()
 
 
-def restrict_kernel(place, charge, along_x, along_zy, out):
+def restrict_kernel(place, charge, along_x, along_zy, out, first_planes, last_planes):
+    first_planes[...] = charge[0:4]
+    last_planes[...] = charge[CZ - 3 : CZ]
     values = charge[...].reshape(CZ * CY, NX)
     high, low = split(values)
     narrow = dot(high, along_x[...]) + dot(low, along_x[...])
@@ -180,12 +189,11 @@
         out[pl.ds(g, SLABS, stride=8), :] = jnp.zeros((SLABS, 128), F32)
 
 
-def near_kernel(place, charge, z_low, z_high, y_low, y_high, out, rows, wide):
+def near_kernel(place, charge, z_low, z_high, y_low, y_high, x_high, x_low, out, rows, wide):
     p, q = place[0], place[1]
-    taps = [math.exp(-0.5 * d * d) for d in range(3)]
 
     def stencil(at):
-        return taps[2] * (at(0) + at(4)) + (taps[1] * (at(1) + at(3)) + at(2))
+        return NEAR[2] * (at(0) + at(4)) + (NEAR[1] * (at(1) + at(3)) + at(2))
 
     def plane(k):
         if k < 3:
@@ -193,10 +201,8 @@
         return charge[k - 3] if k < 3 + CZ else z_high[k - 3 - CZ]
 
     node = lax.broadcasted_iota(jnp.int32, (FY, 128), 0) + (CY * q - 1)
-    keep_y = jnp.where((node >= 0) & (node < NY), NEAR_WEIGHT, 0.0)
+    keep_y = jnp.where((node >= 0) & (node < NY), 1.0, 0.0)
     keep_y = jnp.concatenate([keep_y] * (NX // 128), axis=1)
-    wide[0] = jnp.zeros((FY * FZ, 128), F32)
-    wide[1 + NX // 128] = jnp.zeros((FY * FZ, 128), F32)
     for zo in range(CZ + 3):
         rows[8 : 8 + CY] = stencil(lambda d: plane(zo + d))
         rows[4:8] = stencil(lambda d: y_low[zo + d])
@@ -209,21 +215,19 @@
             total = total * jnp.where(p < SLABS - 1, 1.0, 0.0)
         for piece in range(NX // 128):
             at = 128 * piece
-            wide[1 + piece, pl.ds(zo, FY, stride=FZ), :] = total[:, at : at + 128]
+            wide[piece, pl.ds(zo, FY, stride=FZ), :] = total[:, at : at + 128]
     for zo in range(CZ + 3, FZ):
         for piece in range(NX // 128):
-            wide[1 + piece, pl.ds(zo, FY, stride=FZ), :] = jnp.zeros((FY, 128), F32)
-    lane = lax.broadcasted_iota(jnp.int32, (32, FX), 1)
-    inside = (lane >= 1) & (lane <= NX)
+            wide[piece, pl.ds(zo, FY, stride=FZ), :] = jnp.zeros((FY, 128), F32)
 
     def step(i, carry):
-        at = pl.ds(pl.multiple_of(32 * i, 32), 32)
-        values = jnp.concatenate([wide[c, at, :] for c in range(2 + NX // 128)], axis=1)
-        total = stencil(lambda d: pltpu.roll(values, NX + 256 - 125 - d, 1)[:, :FX])
-        out[at, :] = jnp.where(inside, total, 0.0)
+        at = pl.ds(pl.multiple_of(128 * i, 128), 128)
+        values = jnp.concatenate([wide[c, at, :] for c in range(NX // 128)], axis=1)
+        high, low = split(values)
+        out[at, :] = dot3(high, low, x_high[...], x_low[...])
         return carry
 
-    lax.fori_loop(0, FY * FZ // 32, step, 0)
+    lax.fori_loop(0, FY * FZ // 128, step, 0)
 
 
 def spline_pair(distance):
@@ -253,12 +257,22 @@
         fine_high = fine.astype(BF16).astype(F32)
         fine_low = fine - fine_high
         for t in range(TILES):
-            shift = (FX - 32 * t) % FX
-            a = pltpu.roll(fine_high, shift, 1)[:, :128]
-            b = pltpu.roll(fine_low, (shift + TILE) % FX, 1)[:, :128]
+            tile, first = divmod(32 * t, 128)
+
+            def moved(values, to):
+                here = values[:, 128 * tile : 128 * tile + 128]
+                here = pltpu.roll(here, (128 + to - first) % 128, 1) if to != first else here
+                if first + TILE <= 128:
+                    return here
+                after = values[:, 128 * tile + 128 : 128 * tile + 256]
+                after = pltpu.roll(after, (128 + to - first) % 128, 1)
+                return jnp.where(lane < to + 128 - first, here, after)
+
+            a = moved(fine_high, 0)
+            b = moved(fine_low, TILE)
             c = pltpu.roll(a, 2 * TILE, 1)
             row = jnp.where(lane < TILE, a, jnp.where(lane < 2 * TILE, b, c))
-            table[t, at, :] = jnp.where(lane < 3 * TILE, row, 0.0).astype(BF16)
+            table[t, at, :] = row.astype(BF16)
         return carry
 
     lax.fori_loop(0, FY * FZ // 128, build, 0)
@@ -309,11 +323,11 @@
         )
 
     def step(i, carry):
-        for k in range(4):
-            block(4 * i + k)
+        for k in range(8):
+            block(8 * i + k)
         return carry
 
-    lax.fori_loop(0, BLOCKS // 4, step, 0)
+    lax.fori_loop(0, BLOCKS // 8, step, 0)
 
 
 def whole(shape):
@@ -330,7 +344,11 @@
             out_specs=out_spec,
             scratch_shapes=scratch,
         ),
-        out_shape=jax.ShapeDtypeStruct(out_shape, F32),
+        out_shape=jax.tree.map(
+            lambda shape: jax.ShapeDtypeStruct(shape, F32),
+            out_shape,
+            is_leaf=lambda shape: isinstance(shape, tuple),
+        ),
         compiler_params=pltpu.CompilerParams(vmem_limit_bytes=megabytes * 2**20),
         cost_estimate=pl.CostEstimate(flops=flops, bytes_accessed=moved, transcendentals=0),
     )
@@ -347,7 +365,7 @@
     up_sub = [(i, i + 1) for i in range(SUBS - 1)]
     down_sub = [(b, a) for a, b in up_sub]
 
-    partial = call(
+    partial, first_planes, last_planes = call(
         restrict_kernel,
         1,
         [
@@ -355,10 +373,10 @@
             whole((NX, 128)),
             pl.BlockSpec((1, CZ * CY, 128), lambda i, place: (place[3], 0, 0)),
         ],
-        whole((128, 128)),
-        (128, 128),
+        [whole((128, 128)), whole((4, CY, NX)), whole((3, CY, NX))],
+        [(128, 128), (4, CY, NX), (3, CY, NX)],
         [],
-        32,
+        60,
         2 * 10**8,
         2 * 10**6,
     )(place, charge_grid, consts["restrict_x"], consts["restrict_zy"])
@@ -380,14 +398,14 @@
         2 * 10**8,
         2 * 10**6,
     )(place, pencil, *others, y_high, y_low, z_high, z_low)
-    arrived = lax.all_to_all(folded, "slab", 0, 0, tiled=True)
-
-    below = lax.ppermute(charge_grid[CZ - 3 :], "slab", up)
-    above = lax.ppermute(charge_grid[:4], "slab", down)
+    below = lax.ppermute(last_planes, "slab", up)
+    above = lax.ppermute(first_planes, "slab", down)
     left = jnp.concatenate([below[:, CY - 4 :], charge_grid[:, CY - 4 :], above[:, CY - 4 :]], axis=0)
     right = jnp.concatenate([below[:, :4], charge_grid[:, :4], above[:, :4]], axis=0)
     left = lax.ppermute(left, "sub", up_sub)
     right = lax.ppermute(right, "sub", down_sub)
+    left, right, folded = lax.optimization_barrier((left, right, folded))
+    arrived = lax.all_to_all(folded, "slab", 0, 0, tiled=True)
     near = call(
         near_kernel,
         1,
@@ -397,14 +415,16 @@
             whole((4, CY, NX)),
             whole((15, 4, NX)),
             whole((15, 4, NX)),
+            whole((NX, FX)),
+            whole((NX, FX)),
         ],
         whole((FY * FZ, FX)),
         (FY * FZ, FX),
-        [pltpu.VMEM((CY + 24, NX), F32), pltpu.VMEM((2 + NX // 128, FY * FZ, 128), F32)],
-        40,
+        [pltpu.VMEM((CY + 24, NX), F32), pltpu.VMEM((NX // 128, FY * FZ, 128), F32)],
+        60,
         2 * 10**9,
         16 * 10**6,
-    )(place, charge_grid, below, above, left, right)
+    )(place, charge_grid, below, above, left, right, *consts["near_x"])
 
     x_high, x_low = consts["fine_x"]
     return call(
@@ -422,7 +442,7 @@
         whole((4, BLOCKS * SLOT)),
         (4, BLOCKS * SLOT),
         [pltpu.VMEM((TILES, FY * FZ, 128), BF16), pltpu.VMEM((256, FX), BF16)],
-        48,
+        60,
         10**9,
         8 * 10**6,
     )(

time: 97.1 us -> 85.4 us (0.88); the launches traced: 95.5 us -> 85 us
  local copies, waits for them, and re-layouts: 15.8 us -> 1.77 us
  starting transfers between devices: 32.3 us -> 36.2 us
  waiting for transfers between devices: 13.5 us -> 9.97 us
  Pallas kernels: 33.4 us -> 36.2 us
    unnamed x42 -> x20, local copies, waits for them, and re-layouts: 13.1 us -> 0.75 us
    ppermute x1, waiting for transfers between devices: 4.06 us -> 0.01 us  [on_device(): right = lax.ppermute(right, 'sub', down_sub)]
    ppermute x3, waiting for transfers between devices: 2.3 us -> 5.21 us  [on_device(): lax.ppermute(pencil, 'sub', [(i, (i + k) % SUBS) for i in range(SUBS)])]
    slice x2 -> x0, local copies, waits for them, and re-layouts: 2.69 us -> none  [the longest x1 1.85 us: on_device(): below = lax.ppermute(charge_grid[CZ - 3:], 'slab', up)]
    all_to_all x1, waiting for transfers between devices: 6.58 us -> 4.11 us  [on_device(): pencil = lax.all_to_all(partial, 'slab', 0, 0, tiled=True)]
    all_to_all x1, starting transfers between devices: 5.87 us -> 8.15 us  [on_device(): arrived = lax.all_to_all(folded, 'slab', 0, 0, tiled=True)]
    all_to_all x1, starting transfers between devices: 10.7 us -> 12.9 us  [on_device(): pencil = lax.all_to_all(partial, 'slab', 0, 0, tiled=True)]
    pallas_call x1, Pallas kernels: 9.47 us -> 11.3 us  [on_device(): call(near_kernel, 1, [whole((CZ, CY, NX)), whole((3, CY, NX)), whole((4,...]
  transfers between devices with their start and end apart: 9 -> 9, of which waited for: 5 -> 5; matrix products, arithmetic and copies ran while one was open for 1% -> 1% of each run, Pallas kernels for 15% -> 16%
where the time goes in v2:
time: 85.4 us; the launch traced here: 85 us
  Pallas kernels  36.2 us (42%)
  starting transfers between devices  36.2 us (42%)
  waiting for transfers between devices  9.97 us (12%)
  local copies, waits for them, and re-layouts  1.77 us (2%)
    pallas_call x1, Pallas kernels, on_device(): call(atoms_kernel, 3, [whole((FY * FZ, FX)), whole((512, 128)), whole((51...  18.5 us
    all_to_all x1, starting transfers between devices, on_device(): pencil = lax.all_to_all(partial, 'slab', 0, 0, tiled=True)  12.9 us
    pallas_call x1, Pallas kernels, on_device(): call(near_kernel, 1, [whole((CZ, CY, NX)), whole((3, CY, NX)), whole((4,...  11.3 us
    all_to_all x1, starting transfers between devices, on_device(): arrived = lax.all_to_all(folded, 'slab', 0, 0, tiled=True)  8.15 us
    ppermute x3, waiting for transfers between devices, on_device(): lax.ppermute(pencil, 'sub', [(i, (i + k) % SUBS) for i in range(SUBS)])  5.21 us
    ppermute x1, starting transfers between devices, on_device(): below = lax.ppermute(last_planes, 'slab', up)  4.92 us
    all_to_all x1, waiting for transfers between devices, on_device(): pencil = lax.all_to_all(partial, 'slab', 0, 0, tiled=True)  4.11 us
    pallas_call x1, Pallas kernels, on_device(): call(restrict_kernel, 1, [whole((CZ, CY, NX)), whole((NX, 128)), pl.Block...  3.87 us
  transfers between devices with their start and end apart: 9, of which 5 were waited for; matrix products, arithmetic and copies ran while one was open for 1% of the time, Pallas kernels for 16%

profile of v2, /device:TPU:1, one launch (start us, length us, event | category | flops | bytes accessed | tf_op | source)
XLA Modules:
  0.0 85.0 jit_solution(4626590468908380567)
XLA Ops:
  0.0 0.0 copy-start.2
  0.0 0.0 copy-start.3
  0.0 0.0 copy-start
  0.0 0.0 copy-start.1
  0.0 0.7 pad_add_fusion.place
  0.7 0.0 copy-start.4
  0.7 3.9 %shard_map.154 = (f32[128,128]{1,0:T(8,128)}, f32[4,64,512]{2,1,0:T(8,128)}, f32[3,64,512]{2,1,0:T(8,128)}) custom-call(s32[4]{0:T(128)} %pad_add_fusion.place, f32[8,64,512]{2,1,0:T(8,128)} %charge.3, bf16[512,128]{1,0:T(8,128)(2,1)} %constant.43.clone.along_x, f32[12,512,128]{2,1,0:T(8,128)} %constant.44.clone.along_zy), custom_call_target="tpu_custom_call" | custom-call | flops 200000000 | bytes 2000000 | tf_op jit(solution)/shard_map/pallas_call | solution.py:368
  4.6 4.9 %collective-permute-start = (f32[3,64,512]{2,1,0:T(8,128)}, f32[3,64,512]{2,1,0:T(8,128)S(1)}, u32[]{:S(2)}, u32[]{:S(2)}) collective-permute-start(f32[3,64,512]{2,1,0:T(8,128)} %get-tuple-element.11), channel_id=1, source_target_pairs={{0,4},{4,8},{8,12},{12,16},{16,20},{20,24},{24,28},{28,32},{32,36}... | collective-permute-start | bytes 1179656 | tf_op jit(solution)/shard_map/ppermute | solution.py:401
  9.5 1.9 %collective-permute-start.1 = (f32[4,64,512]{2,1,0:T(8,128)}, f32[4,64,512]{2,1,0:T(8,128)S(1)}, u32[]{:S(2)}, u32[]{:S(2)}) collective-permute-start(f32[4,64,512]{2,1,0:T(8,128)} %get-tuple-element.12), channel_id=1, source_target_pairs={{4,0},{8,4},{12,8},{16,12},{20,16},{24,20},{28,24},{32,28},{36,32}... | collective-permute-start | bytes 1572872 | tf_op jit(solution)/shard_map/ppermute | solution.py:402
  11.4 12.9 %all-to-all-start = ((f32[64,2,128]{2,1,0:T(2,128)}), f32[64,2,128]{2,1,0:T(2,128)S(1)}, u32[]{:S(2)}, u32[]{:S(2)}) async-start(f32[64,2,128]{2,1,0:T(2,128)} %bitcast.13), calls=%async_computation | async-start | bytes 131072 | tf_op jit(solution)/shard_map/all_to_all | solution.py:383
  24.3 1.0 %fusion = (f32[8,4,512]{2,1,0:T(4,128)S(1)}, f32[8,4,512]{2,1,0:T(4,128)S(1)}) fusion(f32[8,64,512]{2,1,0:T(8,128)} %charge.3), kind=kLoop, calls=%fused_computation.3 | loop fusion | bytes 262144 | tf_op jit(solution)/shard_map/slice | solution.py:404
  25.3 0.0 collective-permute-done.z_low
  25.4 0.0 copy-start.7
  25.4 0.0 collective-permute-done.1.z_high
  25.4 0.0 copy-start.6
  25.5 3.2 %collective-permute-start.2 = (f32[15,4,512]{2,1,0:T(4,128)S(1)}, f32[15,4,512]{2,1,0:T(4,128)S(1)}, u32[]{:S(2)}, u32[]{:S(2)}) collective-permute-start(f32[15,4,512]{2,1,0:T(4,128)S(1)} %pad_maximum_fusion), channel_id=1, source_target_pairs={{0,1},{1,2},{2,3},{4,5},{5,6},{6,7},{8,9},{9,10},{10,11},{12,13},{... | collective-permute-start | bytes 368648 | tf_op jit(solution)/shard_map/ppermute | solution.py:405
  28.7 1.3 %collective-permute-start.3 = (f32[15,4,512]{2,1,0:T(4,128)S(1)}, f32[15,4,512]{2,1,0:T(4,128)S(1)}, u32[]{:S(2)}, u32[]{:S(2)}) collective-permute-start(f32[15,4,512]{2,1,0:T(4,128)S(1)} %pad_maximum_fusion.1), channel_id=1, source_target_pairs={{1,0},{2,1},{3,2},{5,4},{6,5},{7,6},{9,8},{10,9},{11,10},{13,12},{... | collective-permute-start | bytes 368648 | tf_op jit(solution)/shard_map/ppermute | solution.py:406
  30.0 4.1 %all-to-all-done = f32[64,2,128]{2,1,0:T(2,128)S(1)} async-done(((f32[64,2,128]{2,1,0:T(2,128)}), f32[64,2,128]{2,1,0:T(2,128)S(1)}, u32[]{:S(2)}, u32[]{:S(2)}) %all-to-all-start) | async-done | bytes 65568 | tf_op jit(solution)/shard_map/all_to_all | solution.py:383
  34.1 2.7 %collective-permute-start.6 = (f32[128,128]{1,0:T(8,128)S(1)}, f32[128,128]{1,0:T(8,128)S(1)}, u32[]{:S(2)}, u32[]{:S(2)}) collective-permute-start(f32[128,128]{1,0:T(8,128)S(1)} %bitcast.8), channel_id=1, source_target_pairs={{0,3},{1,0},{2,1},{3,2},{4,7},{5,4},{6,5},{7,6},{8,11},{9,8},{10,9... | collective-permute-start | bytes 196616 | tf_op jit(solution)/shard_map/ppermute | solution.py:385
  36.9 0.3 collective-permute-start.5
  37.2 0.7 collective-permute-start.4
  37.9 0.3 collective-permute-done.6.three
  38.2 3.4 %collective-permute-done.5.two = f32[128,128]{1,0:T(8,128)S(1)} collective-permute-done((f32[128,128]{1,0:T(8,128)S(1)}, f32[128,128]{1,0:T(8,128)S(1)}, u32[]{:S(2)}, u32[]{:S(2)}) %collective-permute-start.5) | collective-permute-done | bytes 65568 | tf_op jit(solution)/shard_map/ppermute | solution.py:385
  41.5 1.6 %collective-permute-done.4.one = f32[128,128]{1,0:T(8,128)S(1)} collective-permute-done((f32[128,128]{1,0:T(8,128)S(1)}, f32[128,128]{1,0:T(8,128)S(1)}, u32[]{:S(2)}, u32[]{:S(2)}) %collective-permute-start.4) | collective-permute-done | bytes 65568 | tf_op jit(solution)/shard_map/ppermute | solution.py:385
  43.1 0.0 copy-done.2
  43.1 0.0 copy-done.3
  43.1 0.0 copy-done
  43.1 0.0 copy-done.1
  43.1 0.0 copy-done.4
  43.1 2.5 %shard_map.155 = f32[512,128]{1,0:T(8,128)} custom-call(s32[4]{0:T(128)S(1)} %copy-done.4, f32[128,128]{1,0:T(8,128)S(1)} %bitcast.11, f32[128,128]{1,0:T(8,128)S(1)} %collective-permute-done.4.one, f32[128,128]{1,0:T(8,128)S(1)} %collective-permute-done.5.two, f32[128,128]{1,0:T(8,128)S(1)} %collective-permute-done.6.three, ...), custom_call_target="tpu_custom_call" | custom-call | flops 200000000 | bytes 2000000 | tf_op jit(solution)/shard_map/pallas_call | solution.py:390
  45.6 0.0 collective-permute-done.2.y_low
  45.6 0.0 copy-start.8
  45.6 0.0 collective-permute-done.3.y_high
  45.6 0.0 copy-start.9
  45.6 8.2 %all-to-all-start.1 = ((f32[64,8,128]{2,1,0:T(8,128)}), f32[64,8,128]{2,1,0:T(8,128)S(1)}, u32[]{:S(2)}, u32[]{:S(2)}) async-start(f32[64,8,128]{2,1,0:T(8,128)} %bitcast.6), calls=%async_computation.1 | async-start | bytes 524288 | tf_op jit(solution)/shard_map/all_to_all | solution.py:408
  53.8 0.0 copy-done.7
  53.8 0.0 copy-done.6
  53.8 0.0 copy-done.8
  53.8 0.0 copy-done.9
  53.8 11.3 %shard_map.156.near = f32[1152,640]{1,0:T(8,128)} custom-call(s32[4]{0:T(128)} %pad_add_fusion.place, f32[8,64,512]{2,1,0:T(8,128)} %charge.3, f32[3,64,512]{2,1,0:T(8,128)} %copy-done.7, f32[4,64,512]{2,1,0:T(8,128)} %copy-done.6, f32[15,4,512]{2,1,0:T(4,128)} %copy-done.8, f32[15,4,512]{2,1,0:T(4,128)} %copy-done.9, ...), custom_call_target="tpu_custom_call" | custom-call | flops 2000000000 | bytes 16000000 | tf_op jit(solution)/shard_map/pallas_call | solution.py:409
  65.1 0.6 all-to-all-done.1
  65.8 0.0 copy-start.5
  65.8 0.7 copy-done.5
  66.5 18.5 %shard_map.157 = f32[4,16384]{1,0:T(4,128)} custom-call(s32[4]{0:T(128)} %pad_add_fusion.place, s32[128]{0:T(128)} %cell.1, s32[128]{0:T(128)} %count.1, f32[1152,640]{1,0:T(8,128)} %shard_map.156.near, f32[512,128]{1,0:T(8,128)} %bitcast.12, bf16[512,640]{1,0:T(8,128)(2,1)} %constant.51.clone.x_high, bf16[512,640]{1,0:T(8,128)(2,1)} %constant.52.clone.x_low, ...), custom_call_target="tpu_custom_call" | custom-call | flops 1000000000 | bytes 8000000 | tf_op jit(solution)/shard_map/pallas_call | solution.py:430
  (4 shorter events, 0.1 us)
Async XLA Ops:
  0.0 43.1 %copy-start.2 = (bf16[320,384]{1,0:T(8,128)(2,1)S(1)}, bf16[320,384]{1,0:T(8,128)(2,1)}, u32[]{:S(2)}) copy-start(bf16[320,384]{1,0:T(8,128)(2,1)} %constant.48.clone.z_low) | copy-start | bytes 737284
  0.0 43.1 %copy-start.3 = (bf16[320,384]{1,0:T(8,128)(2,1)S(1)}, bf16[320,384]{1,0:T(8,128)(2,1)}, u32[]{:S(2)}) copy-start(bf16[320,384]{1,0:T(8,128)(2,1)} %constant.47.clone.z_high) | copy-start | bytes 737284
  0.0 43.1 %copy-start = (bf16[4,128,384]{2,1,0:T(8,128)(2,1)S(1)}, bf16[4,128,384]{2,1,0:T(8,128)(2,1)}, u32[]{:S(2)}) copy-start(bf16[4,128,384]{2,1,0:T(8,128)(2,1)} %constant.46.clone.y_low) | copy-start | bytes 1179652
  0.0 43.1 %copy-start.1 = (bf16[4,128,384]{2,1,0:T(8,128)(2,1)S(1)}, bf16[4,128,384]{2,1,0:T(8,128)(2,1)}, u32[]{:S(2)}) copy-start(bf16[4,128,384]{2,1,0:T(8,128)(2,1)} %constant.45.clone.y_high) | copy-start | bytes 1179652
  0.7 42.4 %copy-start.4 = (s32[4]{0:T(128)S(1)}, s32[4]{0:T(128)}, u32[]{:S(2)}) copy-start(s32[4]{0:T(128)} %pad_add_fusion.place) | copy-start | bytes 52
  4.6 20.8 %collective-permute-start = (f32[3,64,512]{2,1,0:T(8,128)}, f32[3,64,512]{2,1,0:T(8,128)S(1)}, u32[]{:S(2)}, u32[]{:S(2)}) collective-permute-start(f32[3,64,512]{2,1,0:T(8,128)} %get-tuple-element.11), channel_id=1, source_target_pairs={{0,4},{4,8},{8,12},{12,16},{16,20},{20,24},{24,28},{28,32},{32,36}... | collective-permute-start | bytes 1179656 | tf_op jit(solution)/shard_map/ppermute | solution.py:401
  9.5 15.9 %collective-permute-start.1 = (f32[4,64,512]{2,1,0:T(8,128)}, f32[4,64,512]{2,1,0:T(8,128)S(1)}, u32[]{:S(2)}, u32[]{:S(2)}) collective-permute-start(f32[4,64,512]{2,1,0:T(8,128)} %get-tuple-element.12), channel_id=1, source_target_pairs={{4,0},{8,4},{12,8},{16,12},{20,16},{24,20},{28,24},{32,28},{36,32}... | collective-permute-start | bytes 1572872 | tf_op jit(solution)/shard_map/ppermute | solution.py:402
  11.4 22.7 %all-to-all-start = ((f32[64,2,128]{2,1,0:T(2,128)}), f32[64,2,128]{2,1,0:T(2,128)S(1)}, u32[]{:S(2)}, u32[]{:S(2)}) async-start(f32[64,2,128]{2,1,0:T(2,128)} %bitcast.13), calls=%async_computation | async-start | bytes 131072 | tf_op jit(solution)/shard_map/all_to_all | solution.py:383
  25.4 28.4 %copy-start.7 = (f32[3,64,512]{2,1,0:T(8,128)}, f32[3,64,512]{2,1,0:T(8,128)S(1)}, u32[]{:S(2)}) copy-start(f32[3,64,512]{2,1,0:T(8,128)S(1)} %collective-permute-done.z_low) | copy-start | bytes 1179652
  25.4 28.4 %copy-start.6 = (f32[4,64,512]{2,1,0:T(8,128)}, f32[4,64,512]{2,1,0:T(8,128)S(1)}, u32[]{:S(2)}) copy-start(f32[4,64,512]{2,1,0:T(8,128)S(1)} %collective-permute-done.1.z_high) | copy-start | bytes 1572868
  25.5 20.1 %collective-permute-start.2 = (f32[15,4,512]{2,1,0:T(4,128)S(1)}, f32[15,4,512]{2,1,0:T(4,128)S(1)}, u32[]{:S(2)}, u32[]{:S(2)}) collective-permute-start(f32[15,4,512]{2,1,0:T(4,128)S(1)} %pad_maximum_fusion), channel_id=1, source_target_pairs={{0,1},{1,2},{2,3},{4,5},{5,6},{6,7},{8,9},{9,10},{10,11},{12,13},{... | collective-permute-start | bytes 368648 | tf_op jit(solution)/shard_map/ppermute | solution.py:405
  28.7 16.9 %collective-permute-start.3 = (f32[15,4,512]{2,1,0:T(4,128)S(1)}, f32[15,4,512]{2,1,0:T(4,128)S(1)}, u32[]{:S(2)}, u32[]{:S(2)}) collective-permute-start(f32[15,4,512]{2,1,0:T(4,128)S(1)} %pad_maximum_fusion.1), channel_id=1, source_target_pairs={{1,0},{2,1},{3,2},{5,4},{6,5},{7,6},{9,8},{10,9},{11,10},{13,12},{... | collective-permute-start | bytes 368648 | tf_op jit(solution)/shard_map/ppermute | solution.py:406
  34.1 4.1 %collective-permute-start.6 = (f32[128,128]{1,0:T(8,128)S(1)}, f32[128,128]{1,0:T(8,128)S(1)}, u32[]{:S(2)}, u32[]{:S(2)}) collective-permute-start(f32[128,128]{1,0:T(8,128)S(1)} %bitcast.8), channel_id=1, source_target_pairs={{0,3},{1,0},{2,1},{3,2},{4,7},{5,4},{6,5},{7,6},{8,11},{9,8},{10,9... | collective-permute-start | bytes 196616 | tf_op jit(solution)/shard_map/ppermute | solution.py:385
  36.9 4.7 %collective-permute-start.5 = (f32[128,128]{1,0:T(8,128)S(1)}, f32[128,128]{1,0:T(8,128)S(1)}, u32[]{:S(2)}, u32[]{:S(2)}) collective-permute-start(f32[128,128]{1,0:T(8,128)S(1)} %bitcast.9), channel_id=1, source_target_pairs={{0,2},{1,3},{2,0},{3,1},{4,6},{5,7},{6,4},{7,5},{8,10},{9,11},{10,... | collective-permute-start | bytes 196616 | tf_op jit(solution)/shard_map/ppermute | solution.py:385
  37.2 5.9 %collective-permute-start.4 = (f32[128,128]{1,0:T(8,128)S(1)}, f32[128,128]{1,0:T(8,128)S(1)}, u32[]{:S(2)}, u32[]{:S(2)}) collective-permute-start(f32[128,128]{1,0:T(8,128)S(1)} %bitcast.10), channel_id=1, source_target_pairs={{0,1},{1,2},{2,3},{3,0},{4,5},{5,6},{6,7},{7,4},{8,9},{9,10},{10,1... | collective-permute-start | bytes 196616 | tf_op jit(solution)/shard_map/ppermute | solution.py:385
  45.6 8.2 %copy-start.8 = (f32[15,4,512]{2,1,0:T(4,128)}, f32[15,4,512]{2,1,0:T(4,128)S(1)}, u32[]{:S(2)}) copy-start(f32[15,4,512]{2,1,0:T(4,128)S(1)} %collective-permute-done.2.y_low) | copy-start | bytes 368644
  45.6 8.2 %copy-start.9 = (f32[15,4,512]{2,1,0:T(4,128)}, f32[15,4,512]{2,1,0:T(4,128)S(1)}, u32[]{:S(2)}) copy-start(f32[15,4,512]{2,1,0:T(4,128)S(1)} %collective-permute-done.3.y_high) | copy-start | bytes 368644
  45.6 20.2 %all-to-all-start.1 = ((f32[64,8,128]{2,1,0:T(8,128)}), f32[64,8,128]{2,1,0:T(8,128)S(1)}, u32[]{:S(2)}, u32[]{:S(2)}) async-start(f32[64,8,128]{2,1,0:T(8,128)} %bitcast.6), calls=%async_computation.1 | async-start | bytes 524288 | tf_op jit(solution)/shard_map/all_to_all | solution.py:408
  65.8 0.7 copy-start.5

commit v3 on v2

--- a/solution.py
+++ b/solution.py
@@ -24,6 +24,8 @@
 GS = 21
 TILE = 40
 TILES = 16
+ROWS = 384
+STEP = 8
 
 F32, BF16 = jnp.float32, jnp.bfloat16
 
@@ -80,7 +82,7 @@
 
 def make_constants():
     rz, ry, rx = restriction_twice(NZ), restriction_twice(NY), restriction_twice(NX)
-    restrict_x = rx.T.astype(ml_dtypes.bfloat16)
+    restrict_x = np.concatenate([rx[0::2], rx[1::2]]).T.astype(ml_dtypes.bfloat16)
     restrict_zy = np.zeros((3, SUBS, CZ, CY, 128))
     for kind, p in enumerate(SLAB_KINDS):
         mz = window(rz, 2 * p - 1, TZ, CZ * p, CZ)
@@ -124,19 +126,19 @@
         part = window(rz.T, CZ * p - 1, CZ + 3, 2 * p - 1, TZ)
         for zo in range(TZ):
             prolong_z[kind, :, : CZ + 3, zo * TYS : zo * TYS + TY] = part[None, :, zo, None]
-    prolong_z = prolong_z.reshape(3, 8 * FZ, 128).astype(np.float32)
+    prolong_z = prolong_z.reshape(3, 8 * FZ, 128).astype(ml_dtypes.bfloat16)
     near_x = np.zeros((NX, FX))
     for node in range(NX):
         for offset in range(-2, 3):
             if 0 <= node + offset < NX:
                 near_x[node + offset, node + 1] = NEAR_WEIGHT * NEAR[abs(offset)]
     return dict(
-        near_x=halves(near_x),
+        near_x=np.concatenate(halves(near_x)),
         restrict_x=restrict_x,
         restrict_zy=restrict_zy,
         span_y=halves(span_y),
         span_z=halves(span_z),
-        fine_x=halves(fine_x),
+        fine_x=np.concatenate(halves(fine_x)),
         prolong_y=prolong_y,
         prolong_z=prolong_z,
     )
@@ -145,35 +147,43 @@
 CONSTANTS = make_constants()
 
 
-def restrict_kernel(place, charge, along_x, along_zy, out, first_planes, last_planes):
-    first_planes[...] = charge[0:4]
-    last_planes[...] = charge[CZ - 3 : CZ]
+def restrict_kernel(place, charge, along_x, along_zy, source, out, first, last, sems):
+    copies = [
+        pltpu.make_async_copy(source.at[pl.ds(0, 4)], first, sems.at[0]),
+        pltpu.make_async_copy(source.at[pl.ds(CZ - 3, 3)], last, sems.at[1]),
+    ]
+    for copy in copies:
+        copy.start()
     values = charge[...].reshape(CZ * CY, NX)
     high, low = split(values)
     narrow = dot(high, along_x[...]) + dot(low, along_x[...])
     narrow_high, narrow_low = split(narrow.T)
     zy_high, zy_low = split(along_zy[0])
-    out[...] = dot3(narrow_high, narrow_low, zy_high, zy_low)
-
-
-def middle_kernel(place, own, one, two, three, y_high, y_low, z_high, z_low, out):
+    partial = dot3(narrow_high, narrow_low, zy_high, zy_low)
+    for x in range(2):
+        for q in range(SUBS):
+            out[pl.ds(2 * q + x, SLABS, stride=8), :] = partial[x * SLABS : (x + 1) * SLABS]
+    for copy in copies:
+        copy.wait()
+
+
+def middle_kernel(place, pencil, y_high, y_low, z_high, z_low, out):
     q = place[1]
     lane = lax.broadcasted_iota(jnp.int32, (SLABS, 128), 1)
     gathered = [None] * TZ
-    for back, ref in enumerate((own, one, two, three)):
-        source = lax.rem(q + (SUBS - back), SUBS)
+    for source in range(SUBS):
         for x in range(2):
-            rows = ref[pl.ds(x, SLABS, stride=2), :]
+            rows = pencil[pl.ds(2 * source + x, SLABS, stride=8), :]
             first = 64 * x - 1 + 16 * source
             inside = (lane >= first) & (lane < first + TY)
             for zt in range(TZ):
-                shift = lax.rem(first + (256 - TYS * zt), 128)
+                shift = (first + 256 - TYS * zt) % 128
                 term = jnp.where(inside, pltpu.roll(rows, shift, 1), 0.0)
                 gathered[zt] = term if gathered[zt] is None else gathered[zt] + term
     even = gathered[1] + pltpu.roll(gathered[3], 1, 0)
     odd = gathered[2] + pltpu.roll(gathered[4], 1, 0) + pltpu.roll(gathered[0], SLABS - 1, 0)
     top_high, top_low = split(jnp.concatenate([even, odd], axis=0))
-    mixed = dot3(top_high, top_low, y_high[0], y_low[0])
+    mixed = dot3(top_high, top_low, y_high[q], y_low[q])
     stacked = jnp.concatenate([mixed[:, :128], mixed[:, 128:256], mixed[:, 256:]], axis=0)
     stacked_high, stacked_low = split(stacked)
     folded = dot3(z_high[...], z_low[...], stacked_high, stacked_low)
@@ -189,7 +199,44 @@
         out[pl.ds(g, SLABS, stride=8), :] = jnp.zeros((SLABS, 128), F32)
 
 
-def near_kernel(place, charge, z_low, z_high, y_low, y_high, x_high, x_low, out, rows, wide):
+def fetch(sources, targets, sems):
+    copies = [
+        pltpu.make_async_copy(source, target, sems.at[i])
+        for i, (source, target) in enumerate(zip(sources, targets))
+    ]
+    for copy in copies:
+        copy.start()
+    return copies
+
+
+def near_kernel(
+    place,
+    charge_in,
+    z_low_in,
+    z_high_in,
+    y_low_in,
+    y_high_in,
+    along_x_in,
+    out,
+    charge,
+    z_low,
+    z_high,
+    y_low,
+    y_high,
+    along_x,
+    rows,
+    wide,
+    grid,
+    sems,
+    out_sems,
+):
+    copies = fetch(
+        (charge_in, z_low_in, z_high_in, y_low_in, y_high_in, along_x_in),
+        (charge, z_low, z_high, y_low, y_high, along_x),
+        sems,
+    )
+    for copy in copies[:5]:
+        copy.wait()
     p, q = place[0], place[1]
 
     def stencil(at):
@@ -220,14 +267,23 @@
         for piece in range(NX // 128):
             wide[piece, pl.ds(zo, FY, stride=FZ), :] = jnp.zeros((FY, 128), F32)
 
-    def step(i, carry):
-        at = pl.ds(pl.multiple_of(128 * i, 128), 128)
+    copies[5].wait()
+    stores = []
+    for i in range(FY * FZ // ROWS):
+        at = pl.ds(ROWS * i, ROWS)
         values = jnp.concatenate([wide[c, at, :] for c in range(NX // 128)], axis=1)
         high, low = split(values)
-        out[at, :] = dot3(high, low, x_high[...], x_low[...])
-        return carry
-
-    lax.fori_loop(0, FY * FZ // 128, step, 0)
+        for k0, k1, n0, n1 in ((0, 384, 0, 256), (128, 512, 256, 512), (384, 512, 512, 640)):
+            grid[at, n0:n1] = dot3(
+                high[:, k0:k1],
+                low[:, k0:k1],
+                along_x[k0:k1, n0:n1],
+                along_x[NX + k0 : NX + k1, n0:n1],
+            )
+        stores.append(pltpu.make_async_copy(grid.at[at], out.at[at], out_sems.at[i]))
+        stores[-1].start()
+    for store in stores:
+        store.wait()
 
 
 def spline_pair(distance):
@@ -241,48 +297,83 @@
 
 
 def atoms_kernel(
-    place, cell, count, near, arrived, x_high, x_low, along_y, along_z, offset, out, table, top
+    place,
+    cell,
+    count,
+    arrived,
+    near_in,
+    along_x_in,
+    along_y_in,
+    along_z_in,
+    offset_in,
+    out,
+    near,
+    along_x,
+    along_y,
+    along_z,
+    offset,
+    table,
+    grid,
+    turned,
+    fields,
+    in_sems,
+    sems,
 ):
+    copies = fetch(
+        (
+            along_x_in,
+            along_y_in.at[place[1]],
+            along_z_in.at[place[2]],
+            near_in,
+            offset_in,
+        ),
+        (along_x, along_y, along_z, near, offset),
+        in_sems,
+    )
     top_high, top_low = split(arrived[...].T)
-    potential = dot3(top_high, top_low, x_high[...], x_low[...])
-    high, low = split(potential)
-    top[0:128] = high
-    top[128:256] = low
-    lane = lax.broadcasted_iota(jnp.int32, (128, 128), 1)
+    copies[0].wait()
+    top = dot3(top_high, top_low, along_x[0:512], along_x[512:1024])
+    high, low = split(top)
+    twice = jnp.concatenate([high, high], axis=0)
+    for copy in copies[1:]:
+        copy.wait()
+    z_weight = jnp.concatenate([along_z[...].astype(F32)] * (ROWS // 128), axis=0)
+    for i in range(FY * FZ // ROWS):
+        at = pl.ds(ROWS * i, ROWS)
+        weight_high, weight_low = split(along_y[at, :].astype(F32) * z_weight)
+        both = jnp.concatenate([weight_high, weight_low], axis=1)
+        grid[at, :] = near[at, :] + (dot(both, twice) + dot(weight_high, low))
+
+    lane = lax.broadcasted_iota(jnp.int32, (32, 128), 1)
 
     def build(i, carry):
-        at = pl.ds(pl.multiple_of(128 * i, 128), 128)
-        weight_high, weight_low = split(along_y[0, at, :].astype(F32) * along_z[0])
-        fine = near[at, :] + dot3(weight_high, weight_low, top[0:128], top[128:256])
-        fine_high = fine.astype(BF16).astype(F32)
-        fine_low = fine - fine_high
-        for t in range(TILES):
-            tile, first = divmod(32 * t, 128)
-
-            def moved(values, to):
-                here = values[:, 128 * tile : 128 * tile + 128]
-                here = pltpu.roll(here, (128 + to - first) % 128, 1) if to != first else here
-                if first + TILE <= 128:
-                    return here
-                after = values[:, 128 * tile + 128 : 128 * tile + 256]
-                after = pltpu.roll(after, (128 + to - first) % 128, 1)
-                return jnp.where(lane < to + 128 - first, here, after)
-
-            a = moved(fine_high, 0)
-            b = moved(fine_low, TILE)
-            c = pltpu.roll(a, 2 * TILE, 1)
-            row = jnp.where(lane < TILE, a, jnp.where(lane < 2 * TILE, b, c))
-            table[t, at, :] = row.astype(BF16)
+        at = pl.ds(pl.multiple_of(32 * i, 32), 32)
+        values = grid[at, :]
+        fine_high = values.astype(BF16).astype(F32)
+        fine_low = values - fine_high
+        h = [fine_high[:, 128 * c : 128 * c + 128] for c in range(5)]
+        b = [pltpu.roll(fine_low[:, 128 * c : 128 * c + 128], TILE, 1) for c in range(5)]
+        e = [pltpu.roll(h[c], 2 * TILE, 1) for c in range(5)]
+        for c in range(4):
+            for j in range(4):
+                one, two, three = h[c], b[c], e[c]
+                if j == 3:
+                    one = jnp.where(lane < 64, h[c + 1], one)
+                    two = jnp.where(lane >= TILE, b[c + 1], two)
+                    three = jnp.where(lane >= 2 * TILE, e[c + 1], three)
+                place_in = (lane + (128 - 32 * j)) & 127
+                row = jnp.where(place_in < TILE, one, jnp.where(place_in < 2 * TILE, two, three))
+                table[4 * c + j, at, :] = row.astype(BF16)
         return carry
 
-    lax.fori_loop(0, FY * FZ // 128, build, 0)
+    lax.fori_loop(0, (CY + 3) * FZ // 32 + 1, build, 0)
 
     row16 = lax.broadcasted_iota(jnp.int32, (16, 128), 0).astype(F32) - 1.0
     row40 = lax.broadcasted_iota(jnp.int32, (TILE, 128), 0).astype(F32) - 1.0
     slot = lax.broadcasted_iota(jnp.int32, (1, 128), 1)
     blank = jnp.zeros((8, 256), F32)
 
-    def block(b):
+    def block(b, k):
         at = pl.ds(pl.multiple_of(SLOT * b, SLOT), SLOT)
         t = cell[b]
         brick_y = lax.shift_right_logical(t, 6) & 7
@@ -297,7 +388,11 @@
         weights = jnp.concatenate([both_high, both_high, both - both_high, blank], axis=0)
         first = pl.multiple_of(128 * brick_y, 128)
         patch = table[tile, pl.ds(first, 11 * FZ), :]
-        product = dot(patch, weights.astype(BF16))
+        weights = weights.astype(BF16)
+        turned[k, 0:128] = weights
+        turned[k, 128:256] = weights
+        turn = pl.multiple_of(128 - 32 * (tile & 3), 32)
+        product = dot(patch, turned[k, pl.ds(turn, 128), :])
         base = along = cross = None
         for j in range(11):
             v = product[FZ * j : FZ * (j + 1), :128]
@@ -312,7 +407,7 @@
 
         live = jnp.where(slot < count[b], 1.0, 0.0)
         slope = live * (-1.0 / 72.0)
-        out[:, at] = jnp.concatenate(
+        fields[:, at] = jnp.concatenate(
             [
                 reduce(base * wz) * (live * (1.0 / 216.0)),
                 reduce(base * sz) * slope,
@@ -322,36 +417,40 @@
             axis=0,
         )
 
+    def copy(i):
+        at = pl.ds(pl.multiple_of(STEP * SLOT * i, STEP * SLOT), STEP * SLOT)
+        return pltpu.make_async_copy(fields.at[:, at], out.at[:, at], sems.at[i])
+
     def step(i, carry):
-        for k in range(8):
-            block(8 * i + k)
+        for k in range(STEP):
+            block(STEP * i + k, k)
+        copy(i).start()
         return carry
 
-    lax.fori_loop(0, BLOCKS // 8, step, 0)
+    lax.fori_loop(0, BLOCKS // STEP, step, 0)
+    for i in range(BLOCKS // STEP):
+        copy(i).wait()
 
 
 def whole(shape):
     return pl.BlockSpec(shape, lambda i, *_: (0,) * len(shape))
 
 
-def call(kernel, scalars, in_specs, out_spec, out_shape, scratch, megabytes, flops, moved):
+IN_VMEM = pl.BlockSpec(memory_space=pltpu.VMEM)
+IN_SMEM = pl.BlockSpec(memory_space=pltpu.SMEM)
+ANYWHERE = pl.BlockSpec(memory_space=pl.ANY)
+
+
+def call(kernel, scalars, near_by, far, out_shape, out_spec, scratch, megabytes, flops, moved):
     return pl.pallas_call(
         kernel,
-        grid_spec=pltpu.PrefetchScalarGridSpec(
-            num_scalar_prefetch=scalars,
-            grid=(1,),
-            in_specs=in_specs,
-            out_specs=out_spec,
-            scratch_shapes=scratch,
-        ),
-        out_shape=jax.tree.map(
-            lambda shape: jax.ShapeDtypeStruct(shape, F32),
-            out_shape,
-            is_leaf=lambda shape: isinstance(shape, tuple),
-        ),
+        in_specs=[IN_SMEM] * len(scalars) + [IN_VMEM] * len(near_by) + [ANYWHERE] * len(far),
+        out_specs=out_spec,
+        out_shape=jax.ShapeDtypeStruct(out_shape, F32),
+        scratch_shapes=scratch,
         compiler_params=pltpu.CompilerParams(vmem_limit_bytes=megabytes * 2**20),
         cost_estimate=pl.CostEstimate(flops=flops, bytes_accessed=moved, transcendentals=0),
-    )
+    )(*scalars, *near_by, *far)
 
 
 def on_device(charge_grid, atom_offset, block_cell, block_count):
@@ -365,97 +464,99 @@
     up_sub = [(i, i + 1) for i in range(SUBS - 1)]
     down_sub = [(b, a) for a, b in up_sub]
 
-    partial, first_planes, last_planes = call(
+    partial, first_planes, last_planes = pl.pallas_call(
         restrict_kernel,
-        1,
-        [
-            whole((CZ, CY, NX)),
-            whole((NX, 128)),
-            pl.BlockSpec((1, CZ * CY, 128), lambda i, place: (place[3], 0, 0)),
+        grid_spec=pltpu.PrefetchScalarGridSpec(
+            num_scalar_prefetch=1,
+            grid=(1,),
+            in_specs=[
+                whole((CZ, CY, NX)),
+                whole((NX, 128)),
+                pl.BlockSpec((1, CZ * CY, 128), lambda i, place: (place[3], 0, 0)),
+                ANYWHERE,
+            ],
+            out_specs=[whole((512, 128)), ANYWHERE, ANYWHERE],
+            scratch_shapes=[pltpu.SemaphoreType.DMA((2,))],
+        ),
+        out_shape=[
+            jax.ShapeDtypeStruct((512, 128), F32),
+            jax.ShapeDtypeStruct((4, CY, NX), F32),
+            jax.ShapeDtypeStruct((3, CY, NX), F32),
         ],
-        [whole((128, 128)), whole((4, CY, NX)), whole((3, CY, NX))],
-        [(128, 128), (4, CY, NX), (3, CY, NX)],
-        [],
-        60,
-        2 * 10**8,
-        2 * 10**6,
-    )(place, charge_grid, consts["restrict_x"], consts["restrict_zy"])
-    pencil = lax.all_to_all(partial, "slab", 0, 0, tiled=True)
-    others = [
-        lax.ppermute(pencil, "sub", [(i, (i + k) % SUBS) for i in range(SUBS)]) for k in (1, 2, 3)
-    ]
-    y_high, y_low = consts["span_y"]
-    z_high, z_low = consts["span_z"]
-    by_sub = pl.BlockSpec((1, 128, 384), lambda i, place: (place[1], 0, 0))
-    folded = call(
-        middle_kernel,
-        1,
-        [whole((128, 128))] * 4 + [by_sub, by_sub, whole((320, 384)), whole((320, 384))],
-        whole((512, 128)),
-        (512, 128),
-        [],
-        32,
-        2 * 10**8,
-        2 * 10**6,
-    )(place, pencil, *others, y_high, y_low, z_high, z_low)
+        compiler_params=pltpu.CompilerParams(vmem_limit_bytes=60 * 2**20),
+        cost_estimate=pl.CostEstimate(flops=10**8, bytes_accessed=10**6, transcendentals=0),
+    )(place, charge_grid, consts["restrict_x"], consts["restrict_zy"], charge_grid)
+    pencil = lax.all_to_all(partial, ("slab", "sub"), 0, 0, tiled=True)
+
     below = lax.ppermute(last_planes, "slab", up)
     above = lax.ppermute(first_planes, "slab", down)
     left = jnp.concatenate([below[:, CY - 4 :], charge_grid[:, CY - 4 :], above[:, CY - 4 :]], axis=0)
     right = jnp.concatenate([below[:, :4], charge_grid[:, :4], above[:, :4]], axis=0)
     left = lax.ppermute(left, "sub", up_sub)
     right = lax.ppermute(right, "sub", down_sub)
-    left, right, folded = lax.optimization_barrier((left, right, folded))
+    pencil, left, right = lax.optimization_barrier((pencil, left, right))
+
+    folded = call(
+        middle_kernel,
+        [place],
+        [pencil, *consts["span_y"], *consts["span_z"]],
+        [],
+        (512, 128),
+        IN_VMEM,
+        [],
+        12,
+        2 * 10**8,
+        2 * 10**6,
+    )
     arrived = lax.all_to_all(folded, "slab", 0, 0, tiled=True)
+    left, right, _ = lax.optimization_barrier((left, right, folded))
     near = call(
         near_kernel,
-        1,
+        [place],
+        [],
+        [charge_grid, below, above, left, right, consts["near_x"]],
+        (FY * FZ, FX),
+        ANYWHERE,
         [
-            whole((CZ, CY, NX)),
-            whole((3, CY, NX)),
-            whole((4, CY, NX)),
-            whole((15, 4, NX)),
-            whole((15, 4, NX)),
-            whole((NX, FX)),
-            whole((NX, FX)),
+            pltpu.VMEM((CZ, CY, NX), F32),
+            pltpu.VMEM((3, CY, NX), F32),
+            pltpu.VMEM((4, CY, NX), F32),
+            pltpu.VMEM((15, 4, NX), F32),
+            pltpu.VMEM((15, 4, NX), F32),
+            pltpu.VMEM((2 * NX, FX), BF16),
+            pltpu.VMEM((CY + 24, NX), F32),
+            pltpu.VMEM((NX // 128, FY * FZ, 128), F32),
+            pltpu.VMEM((FY * FZ, FX), F32),
+            pltpu.SemaphoreType.DMA((6,)),
+            pltpu.SemaphoreType.DMA((FY * FZ // ROWS,)),
         ],
-        whole((FY * FZ, FX)),
-        (FY * FZ, FX),
-        [pltpu.VMEM((CY + 24, NX), F32), pltpu.VMEM((NX // 128, FY * FZ, 128), F32)],
         60,
         2 * 10**9,
         16 * 10**6,
-    )(place, charge_grid, below, above, left, right, *consts["near_x"])
-
-    x_high, x_low = consts["fine_x"]
+    )
     return call(
         atoms_kernel,
-        3,
+        [place, block_cell, block_count],
+        [arrived],
+        [near, consts["fine_x"], consts["prolong_y"], consts["prolong_z"], atom_offset],
+        (4, BLOCKS * SLOT),
+        ANYWHERE,
         [
-            whole((FY * FZ, FX)),
-            whole((512, 128)),
-            whole((512, FX)),
-            whole((512, FX)),
-            pl.BlockSpec((1, FY * FZ, 128), lambda i, place, *_: (place[1], 0, 0)),
-            pl.BlockSpec((1, 128, 128), lambda i, place, *_: (place[2], 0, 0)),
-            whole((3, BLOCKS * SLOT)),
+            pltpu.VMEM((FY * FZ, FX), F32),
+            pltpu.VMEM((1024, FX), BF16),
+            pltpu.VMEM((FY * FZ, 128), BF16),
+            pltpu.VMEM((128, 128), BF16),
+            pltpu.VMEM((3, BLOCKS * SLOT), F32),
+            pltpu.VMEM((TILES, FY * FZ, 128), BF16),
+            pltpu.VMEM((FY * FZ, FX), F32),
+            pltpu.VMEM((STEP, 256, 256), BF16),
+            pltpu.VMEM((4, BLOCKS * SLOT), F32),
+            pltpu.SemaphoreType.DMA((5,)),
+            pltpu.SemaphoreType.DMA((BLOCKS // STEP,)),
         ],
-        whole((4, BLOCKS * SLOT)),
-        (4, BLOCKS * SLOT),
-        [pltpu.VMEM((TILES, FY * FZ, 128), BF16), pltpu.VMEM((256, FX), BF16)],
         60,
         10**9,
         8 * 10**6,
-    )(
-        place,
-        block_cell,
-        block_count,
-        near,
-        arrived,
-        x_high,
-        x_low,
-        consts["prolong_y"],
-        consts["prolong_z"],
-        atom_offset,
     )
 
 

time: 85.4 us -> 110 us (1.29)
  Pallas kernels: 36.2 us -> 59.2 us
  waiting for transfers between devices: 9.97 us -> 13.8 us
  starting transfers between devices: 36.2 us -> 34.1 us
    pallas_call x4, Pallas kernels: 36.2 us -> 59.2 us  [the longest x1 31.6 us: on_device(): pl.pallas_call(restrict_kernel, grid_spec=pltpu.PrefetchScalarGridSpec(nu...]
    all_to_all x1, waiting for transfers between devices: 4.11 us -> 9.94 us  [on_device(): pencil = lax.all_to_all(partial, ('slab', 'sub'), 0, 0, tiled=True)]
    ppermute x3 -> x0, waiting for transfers between devices: 5.21 us -> none  [on_device(): lax.ppermute(pencil, 'sub', [(i, (i + k) % SUBS) for i in range(SUBS)])]
    ppermute x3 -> x0, starting transfers between devices: 3.77 us -> none  [on_device(): lax.ppermute(pencil, 'sub', [(i, (i + k) % SUBS) for i in range(SUBS)])]
    all_to_all x1, waiting for transfers between devices: 0.63 us -> 3.85 us  [on_device(): arrived = lax.all_to_all(folded, 'slab', 0, 0, tiled=True)]
    all_to_all x1, starting transfers between devices: 12.9 us -> 15.6 us  [on_device(): pencil = lax.all_to_all(partial, ('slab', 'sub'), 0, 0, tiled=True)]
    all_to_all x1, starting transfers between devices: 8.15 us -> 6.98 us  [on_device(): arrived = lax.all_to_all(folded, 'slab', 0, 0, tiled=True)]
  transfers between devices with their start and end apart: 9 -> 6, of which waited for: 5 -> 2; matrix products, arithmetic and copies ran while one was open for 1% -> 1% of each run, Pallas kernels for 16% -> 7%
where the time goes in v3:
time: 110 us
  Pallas kernels  59.2 us (54%)
  starting transfers between devices  34.1 us (31%)
  waiting for transfers between devices  13.8 us (13%)
  local copies, waits for them, and re-layouts  1.78 us (2%)
    pallas_call x1, Pallas kernels, on_device(): pl.pallas_call(restrict_kernel, grid_spec=pltpu.PrefetchScalarGridSpec(nu...  31.6 us
    pallas_call x3, Pallas kernels, call(): pl.pallas_call(kernel, in_specs=[IN_SMEM] * len(scalars) + [IN_VMEM] * le...  27.6 us
    all_to_all x1, starting transfers between devices, on_device(): pencil = lax.all_to_all(partial, ('slab', 'sub'), 0, 0, tiled=True)  15.6 us
    all_to_all x1, waiting for transfers between devices, on_device(): pencil = lax.all_to_all(partial, ('slab', 'sub'), 0, 0, tiled=True)  9.94 us
    all_to_all x1, starting transfers between devices, on_device(): arrived = lax.all_to_all(folded, 'slab', 0, 0, tiled=True)  6.98 us
    ppermute x1, starting transfers between devices, on_device(): below = lax.ppermute(last_planes, 'slab', up)  5.07 us
    all_to_all x1, waiting for transfers between devices, on_device(): arrived = lax.all_to_all(folded, 'slab', 0, 0, tiled=True)  3.85 us
    ppermute x1, starting transfers between devices, on_device(): left = lax.ppermute(left, 'sub', up_sub)  3.3 us
  transfers between devices with their start and end apart: 6, of which 2 were waited for; matrix products, arithmetic and copies ran while one was open for 1% of the time, Pallas kernels for 7%

profile of v3, /device:TPU:1, one launch (start us, length us, event | category | flops | bytes accessed | tf_op | source)
XLA Modules:
  0.0 109.8 jit_solution(589460445955176858)
XLA Ops:
  0.0 0.6 pad_add_fusion.place
  0.6 31.6 %shard_map.136 = (f32[512,128]{1,0:T(8,128)}, f32[4,64,512]{2,1,0:T(8,128)}, f32[3,64,512]{2,1,0:T(8,128)}) custom-call(s32[4]{0:T(128)} %pad_add_fusion.place, f32[8,64,512]{2,1,0:T(8,128)} %charge_in.1, bf16[512,128]{1,0:T(8,128)(2,1)} %constant.39.clone.along_x, f32[12,512,128]{2,1,0:T(8,128)} %constant.40.clone.along_zy, f32[8,64,512]{2,1,0:T(8,128)} %charge_in.1), custom_call_target="tpu_custom_call" | custom-call | flops 100000000 | bytes 1000000 | tf_op jit(solution)/shard_map/pallas_call | solution.py:467
  32.2 0.0 copy-start
  32.3 0.0 copy-start.1
  32.3 0.0 copy-start.2
  32.3 0.0 copy-start.3
  32.3 0.0 copy-start.4
  32.3 5.1 %collective-permute-start = (f32[3,64,512]{2,1,0:T(8,128)}, f32[3,64,512]{2,1,0:T(8,128)S(1)}, u32[]{:S(2)}, u32[]{:S(2)}) collective-permute-start(f32[3,64,512]{2,1,0:T(8,128)} %get-tuple-element.14), channel_id=1, source_target_pairs={{0,4},{4,8},{8,12},{12,16},{16,20},{20,24},{24,28},{28,32},{32,36}... | collective-permute-start | bytes 1179656 | tf_op jit(solution)/shard_map/ppermute | solution.py:491
  37.4 1.9 %collective-permute-start.1 = (f32[4,64,512]{2,1,0:T(8,128)}, f32[4,64,512]{2,1,0:T(8,128)S(1)}, u32[]{:S(2)}, u32[]{:S(2)}) collective-permute-start(f32[4,64,512]{2,1,0:T(8,128)} %get-tuple-element.15), channel_id=1, source_target_pairs={{4,0},{8,4},{12,8},{16,12},{20,16},{24,20},{28,24},{32,28},{36,32}... | collective-permute-start | bytes 1572872 | tf_op jit(solution)/shard_map/ppermute | solution.py:492
  39.3 15.6 %all-to-all-start = ((f32[256,2,128]{2,1,0:T(2,128)}), f32[256,2,128]{2,1,0:T(2,128)S(1)}, u32[]{:S(2)}, u32[]{:S(2)}) async-start(f32[256,2,128]{2,1,0:T(2,128)} %bitcast.10), calls=%async_computation | async-start | bytes 524288 | tf_op jit(solution)/shard_map/all_to_all | solution.py:489
  54.9 1.0 fusion
  55.9 0.0 collective-permute-done.z_low_in
  55.9 0.0 copy-start.7
  55.9 0.0 collective-permute-done.1.z_high_in
  55.9 0.0 copy-start.6
  56.0 3.3 %collective-permute-start.2 = (f32[15,4,512]{2,1,0:T(4,128)S(1)}, f32[15,4,512]{2,1,0:T(4,128)S(1)}, u32[]{:S(2)}, u32[]{:S(2)}) collective-permute-start(f32[15,4,512]{2,1,0:T(4,128)S(1)} %pad_maximum_fusion), channel_id=1, source_target_pairs={{0,1},{1,2},{2,3},{4,5},{5,6},{6,7},{8,9},{9,10},{10,11},{12,13},{... | collective-permute-start | bytes 368648 | tf_op jit(solution)/shard_map/ppermute | solution.py:495
  59.4 1.3 %collective-permute-start.3 = (f32[15,4,512]{2,1,0:T(4,128)S(1)}, f32[15,4,512]{2,1,0:T(4,128)S(1)}, u32[]{:S(2)}, u32[]{:S(2)}) collective-permute-start(f32[15,4,512]{2,1,0:T(4,128)S(1)} %pad_maximum_fusion.1), channel_id=1, source_target_pairs={{1,0},{2,1},{3,2},{5,4},{6,5},{7,6},{9,8},{10,9},{11,10},{13,12},{... | collective-permute-start | bytes 368648 | tf_op jit(solution)/shard_map/ppermute | solution.py:496
  60.7 9.9 %all-to-all-done = f32[256,2,128]{2,1,0:T(2,128)S(1)} async-done(((f32[256,2,128]{2,1,0:T(2,128)}), f32[256,2,128]{2,1,0:T(2,128)S(1)}, u32[]{:S(2)}, u32[]{:S(2)}) %all-to-all-start) | async-done | bytes 262176 | tf_op jit(solution)/shard_map/all_to_all | solution.py:489
  70.6 0.0 collective-permute-done.2.y_low_in
  70.6 0.0 copy-start.8
  70.6 0.0 collective-permute-done.3.y_high_in
  70.6 0.0 copy-start.9
  70.6 0.0 copy-done
  70.6 0.0 copy-done.1
  70.6 0.0 copy-done.2
  70.7 0.0 copy-done.3
  70.7 0.0 copy-done.4
  70.7 2.4 %shard_map.137 = f32[512,128]{1,0:T(8,128)} custom-call(s32[4]{0:T(128)S(1)} %copy-done.4, f32[512,128]{1,0:T(8,128)S(1)} %bitcast.8, bf16[4,128,384]{2,1,0:T(8,128)(2,1)S(1)} %copy-done.1, bf16[4,128,384]{2,1,0:T(8,128)(2,1)S(1)} %copy-done, bf16[320,384]{1,0:T(8,128)(2,1)S(1)} %copy-done.3, bf16[320,384]{1,0:T(8,128)(2,1)S(1)} %copy-done.2), custom_call_target="tpu_custom_call" | custom-call | flops 200000000 | bytes 2000000 | tf_op jit(solution)/shard_map/pallas_call | solution.py:445
  73.1 0.0 copy-done.7
  73.1 0.0 copy-done.6
  73.1 7.0 %all-to-all-start.1 = ((f32[64,8,128]{2,1,0:T(8,128)}), f32[64,8,128]{2,1,0:T(8,128)S(1)}, u32[]{:S(2)}, u32[]{:S(2)}) async-start(f32[64,8,128]{2,1,0:T(8,128)} %bitcast.6), calls=%async_computation.1 | async-start | bytes 524288 | tf_op jit(solution)/shard_map/all_to_all | solution.py:511
  80.1 0.0 copy-done.8
  80.1 0.0 copy-done.9
  80.1 8.1 %shard_map.138.near_in = f32[1152,640]{1,0:T(8,128)} custom-call(s32[4]{0:T(128)} %pad_add_fusion.place, f32[8,64,512]{2,1,0:T(8,128)} %charge_in.1, f32[3,64,512]{2,1,0:T(8,128)} %copy-done.7, f32[4,64,512]{2,1,0:T(8,128)} %copy-done.6, f32[15,4,512]{2,1,0:T(4,128)} %copy-done.8, f32[15,4,512]{2,1,0:T(4,128)} %copy-done.9, ...), custom_call_target="tpu_custom_call" | custom-call | flops 2000000000 | bytes 16000000 | tf_op jit(solution)/shard_map/pallas_call | solution.py:445
  88.3 3.9 %all-to-all-done.1 = f32[64,8,128]{2,1,0:T(8,128)S(1)} async-done(((f32[64,8,128]{2,1,0:T(8,128)}), f32[64,8,128]{2,1,0:T(8,128)S(1)}, u32[]{:S(2)}, u32[]{:S(2)}) %all-to-all-start.1) | async-done | bytes 262176 | tf_op jit(solution)/shard_map/all_to_all | solution.py:511
  92.1 0.0 copy-start.5
  92.1 0.7 copy-done.5
  92.8 17.0 %shard_map.139 = f32[4,16384]{1,0:T(4,128)} custom-call(s32[4]{0:T(128)} %pad_add_fusion.place, s32[128]{0:T(128)} %cell.1, s32[128]{0:T(128)} %count.1, f32[512,128]{1,0:T(8,128)} %bitcast.9, f32[1152,640]{1,0:T(8,128)} %shard_map.138.near_in, bf16[1024,640]{1,0:T(8,128)(2,1)} %constant.46.clone.along_x_in, ...), custom_call_target="tpu_custom_call" | custom-call | flops 1000000000 | bytes 8000000 | tf_op jit(solution)/shard_map/pallas_call | solution.py:445
  (4 shorter events, 0.1 us)
Async XLA Ops:
  32.2 38.4 %copy-start = (bf16[4,128,384]{2,1,0:T(8,128)(2,1)S(1)}, bf16[4,128,384]{2,1,0:T(8,128)(2,1)}, u32[]{:S(2)}) copy-start(bf16[4,128,384]{2,1,0:T(8,128)(2,1)} %constant.42.clone.y_low) | copy-start | bytes 1179652
  32.3 38.4 %copy-start.1 = (bf16[4,128,384]{2,1,0:T(8,128)(2,1)S(1)}, bf16[4,128,384]{2,1,0:T(8,128)(2,1)}, u32[]{:S(2)}) copy-start(bf16[4,128,384]{2,1,0:T(8,128)(2,1)} %constant.41.clone.y_high) | copy-start | bytes 1179652
  32.3 38.4 %copy-start.2 = (bf16[320,384]{1,0:T(8,128)(2,1)S(1)}, bf16[320,384]{1,0:T(8,128)(2,1)}, u32[]{:S(2)}) copy-start(bf16[320,384]{1,0:T(8,128)(2,1)} %constant.44.clone.z_low) | copy-start | bytes 737284
  32.3 38.4 %copy-start.3 = (bf16[320,384]{1,0:T(8,128)(2,1)S(1)}, bf16[320,384]{1,0:T(8,128)(2,1)}, u32[]{:S(2)}) copy-start(bf16[320,384]{1,0:T(8,128)(2,1)} %constant.43.clone.z_high) | copy-start | bytes 737284
  32.3 38.4 %copy-start.4 = (s32[4]{0:T(128)S(1)}, s32[4]{0:T(128)}, u32[]{:S(2)}) copy-start(s32[4]{0:T(128)} %pad_add_fusion.place) | copy-start | bytes 52
  32.3 23.6 %collective-permute-start = (f32[3,64,512]{2,1,0:T(8,128)}, f32[3,64,512]{2,1,0:T(8,128)S(1)}, u32[]{:S(2)}, u32[]{:S(2)}) collective-permute-start(f32[3,64,512]{2,1,0:T(8,128)} %get-tuple-element.14), channel_id=1, source_target_pairs={{0,4},{4,8},{8,12},{12,16},{16,20},{20,24},{24,28},{28,32},{32,36}... | collective-permute-start | bytes 1179656 | tf_op jit(solution)/shard_map/ppermute | solution.py:491
  37.4 18.6 %collective-permute-start.1 = (f32[4,64,512]{2,1,0:T(8,128)}, f32[4,64,512]{2,1,0:T(8,128)S(1)}, u32[]{:S(2)}, u32[]{:S(2)}) collective-permute-start(f32[4,64,512]{2,1,0:T(8,128)} %get-tuple-element.15), channel_id=1, source_target_pairs={{4,0},{8,4},{12,8},{16,12},{20,16},{24,20},{28,24},{32,28},{36,32}... | collective-permute-start | bytes 1572872 | tf_op jit(solution)/shard_map/ppermute | solution.py:492
  39.3 31.3 %all-to-all-start = ((f32[256,2,128]{2,1,0:T(2,128)}), f32[256,2,128]{2,1,0:T(2,128)S(1)}, u32[]{:S(2)}, u32[]{:S(2)}) async-start(f32[256,2,128]{2,1,0:T(2,128)} %bitcast.10), calls=%async_computation | async-start | bytes 524288 | tf_op jit(solution)/shard_map/all_to_all | solution.py:489
  55.9 17.2 %copy-start.7 = (f32[3,64,512]{2,1,0:T(8,128)}, f32[3,64,512]{2,1,0:T(8,128)S(1)}, u32[]{:S(2)}) copy-start(f32[3,64,512]{2,1,0:T(8,128)S(1)} %collective-permute-done.z_low_in) | copy-start | bytes 1179652
  55.9 17.2 %copy-start.6 = (f32[4,64,512]{2,1,0:T(8,128)}, f32[4,64,512]{2,1,0:T(8,128)S(1)}, u32[]{:S(2)}) copy-start(f32[4,64,512]{2,1,0:T(8,128)S(1)} %collective-permute-done.1.z_high_in) | copy-start | bytes 1572868
  56.0 14.6 %collective-permute-start.2 = (f32[15,4,512]{2,1,0:T(4,128)S(1)}, f32[15,4,512]{2,1,0:T(4,128)S(1)}, u32[]{:S(2)}, u32[]{:S(2)}) collective-permute-start(f32[15,4,512]{2,1,0:T(4,128)S(1)} %pad_maximum_fusion), channel_id=1, source_target_pairs={{0,1},{1,2},{2,3},{4,5},{5,6},{6,7},{8,9},{9,10},{10,11},{12,13},{... | collective-permute-start | bytes 368648 | tf_op jit(solution)/shard_map/ppermute | solution.py:495
  59.4 11.3 %collective-permute-start.3 = (f32[15,4,512]{2,1,0:T(4,128)S(1)}, f32[15,4,512]{2,1,0:T(4,128)S(1)}, u32[]{:S(2)}, u32[]{:S(2)}) collective-permute-start(f32[15,4,512]{2,1,0:T(4,128)S(1)} %pad_maximum_fusion.1), channel_id=1, source_target_pairs={{1,0},{2,1},{3,2},{5,4},{6,5},{7,6},{9,8},{10,9},{11,10},{13,12},{... | collective-permute-start | bytes 368648 | tf_op jit(solution)/shard_map/ppermute | solution.py:496
  70.6 9.5 %copy-start.8 = (f32[15,4,512]{2,1,0:T(4,128)}, f32[15,4,512]{2,1,0:T(4,128)S(1)}, u32[]{:S(2)}) copy-start(f32[15,4,512]{2,1,0:T(4,128)S(1)} %collective-permute-done.2.y_low_in) | copy-start | bytes 368644
  70.6 9.5 %copy-start.9 = (f32[15,4,512]{2,1,0:T(4,128)}, f32[15,4,512]{2,1,0:T(4,128)S(1)}, u32[]{:S(2)}) copy-start(f32[15,4,512]{2,1,0:T(4,128)S(1)} %collective-permute-done.3.y_high_in) | copy-start | bytes 368644
  73.1 19.0 %all-to-all-start.1 = ((f32[64,8,128]{2,1,0:T(8,128)}), f32[64,8,128]{2,1,0:T(8,128)S(1)}, u32[]{:S(2)}, u32[]{:S(2)}) async-start(f32[64,8,128]{2,1,0:T(8,128)} %bitcast.6), calls=%async_computation.1 | async-start | bytes 524288 | tf_op jit(solution)/shard_map/all_to_all | solution.py:511
  92.1 0.7 copy-start.5

commit v4 on v3

--- a/solution.py
+++ b/solution.py
@@ -147,13 +147,7 @@
 CONSTANTS = make_constants()
 
 
-def restrict_kernel(place, charge, along_x, along_zy, source, out, first, last, sems):
-    copies = [
-        pltpu.make_async_copy(source.at[pl.ds(0, 4)], first, sems.at[0]),
-        pltpu.make_async_copy(source.at[pl.ds(CZ - 3, 3)], last, sems.at[1]),
-    ]
-    for copy in copies:
-        copy.start()
+def restrict_kernel(place, charge, along_x, along_zy, out):
     values = charge[...].reshape(CZ * CY, NX)
     high, low = split(values)
     narrow = dot(high, along_x[...]) + dot(low, along_x[...])
@@ -163,8 +157,6 @@
     for x in range(2):
         for q in range(SUBS):
             out[pl.ds(2 * q + x, SLABS, stride=8), :] = partial[x * SLABS : (x + 1) * SLABS]
-    for copy in copies:
-        copy.wait()
 
 
 def middle_kernel(place, pencil, y_high, y_low, z_high, z_low, out):
@@ -231,7 +223,7 @@
     out_sems,
 ):
     copies = fetch(
-        (charge_in, z_low_in, z_high_in, y_low_in, y_high_in, along_x_in),
+        (charge_in, z_low_in.at[pl.ds(CZ - 3, 3)], z_high_in.at[pl.ds(0, 4)], y_low_in, y_high_in, along_x_in),
         (charge, z_low, z_high, y_low, y_high, along_x),
         sems,
     )
@@ -464,7 +456,9 @@
     up_sub = [(i, i + 1) for i in range(SUBS - 1)]
     down_sub = [(b, a) for a, b in up_sub]
 
-    partial, first_planes, last_planes = pl.pallas_call(
+    below = lax.ppermute(charge_grid, "slab", up)
+    above = lax.ppermute(charge_grid, "slab", down)
+    partial = pl.pallas_call(
         restrict_kernel,
         grid_spec=pltpu.PrefetchScalarGridSpec(
             num_scalar_prefetch=1,
@@ -473,25 +467,18 @@
                 whole((CZ, CY, NX)),
                 whole((NX, 128)),
                 pl.BlockSpec((1, CZ * CY, 128), lambda i, place: (place[3], 0, 0)),
-                ANYWHERE,
             ],
-            out_specs=[whole((512, 128)), ANYWHERE, ANYWHERE],
-            scratch_shapes=[pltpu.SemaphoreType.DMA((2,))],
+            out_specs=whole((512, 128)),
         ),
-        out_shape=[
-            jax.ShapeDtypeStruct((512, 128), F32),
-            jax.ShapeDtypeStruct((4, CY, NX), F32),
-            jax.ShapeDtypeStruct((3, CY, NX), F32),
-        ],
+        out_shape=jax.ShapeDtypeStruct((512, 128), F32),
         compiler_params=pltpu.CompilerParams(vmem_limit_bytes=60 * 2**20),
         cost_estimate=pl.CostEstimate(flops=10**8, bytes_accessed=10**6, transcendentals=0),
-    )(place, charge_grid, consts["restrict_x"], consts["restrict_zy"], charge_grid)
+    )(place, charge_grid, consts["restrict_x"], consts["restrict_zy"])
     pencil = lax.all_to_all(partial, ("slab", "sub"), 0, 0, tiled=True)
 
-    below = lax.ppermute(last_planes, "slab", up)
-    above = lax.ppermute(first_planes, "slab", down)
-    left = jnp.concatenate([below[:, CY - 4 :], charge_grid[:, CY - 4 :], above[:, CY - 4 :]], axis=0)
-    right = jnp.concatenate([below[:, :4], charge_grid[:, :4], above[:, :4]], axis=0)
+    planes = (below[CZ - 3 :], charge_grid, above[:4])
+    left = jnp.concatenate([plane[:, CY - 4 :] for plane in planes], axis=0)
+    right = jnp.concatenate([plane[:, :4] for plane in planes], axis=0)
     left = lax.ppermute(left, "sub", up_sub)
     right = lax.ppermute(right, "sub", down_sub)
     pencil, left, right = lax.optimization_barrier((pencil, left, right))

time: 110 us -> 82.1 us (0.75)
  Pallas kernels: 59.2 us -> 31.2 us
    pallas_call x1, Pallas kernels: 31.6 us -> 3.57 us  [on_device(): pl.pallas_call(restrict_kernel, grid_spec=pltpu.PrefetchScalarGridSpec(nu...]
    all_to_all x1, starting transfers between devices: 15.6 us -> 14.4 us  [on_device(): pencil = lax.all_to_all(partial, ('slab', 'sub'), 0, 0, tiled=True)]
  transfers between devices with their start and end apart: 6 -> 6, of which waited for: 2 -> 2; matrix products, arithmetic and copies ran while one was open for 1% -> 3% of each run, Pallas kernels for 7% -> 14%
where the time goes in v4:
time: 82.1 us; the launch traced here: 81.6 us
  starting transfers between devices  33.9 us (41%)
  Pallas kernels  31.2 us (38%)
  waiting for transfers between devices  12.9 us (16%)
  local copies, waits for them, and re-layouts  2.69 us (3%)
    pallas_call x3, Pallas kernels, call(): pl.pallas_call(kernel, in_specs=[IN_SMEM] * len(scalars) + [IN_VMEM] * le...  27.6 us
    all_to_all x1, starting transfers between devices, on_device(): pencil = lax.all_to_all(partial, ('slab', 'sub'), 0, 0, tiled=True)  14.4 us
    all_to_all x1, waiting for transfers between devices, on_device(): pencil = lax.all_to_all(partial, ('slab', 'sub'), 0, 0, tiled=True)  9.02 us
    all_to_all x1, starting transfers between devices, on_device(): arrived = lax.all_to_all(folded, 'slab', 0, 0, tiled=True)  7.9 us
    ppermute x1, starting transfers between devices, on_device(): above = lax.ppermute(charge_grid, 'slab', down)  5.14 us
    all_to_all x1, waiting for transfers between devices, on_device(): arrived = lax.all_to_all(folded, 'slab', 0, 0, tiled=True)  3.83 us
    pallas_call x1, Pallas kernels, on_device(): pl.pallas_call(restrict_kernel, grid_spec=pltpu.PrefetchScalarGridSpec(nu...  3.57 us
    ppermute x1, starting transfers between devices, on_device(): left = lax.ppermute(left, 'sub', up_sub)  3.3 us
  transfers between devices with their start and end apart: 6, of which 2 were waited for; matrix products, arithmetic and copies ran while one was open for 3% of the time, Pallas kernels for 14%

profile of v4, /device:TPU:1, one launch (start us, length us, event | category | flops | bytes accessed | tf_op | source)
XLA Modules:
  0.0 81.6 jit_solution(13072783180422454588)
XLA Ops:
  0.0 5.1 %collective-permute-start.1 = (f32[8,64,512]{2,1,0:T(8,128)}, f32[8,64,512]{2,1,0:T(8,128)S(1)}, u32[]{:S(2)}, u32[]{:S(2)}) collective-permute-start(f32[8,64,512]{2,1,0:T(8,128)} %charge_in.1), channel_id=1, source_target_pairs={{4,0},{8,4},{12,8},{16,12},{20,16},{24,20},{28,24},{32,28},{36,32}... | collective-permute-start | bytes 3145736 | tf_op jit(solution)/shard_map/ppermute | solution.py:460
  5.1 1.9 %collective-permute-start = (f32[8,64,512]{2,1,0:T(8,128)}, f32[8,64,512]{2,1,0:T(8,128)}, u32[]{:S(2)}, u32[]{:S(2)}) collective-permute-start(f32[8,64,512]{2,1,0:T(8,128)} %charge_in.1), channel_id=1, source_target_pairs={{0,4},{4,8},{8,12},{12,16},{16,20},{20,24},{24,28},{28,32},{32,36}... | collective-permute-start | bytes 3145736 | tf_op jit(solution)/shard_map/ppermute | solution.py:459
  7.1 0.7 pad_add_fusion.place
  7.8 3.6 %shard_map.136 = f32[512,128]{1,0:T(8,128)} custom-call(s32[4]{0:T(128)} %pad_add_fusion.place, f32[8,64,512]{2,1,0:T(8,128)} %charge_in.1, bf16[512,128]{1,0:T(8,128)(2,1)} %constant.39.clone.along_x, f32[12,512,128]{2,1,0:T(8,128)} %constant.40.clone.along_zy), custom_call_target="tpu_custom_call" | custom-call | flops 100000000 | bytes 1000000 | tf_op jit(solution)/shard_map/pallas_call | solution.py:461
  11.3 0.0 copy-start
  11.3 0.0 copy-start.1
  11.3 0.0 copy-start.2
  11.3 0.0 copy-start.3
  11.3 0.0 copy-start.4
  11.4 14.4 %all-to-all-start = ((f32[256,2,128]{2,1,0:T(2,128)}), f32[256,2,128]{2,1,0:T(2,128)S(1)}, u32[]{:S(2)}, u32[]{:S(2)}) async-start(f32[256,2,128]{2,1,0:T(2,128)} %bitcast.9), calls=%async_computation | async-start | bytes 524288 | tf_op jit(solution)/shard_map/all_to_all | solution.py:477
  25.7 1.0 %fusion.1 = (f32[8,4,512]{2,1,0:T(4,128)S(1)}, f32[8,4,512]{2,1,0:T(4,128)S(1)}) fusion(f32[8,64,512]{2,1,0:T(8,128)} %charge_in.1), kind=kLoop, calls=%fused_computation.4 | loop fusion | bytes 262144 | tf_op jit(solution)/shard_map/slice | solution.py:481
  26.7 0.0 collective-permute-done.1.z_high_in
  26.7 0.0 copy-start.5
  26.8 0.0 collective-permute-done.z_low_in
  26.8 1.0 %fusion = (f32[3,4,512]{2,1,0:T(4,128)S(1)}, f32[3,4,512]{2,1,0:T(4,128)S(1)}) fusion(f32[8,64,512]{2,1,0:T(8,128)} %collective-permute-done.z_low_in), kind=kLoop, calls=%fused_computation.3 | loop fusion | bytes 98304 | tf_op jit(solution)/shard_map/slice | solution.py:481
  27.8 3.3 %collective-permute-start.2 = (f32[15,4,512]{2,1,0:T(4,128)S(1)}, f32[15,4,512]{2,1,0:T(4,128)S(1)}, u32[]{:S(2)}, u32[]{:S(2)}) collective-permute-start(f32[15,4,512]{2,1,0:T(4,128)S(1)} %pad_maximum_fusion), channel_id=1, source_target_pairs={{0,1},{1,2},{2,3},{4,5},{5,6},{6,7},{8,9},{9,10},{10,11},{12,13},{... | collective-permute-start | bytes 368648 | tf_op jit(solution)/shard_map/ppermute | solution.py:482
  31.1 1.3 %collective-permute-start.3 = (f32[15,4,512]{2,1,0:T(4,128)S(1)}, f32[15,4,512]{2,1,0:T(4,128)S(1)}, u32[]{:S(2)}, u32[]{:S(2)}) collective-permute-start(f32[15,4,512]{2,1,0:T(4,128)S(1)} %pad_maximum_fusion.1), channel_id=1, source_target_pairs={{1,0},{2,1},{3,2},{5,4},{6,5},{7,6},{9,8},{10,9},{11,10},{13,12},{... | collective-permute-start | bytes 368648 | tf_op jit(solution)/shard_map/ppermute | solution.py:483
  32.4 9.0 %all-to-all-done = f32[256,2,128]{2,1,0:T(2,128)S(1)} async-done(((f32[256,2,128]{2,1,0:T(2,128)}), f32[256,2,128]{2,1,0:T(2,128)S(1)}, u32[]{:S(2)}, u32[]{:S(2)}) %all-to-all-start) | async-done | bytes 262176 | tf_op jit(solution)/shard_map/all_to_all | solution.py:477
  41.4 0.0 collective-permute-done.2.y_low_in
  41.4 0.0 copy-start.7
  41.4 0.0 collective-permute-done.3.y_high_in
  41.5 0.0 copy-start.8
  41.5 0.0 copy-done
  41.5 0.0 copy-done.1
  41.5 0.0 copy-done.2
  41.5 0.0 copy-done.3
  41.5 0.0 copy-done.4
  41.5 2.4 %shard_map.137 = f32[512,128]{1,0:T(8,128)} custom-call(s32[4]{0:T(128)S(1)} %copy-done.4, f32[512,128]{1,0:T(8,128)S(1)} %bitcast.8, bf16[4,128,384]{2,1,0:T(8,128)(2,1)S(1)} %copy-done.1, bf16[4,128,384]{2,1,0:T(8,128)(2,1)S(1)} %copy-done, bf16[320,384]{1,0:T(8,128)(2,1)S(1)} %copy-done.3, bf16[320,384]{1,0:T(8,128)(2,1)S(1)} %copy-done.2), custom_call_target="tpu_custom_call" | custom-call | flops 200000000 | bytes 2000000 | tf_op jit(solution)/shard_map/pallas_call | solution.py:437
  44.0 0.0 copy-done.5
  44.0 7.9 %all-to-all-start.1 = ((f32[64,8,128]{2,1,0:T(8,128)}), f32[64,8,128]{2,1,0:T(8,128)S(1)}, u32[]{:S(2)}, u32[]{:S(2)}) async-start(f32[64,8,128]{2,1,0:T(8,128)} %bitcast.6), calls=%async_computation.1 | async-start | bytes 524288 | tf_op jit(solution)/shard_map/all_to_all | solution.py:498
  51.9 0.0 copy-done.7
  51.9 0.0 copy-done.8
  51.9 8.1 %shard_map.138.near_in = f32[1152,640]{1,0:T(8,128)} custom-call(s32[4]{0:T(128)} %pad_add_fusion.place, f32[8,64,512]{2,1,0:T(8,128)} %charge_in.1, f32[8,64,512]{2,1,0:T(8,128)} %collective-permute-done.z_low_in, f32[8,64,512]{2,1,0:T(8,128)} %copy-done.5, f32[15,4,512]{2,1,0:T(4,128)} %copy-done.7, f32[15,4,512]{2,1,0:T(4,128)} %copy-done.8, ...), custom_call_target="tpu_custom_call" | custom-call | flops 2000000000 | bytes 16000000 | tf_op jit(solution)/shard_map/pallas_call | solution.py:437
  60.0 3.8 %all-to-all-done.1 = f32[64,8,128]{2,1,0:T(8,128)S(1)} async-done(((f32[64,8,128]{2,1,0:T(8,128)}), f32[64,8,128]{2,1,0:T(8,128)S(1)}, u32[]{:S(2)}, u32[]{:S(2)}) %all-to-all-start.1) | async-done | bytes 262176 | tf_op jit(solution)/shard_map/all_to_all | solution.py:498
  63.9 0.0 copy-start.6
  63.9 0.7 copy-done.6
  64.6 17.1 %shard_map.139 = f32[4,16384]{1,0:T(4,128)} custom-call(s32[4]{0:T(128)} %pad_add_fusion.place, s32[128]{0:T(128)} %cell.1, s32[128]{0:T(128)} %count.1, f32[512,128]{1,0:T(8,128)} %bitcast.10, f32[1152,640]{1,0:T(8,128)} %shard_map.138.near_in, bf16[1024,640]{1,0:T(8,128)(2,1)} %constant.46.clone.along_x_in, ...), custom_call_target="tpu_custom_call" | custom-call | flops 1000000000 | bytes 8000000 | tf_op jit(solution)/shard_map/pallas_call | solution.py:437
  (3 shorter events, 0.1 us)
Async XLA Ops:
  0.0 26.7 %collective-permute-start.1 = (f32[8,64,512]{2,1,0:T(8,128)}, f32[8,64,512]{2,1,0:T(8,128)S(1)}, u32[]{:S(2)}, u32[]{:S(2)}) collective-permute-start(f32[8,64,512]{2,1,0:T(8,128)} %charge_in.1), channel_id=1, source_target_pairs={{4,0},{8,4},{12,8},{16,12},{20,16},{24,20},{28,24},{32,28},{36,32}... | collective-permute-start | bytes 3145736 | tf_op jit(solution)/shard_map/ppermute | solution.py:460
  5.1 21.6 %collective-permute-start = (f32[8,64,512]{2,1,0:T(8,128)}, f32[8,64,512]{2,1,0:T(8,128)}, u32[]{:S(2)}, u32[]{:S(2)}) collective-permute-start(f32[8,64,512]{2,1,0:T(8,128)} %charge_in.1), channel_id=1, source_target_pairs={{0,4},{4,8},{8,12},{12,16},{16,20},{20,24},{24,28},{28,32},{32,36}... | collective-permute-start | bytes 3145736 | tf_op jit(solution)/shard_map/ppermute | solution.py:459
  11.3 30.1 %copy-start = (bf16[4,128,384]{2,1,0:T(8,128)(2,1)S(1)}, bf16[4,128,384]{2,1,0:T(8,128)(2,1)}, u32[]{:S(2)}) copy-start(bf16[4,128,384]{2,1,0:T(8,128)(2,1)} %constant.42.clone.y_low) | copy-start | bytes 1179652
  11.3 30.1 %copy-start.1 = (bf16[4,128,384]{2,1,0:T(8,128)(2,1)S(1)}, bf16[4,128,384]{2,1,0:T(8,128)(2,1)}, u32[]{:S(2)}) copy-start(bf16[4,128,384]{2,1,0:T(8,128)(2,1)} %constant.41.clone.y_high) | copy-start | bytes 1179652
  11.3 30.2 %copy-start.2 = (bf16[320,384]{1,0:T(8,128)(2,1)S(1)}, bf16[320,384]{1,0:T(8,128)(2,1)}, u32[]{:S(2)}) copy-start(bf16[320,384]{1,0:T(8,128)(2,1)} %constant.44.clone.z_low) | copy-start | bytes 737284
  11.3 30.2 %copy-start.3 = (bf16[320,384]{1,0:T(8,128)(2,1)S(1)}, bf16[320,384]{1,0:T(8,128)(2,1)}, u32[]{:S(2)}) copy-start(bf16[320,384]{1,0:T(8,128)(2,1)} %constant.43.clone.z_high) | copy-start | bytes 737284
  11.3 30.2 %copy-start.4 = (s32[4]{0:T(128)S(1)}, s32[4]{0:T(128)}, u32[]{:S(2)}) copy-start(s32[4]{0:T(128)} %pad_add_fusion.place) | copy-start | bytes 52
  11.4 30.1 %all-to-all-start = ((f32[256,2,128]{2,1,0:T(2,128)}), f32[256,2,128]{2,1,0:T(2,128)S(1)}, u32[]{:S(2)}, u32[]{:S(2)}) async-start(f32[256,2,128]{2,1,0:T(2,128)} %bitcast.9), calls=%async_computation | async-start | bytes 524288 | tf_op jit(solution)/shard_map/all_to_all | solution.py:477
  26.7 17.2 %copy-start.5 = (f32[8,64,512]{2,1,0:T(8,128)}, f32[8,64,512]{2,1,0:T(8,128)S(1)}, u32[]{:S(2)}) copy-start(f32[8,64,512]{2,1,0:T(8,128)S(1)} %collective-permute-done.1.z_high_in) | copy-start | bytes 3145732
  27.8 13.7 %collective-permute-start.2 = (f32[15,4,512]{2,1,0:T(4,128)S(1)}, f32[15,4,512]{2,1,0:T(4,128)S(1)}, u32[]{:S(2)}, u32[]{:S(2)}) collective-permute-start(f32[15,4,512]{2,1,0:T(4,128)S(1)} %pad_maximum_fusion), channel_id=1, source_target_pairs={{0,1},{1,2},{2,3},{4,5},{5,6},{6,7},{8,9},{9,10},{10,11},{12,13},{... | collective-permute-start | bytes 368648 | tf_op jit(solution)/shard_map/ppermute | solution.py:482
  31.1 10.3 %collective-permute-start.3 = (f32[15,4,512]{2,1,0:T(4,128)S(1)}, f32[15,4,512]{2,1,0:T(4,128)S(1)}, u32[]{:S(2)}, u32[]{:S(2)}) collective-permute-start(f32[15,4,512]{2,1,0:T(4,128)S(1)} %pad_maximum_fusion.1), channel_id=1, source_target_pairs={{1,0},{2,1},{3,2},{5,4},{6,5},{7,6},{9,8},{10,9},{11,10},{13,12},{... | collective-permute-start | bytes 368648 | tf_op jit(solution)/shard_map/ppermute | solution.py:483
  41.4 10.4 %copy-start.7 = (f32[15,4,512]{2,1,0:T(4,128)}, f32[15,4,512]{2,1,0:T(4,128)S(1)}, u32[]{:S(2)}) copy-start(f32[15,4,512]{2,1,0:T(4,128)S(1)} %collective-permute-done.2.y_low_in) | copy-start | bytes 368644
  41.5 10.4 %copy-start.8 = (f32[15,4,512]{2,1,0:T(4,128)}, f32[15,4,512]{2,1,0:T(4,128)S(1)}, u32[]{:S(2)}) copy-start(f32[15,4,512]{2,1,0:T(4,128)S(1)} %collective-permute-done.3.y_high_in) | copy-start | bytes 368644
  44.0 19.9 %all-to-all-start.1 = ((f32[64,8,128]{2,1,0:T(8,128)}), f32[64,8,128]{2,1,0:T(8,128)S(1)}, u32[]{:S(2)}, u32[]{:S(2)}) async-start(f32[64,8,128]{2,1,0:T(8,128)} %bitcast.6), calls=%async_computation.1 | async-start | bytes 524288 | tf_op jit(solution)/shard_map/all_to_all | solution.py:498
  63.9 0.7 copy-start.6

commit v5 on v4

--- a/solution.py
+++ b/solution.py
@@ -55,6 +55,29 @@
             if 0 <= row0 + r < matrix.shape[0] and 0 <= col0 + c < matrix.shape[1]:
                 out[r, c] = matrix[row0 + r, col0 + c]
     return out
+
+
+def far_nodes(n, first):
+    natural = np.zeros(13)
+    for outer in range(5):
+        for inner in range(5):
+            natural[2 * inner + outer] += TAPS[outer] * TAPS[inner]
+    true = restriction_twice(n).T
+    rows = np.zeros((8, n // 4))
+    high = first + 8 == n
+    for r in range(8):
+        if r < 4 or (r == 4 and not high):
+            cell = first // 4 + r - 1
+            if 0 <= cell < n // 4:
+                rows[r, cell] = 1.0
+            continue
+        at = first + (r + 2 if high else r - 6)
+        if 0 <= at < n:
+            rows[r] = true[at]
+        for cell in range(n // 4):
+            if abs(at - 4 * cell) <= 6:
+                rows[r, cell] -= natural[at - 4 * cell + 6]
+    return rows
 
 
 def halves(matrix):
@@ -96,7 +119,9 @@
 
     span_y = np.zeros((SUBS, 128, 3 * 128))
     span_z = np.zeros((TZ, SLABS, 3, 2, SLABS))
-    fine_x = np.zeros((SLABS, 8, FX))
+    far_x = np.zeros((SLABS, 8, NX))
+    spread = np.concatenate([far_nodes(NX, 8 * brick) for brick in range(NX // 8)])
+    order = np.arange(NX).reshape(4, 4, 4, 8).transpose(0, 2, 1, 3).reshape(NX)
     for s, span in enumerate(SPANS):
         gy, gz, gx = gauss(NY // 4, span), gauss(NZ // 4, span), gauss(NX // 4, span)
         for q in range(SUBS):
@@ -109,24 +134,26 @@
         for k in range(TZ):
             rows = wide[k : k + NZ // 4 : 2]
             span_z[k, :, s] = rows.reshape(SLABS, SLABS, 2).transpose(0, 2, 1)
-        px = rx.T @ gx
+        px = (spread @ gx)[order]
         for x in range(2):
-            fine_x[:, s * 2 + x, 1 : 1 + NX] = px[:, x::2].T
+            far_x[:, s * 2 + x] = px[:, x::2].T
     span_z = span_z.reshape(TZ * SLABS, 3 * 128)
-    fine_x = fine_x.reshape(SLABS * 8, FX)
-
-    prolong_y = np.zeros((SUBS, FY, FZ, 128))
+    far_x = far_x.reshape(SLABS * 8, NX)
+
+    far_y = np.zeros((SUBS, CY // 8, 8, 8, 128))
     for q in range(SUBS):
-        part = window(ry.T, CY * q - 1, CY + 3, 16 * q - 1, TY)
+        for brick in range(CY // 8):
+            nodes = far_nodes(NY, CY * q + 8 * brick)
+            part = window(nodes, 0, 8, 16 * q - 1, TY)
+            for zo in range(TZ):
+                far_y[q, brick, :, :, zo * TYS : zo * TYS + TY] = part[:, None, :]
+    far_y = far_y.reshape(SUBS, 512, 128).astype(ml_dtypes.bfloat16)
+    far_z = np.zeros((3, 8, 8, 128))
+    for kind, p in enumerate(SLAB_KINDS):
+        part = window(far_nodes(NZ, CZ * p), 0, 8, 2 * p - 1, TZ)
         for zo in range(TZ):
-            prolong_y[q, : CY + 3, :, zo * TYS : zo * TYS + TY] = part[:, None, :]
-    prolong_y = prolong_y.reshape(SUBS, FY * FZ, 128).astype(ml_dtypes.bfloat16)
-    prolong_z = np.zeros((3, 8, FZ, 128))
-    for kind, p in enumerate(SLAB_KINDS):
-        part = window(rz.T, CZ * p - 1, CZ + 3, 2 * p - 1, TZ)
-        for zo in range(TZ):
-            prolong_z[kind, :, : CZ + 3, zo * TYS : zo * TYS + TY] = part[None, :, zo, None]
-    prolong_z = prolong_z.reshape(3, 8 * FZ, 128).astype(ml_dtypes.bfloat16)
+            far_z[kind, :, :, zo * TYS : zo * TYS + TY] = part[None, :, zo, None]
+    far_z = far_z.reshape(3, 64, 128).astype(ml_dtypes.bfloat16)
     near_x = np.zeros((NX, FX))
     for node in range(NX):
         for offset in range(-2, 3):
@@ -138,9 +165,9 @@
         restrict_zy=restrict_zy,
         span_y=halves(span_y),
         span_z=halves(span_z),
-        fine_x=np.concatenate(halves(fine_x)),
-        prolong_y=prolong_y,
-        prolong_z=prolong_z,
+        far_x=np.concatenate(halves(far_x)),
+        far_y=far_y,
+        far_z=far_z,
     )
 
 
@@ -288,54 +315,10 @@
     return value, jnp.where(distance < 0.0, -slope, slope)
 
 
-def atoms_kernel(
-    place,
-    cell,
-    count,
-    arrived,
-    near_in,
-    along_x_in,
-    along_y_in,
-    along_z_in,
-    offset_in,
-    out,
-    near,
-    along_x,
-    along_y,
-    along_z,
-    offset,
-    table,
-    grid,
-    turned,
-    fields,
-    in_sems,
-    sems,
-):
-    copies = fetch(
-        (
-            along_x_in,
-            along_y_in.at[place[1]],
-            along_z_in.at[place[2]],
-            near_in,
-            offset_in,
-        ),
-        (along_x, along_y, along_z, near, offset),
-        in_sems,
-    )
-    top_high, top_low = split(arrived[...].T)
-    copies[0].wait()
-    top = dot3(top_high, top_low, along_x[0:512], along_x[512:1024])
-    high, low = split(top)
-    twice = jnp.concatenate([high, high], axis=0)
-    for copy in copies[1:]:
+def atoms_kernel(cell, count, near_in, offset_in, out, grid, offset, table, turned, fields, in_sems, sems):
+    copies = fetch((near_in, offset_in), (grid, offset), in_sems)
+    for copy in copies:
         copy.wait()
-    z_weight = jnp.concatenate([along_z[...].astype(F32)] * (ROWS // 128), axis=0)
-    for i in range(FY * FZ // ROWS):
-        at = pl.ds(ROWS * i, ROWS)
-        weight_high, weight_low = split(along_y[at, :].astype(F32) * z_weight)
-        both = jnp.concatenate([weight_high, weight_low], axis=1)
-        grid[at, :] = near[at, :] + (dot(both, twice) + dot(weight_high, low))
-
     lane = lax.broadcasted_iota(jnp.int32, (32, 128), 1)
 
     def build(i, carry):
@@ -424,6 +407,131 @@
         copy(i).wait()
 
 
+def far_kernel(
+    place,
+    cell,
+    count,
+    arrived,
+    along_x_in,
+    along_y_in,
+    along_z_in,
+    offset_in,
+    near_in,
+    out,
+    along_x,
+    along_y,
+    along_z,
+    offset,
+    fields,
+    table,
+    turned,
+    in_sems,
+    sems,
+):
+    copies = fetch(
+        (along_x_in, along_y_in.at[place[1]], along_z_in.at[place[2]], offset_in, near_in),
+        (along_x, along_y, along_z, offset, fields),
+        in_sems,
+    )
+    turned[...] = jnp.zeros(turned.shape, BF16)
+    lane = lax.broadcasted_iota(jnp.int32, (128, 128), 1) & 31
+    top_high, top_low = split(arrived[...].T)
+    for copy in copies:
+        copy.wait()
+    top = dot3(top_high, top_low, along_x[0:512], along_x[512:1024])
+    z_weight = jnp.concatenate([along_z[...].astype(F32)] * 8, axis=0)
+    weight_high, weight_low = split(along_y[...].astype(F32) * z_weight)
+    both = jnp.concatenate([weight_high, weight_low], axis=1)
+    for c in range(4):
+        source = top[:, 128 * c : 128 * c + 128]
+        wide = []
+        for m in range(4):
+            a, b, e = (
+                pltpu.roll(source, (128 + to - 8 * m) % 128, 1) if to != 8 * m else source
+                for to in (0, 8, 16)
+            )
+            wide.append(jnp.where(lane < 8, a, jnp.where(lane < 16, b, e)))
+        high, low = split(jnp.concatenate(wide, axis=1))
+        values = dot(both, jnp.concatenate([high, high], axis=0)) + dot(weight_high, low)
+        for m in range(4):
+            for r in range(0, 512, 128):
+                piece = values[r : r + 128, 128 * m : 128 * m + 128]
+                rounded = piece.astype(BF16).astype(F32)
+                keep_low = (lane >= 8) & (lane < 16)
+                table[4 * c + m, r : r + 128, :] = jnp.where(
+                    keep_low, piece - rounded, rounded
+                ).astype(BF16)
+
+    row = lax.broadcasted_iota(jnp.int32, (8, 128), 0)
+    row_value = row.astype(F32)
+    scales = [jnp.where(row < 5 - high, 0.25, 1.0) for high in range(2)]
+    starts = [
+        jnp.where(row < 5 - high, row_value - 1.0, row_value + (2.0 if high else -6.0))
+        for high in range(2)
+    ]
+    slot = lax.broadcasted_iota(jnp.int32, (1, 128), 1)
+    blank = jnp.zeros((8, 256), F32)
+
+    def weigh(position, high):
+        scale = jnp.where(high, scales[1], scales[0])
+        value, slope = spline_pair(position * scale - jnp.where(high, starts[1], starts[0]))
+        return value, slope * scale
+
+    def reduce(values):
+        return jnp.sum(values, axis=0, keepdims=True)
+
+    def block(b, k):
+        at = pl.ds(pl.multiple_of(SLOT * b, SLOT), SLOT)
+        t = cell[b]
+        brick_y = lax.shift_right_logical(t, 6) & 7
+        brick_x = t & 63
+        here = offset[:, at]
+        wz, sz = weigh(here[0:1], place[0] == SLABS - 1)
+        wy, sy = weigh(here[1:2], (place[1] == SUBS - 1) & (brick_y == CY // 8 - 1))
+        wx, sx = weigh(here[2:3], brick_x == NX // 8 - 1)
+        pair = jnp.concatenate([wx, sx], axis=1)
+        pair_high = pair.astype(BF16).astype(F32)
+        weights = jnp.concatenate([pair_high, pair_high, pair - pair_high, blank], axis=0)
+        turned[k, 128:160] = weights.astype(BF16)
+        first = pl.multiple_of(64 * brick_y, 64)
+        patch = table[lax.shift_right_logical(brick_x, 2), pl.ds(first, 64), :]
+        turn = pl.multiple_of(128 - 32 * (brick_x & 3), 32)
+        product = dot(patch, turned[k, pl.ds(turn, 128), :])
+        base = along = cross = None
+        for j in range(8):
+            v = product[8 * j : 8 * j + 8, :128]
+            d = product[8 * j : 8 * j + 8, 128:]
+            w, s = wy[j : j + 1], sy[j : j + 1]
+            base = v * w if base is None else base + v * w
+            along = v * s if along is None else along + v * s
+            cross = d * w if cross is None else cross + d * w
+        live = jnp.where(slot < count[b], 1.0, 0.0)
+        slope = live * (-1.0 / 72.0)
+        fields[:, at] = fields[:, at] + jnp.concatenate(
+            [
+                reduce(base * wz) * (live * (1.0 / 216.0)),
+                reduce(base * sz) * slope,
+                reduce(along * wz) * slope,
+                reduce(cross * wz) * slope,
+            ],
+            axis=0,
+        )
+
+    def copy(i):
+        at = pl.ds(pl.multiple_of(STEP * SLOT * i, STEP * SLOT), STEP * SLOT)
+        return pltpu.make_async_copy(fields.at[:, at], out.at[:, at], sems.at[i])
+
+    def step(i, carry):
+        for k in range(STEP):
+            block(STEP * i + k, k)
+        copy(i).start()
+        return carry
+
+    lax.fori_loop(0, BLOCKS // STEP, step, 0)
+    for i in range(BLOCKS // STEP):
+        copy(i).wait()
+
+
 def whole(shape):
     return pl.BlockSpec(shape, lambda i, *_: (0,) * len(shape))
 
@@ -481,22 +589,6 @@
     right = jnp.concatenate([plane[:, :4] for plane in planes], axis=0)
     left = lax.ppermute(left, "sub", up_sub)
     right = lax.ppermute(right, "sub", down_sub)
-    pencil, left, right = lax.optimization_barrier((pencil, left, right))
-
-    folded = call(
-        middle_kernel,
-        [place],
-        [pencil, *consts["span_y"], *consts["span_z"]],
-        [],
-        (512, 128),
-        IN_VMEM,
-        [],
-        12,
-        2 * 10**8,
-        2 * 10**6,
-    )
-    arrived = lax.all_to_all(folded, "slab", 0, 0, tiled=True)
-    left, right, _ = lax.optimization_barrier((left, right, folded))
     near = call(
         near_kernel,
         [place],
@@ -521,23 +613,57 @@
         2 * 10**9,
         16 * 10**6,
     )
-    return call(
+    pencil, near = lax.optimization_barrier((pencil, near))
+
+    folded = call(
+        middle_kernel,
+        [place],
+        [pencil, *consts["span_y"], *consts["span_z"]],
+        [],
+        (512, 128),
+        IN_VMEM,
+        [],
+        12,
+        2 * 10**8,
+        2 * 10**6,
+    )
+    arrived = lax.all_to_all(folded, "slab", 0, 0, tiled=True)
+    near, _ = lax.optimization_barrier((near, folded))
+    fields = call(
         atoms_kernel,
-        [place, block_cell, block_count],
-        [arrived],
-        [near, consts["fine_x"], consts["prolong_y"], consts["prolong_z"], atom_offset],
+        [block_cell, block_count],
+        [],
+        [near, atom_offset],
         (4, BLOCKS * SLOT),
         ANYWHERE,
         [
             pltpu.VMEM((FY * FZ, FX), F32),
-            pltpu.VMEM((1024, FX), BF16),
-            pltpu.VMEM((FY * FZ, 128), BF16),
-            pltpu.VMEM((128, 128), BF16),
             pltpu.VMEM((3, BLOCKS * SLOT), F32),
             pltpu.VMEM((TILES, FY * FZ, 128), BF16),
-            pltpu.VMEM((FY * FZ, FX), F32),
             pltpu.VMEM((STEP, 256, 256), BF16),
             pltpu.VMEM((4, BLOCKS * SLOT), F32),
+            pltpu.SemaphoreType.DMA((2,)),
+            pltpu.SemaphoreType.DMA((BLOCKS // STEP,)),
+        ],
+        60,
+        10**10,
+        8 * 10**6,
+    )
+    return call(
+        far_kernel,
+        [place, block_cell, block_count],
+        [arrived],
+        [consts["far_x"], consts["far_y"], consts["far_z"], atom_offset, fields],
+        (4, BLOCKS * SLOT),
+        ANYWHERE,
+        [
+            pltpu.VMEM((1024, NX), BF16),
+            pltpu.VMEM((512, 128), BF16),
+            pltpu.VMEM((64, 128), BF16),
+            pltpu.VMEM((3, BLOCKS * SLOT), F32),
+            pltpu.VMEM((4, BLOCKS * SLOT), F32),
+            pltpu.VMEM((TILES, 512, 128), BF16),
+            pltpu.VMEM((STEP, 256, 256), BF16),
             pltpu.SemaphoreType.DMA((5,)),
             pltpu.SemaphoreType.DMA((BLOCKS // STEP,)),
         ],

time: 82.1 us -> 86.1 us (1.049)
  Pallas kernels: 31.2 us -> 39.2 us
  waiting for transfers between devices: 12.9 us -> 5.95 us
  starting transfers between devices: 33.9 us -> 37.2 us
    all_to_all x1, waiting for transfers between devices: 9.02 us -> 0.01 us  [on_device(): pencil = lax.all_to_all(partial, ('slab', 'sub'), 0, 0, tiled=True)]
    pallas_call x3 -> x4, Pallas kernels: 27.6 us -> 35.6 us  [call(): pl.pallas_call(kernel, in_specs=[IN_SMEM] * len(scalars) + [IN_VMEM] * le...]
    all_to_all x1, waiting for transfers between devices: 3.83 us -> 0.01 us  [on_device(): arrived = lax.all_to_all(folded, 'slab', 0, 0, tiled=True)]
    ppermute x1, waiting for transfers between devices: 0.01 us -> 3.74 us  [on_device(): right = lax.ppermute(right, 'sub', down_sub)]
    all_to_all x1, starting transfers between devices: 7.9 us -> 11 us  [on_device(): arrived = lax.all_to_all(folded, 'slab', 0, 0, tiled=True)]
    ppermute x1, waiting for transfers between devices: 0.01 us -> 2.2 us  [on_device(): left = lax.ppermute(left, 'sub', up_sub)]
    slice x3, local copies, waits for them, and re-layouts: 1.96 us -> 1.02 us  [on_device(): right = jnp.concatenate([plane[:, :4] for plane in planes], axis=0)]
  transfers between devices with their start and end apart: 6 -> 6, of which waited for: 2 -> 2; matrix products, arithmetic and copies ran while one was open for 3% -> 2% of each run, Pallas kernels for 14% -> 31%
where the time goes in v5:
time: 86.1 us; the launch traced here: 85.7 us
  Pallas kernels  39.2 us (46%)
  starting transfers between devices  37.2 us (43%)
  waiting for transfers between devices  5.95 us (7%)
  local copies, waits for them, and re-layouts  2.45 us (3%)
    pallas_call x4, Pallas kernels, call(): pl.pallas_call(kernel, in_specs=[IN_SMEM] * len(scalars) + [IN_VMEM] * le...  35.6 us
    all_to_all x1, starting transfers between devices, on_device(): pencil = lax.all_to_all(partial, ('slab', 'sub'), 0, 0, tiled=True)  14.4 us
    all_to_all x1, starting transfers between devices, on_device(): arrived = lax.all_to_all(folded, 'slab', 0, 0, tiled=True)  11 us
    ppermute x1, starting transfers between devices, on_device(): above = lax.ppermute(charge_grid, 'slab', down)  5.14 us
    ppermute x1, waiting for transfers between devices, on_device(): right = lax.ppermute(right, 'sub', down_sub)  3.74 us
    pallas_call x1, Pallas kernels, on_device(): pl.pallas_call(restrict_kernel, grid_spec=pltpu.PrefetchScalarGridSpec(nu...  3.57 us
    ppermute x1, starting transfers between devices, on_device(): left = lax.ppermute(left, 'sub', up_sub)  3.3 us
    ppermute x1, waiting for transfers between devices, on_device(): left = lax.ppermute(left, 'sub', up_sub)  2.2 us
  transfers between devices with their start and end apart: 6, of which 2 were waited for; matrix products, arithmetic and copies ran while one was open for 2% of the time, Pallas kernels for 31%

profile of v5, /device:TPU:1, one launch (start us, length us, event | category | flops | bytes accessed | tf_op | source)
XLA Modules:
  0.0 85.7 jit_solution(5500871727663768022)
XLA Ops:
  0.0 5.1 %collective-permute-start.1 = (f32[8,64,512]{2,1,0:T(8,128)}, f32[8,64,512]{2,1,0:T(8,128)S(1)}, u32[]{:S(2)}, u32[]{:S(2)}) collective-permute-start(f32[8,64,512]{2,1,0:T(8,128)} %charge_in.1), channel_id=1, source_target_pairs={{4,0},{8,4},{12,8},{16,12},{20,16},{24,20},{28,24},{32,28},{36,32}... | collective-permute-start | bytes 3145736 | tf_op jit(solution)/shard_map/ppermute | solution.py:568
  5.1 1.9 %collective-permute-start = (f32[8,64,512]{2,1,0:T(8,128)}, f32[8,64,512]{2,1,0:T(8,128)S(1)}, u32[]{:S(2)}, u32[]{:S(2)}) collective-permute-start(f32[8,64,512]{2,1,0:T(8,128)} %charge_in.1), channel_id=1, source_target_pairs={{0,4},{4,8},{8,12},{12,16},{16,20},{20,24},{24,28},{28,32},{32,36}... | collective-permute-start | bytes 3145736 | tf_op jit(solution)/shard_map/ppermute | solution.py:567
  7.1 0.6 pad_add_fusion.place
  7.7 3.6 %shard_map.136 = f32[512,128]{1,0:T(8,128)} custom-call(s32[4]{0:T(128)} %pad_add_fusion.place, f32[8,64,512]{2,1,0:T(8,128)} %charge_in.1, bf16[512,128]{1,0:T(8,128)(2,1)} %constant.39.clone.along_x, f32[12,512,128]{2,1,0:T(8,128)} %constant.40.clone.along_zy), custom_call_target="tpu_custom_call" | custom-call | flops 100000000 | bytes 1000000 | tf_op jit(solution)/shard_map/pallas_call | solution.py:569
  11.2 14.4 %all-to-all-start = ((f32[256,2,128]{2,1,0:T(2,128)}), f32[256,2,128]{2,1,0:T(2,128)S(1)}, u32[]{:S(2)}, u32[]{:S(2)}) async-start(f32[256,2,128]{2,1,0:T(2,128)} %bitcast.9), calls=%async_computation | async-start | bytes 524288 | tf_op jit(solution)/shard_map/all_to_all | solution.py:585
  25.6 1.0 %fusion.1 = (f32[8,4,512]{2,1,0:T(4,128)S(1)}, f32[8,4,512]{2,1,0:T(4,128)S(1)}) fusion(f32[8,64,512]{2,1,0:T(8,128)} %charge_in.1), kind=kLoop, calls=%fused_computation.4 | loop fusion | bytes 262144 | tf_op jit(solution)/shard_map/slice | solution.py:589
  26.6 0.0 collective-permute-done.1.z_high_in
  26.6 0.0 copy-start.5
  26.7 0.0 collective-permute-done.z_low_in
  26.7 0.0 copy-start.6
  26.7 3.3 %collective-permute-start.2 = (f32[15,4,512]{2,1,0:T(4,128)S(1)}, f32[15,4,512]{2,1,0:T(4,128)S(1)}, u32[]{:S(2)}, u32[]{:S(2)}) collective-permute-start(f32[15,4,512]{2,1,0:T(4,128)S(1)} %pad_maximum_fusion), channel_id=1, source_target_pairs={{0,1},{1,2},{2,3},{4,5},{5,6},{6,7},{8,9},{9,10},{10,11},{12,13},{... | collective-permute-start | bytes 368648 | tf_op jit(solution)/shard_map/ppermute | solution.py:590
  30.0 0.0 copy-done.6
  30.1 0.0 copy-start
  30.1 0.0 copy-start.1
  30.1 0.0 copy-start.2
  30.1 0.0 copy-start.3
  30.1 0.0 copy-start.4
  30.2 1.4 %collective-permute-start.3 = (f32[15,4,512]{2,1,0:T(4,128)S(1)}, f32[15,4,512]{2,1,0:T(4,128)S(1)}, u32[]{:S(2)}, u32[]{:S(2)}) collective-permute-start(f32[15,4,512]{2,1,0:T(4,128)S(1)} %pad_maximum_fusion.1), channel_id=1, source_target_pairs={{1,0},{2,1},{3,2},{5,4},{6,5},{7,6},{9,8},{10,9},{11,10},{13,12},{... | collective-permute-start | bytes 368648 | tf_op jit(solution)/shard_map/ppermute | solution.py:591
  31.6 2.2 %collective-permute-done.2.y_low_in = f32[15,4,512]{2,1,0:T(4,128)S(1)} collective-permute-done((f32[15,4,512]{2,1,0:T(4,128)S(1)}, f32[15,4,512]{2,1,0:T(4,128)S(1)}, u32[]{:S(2)}, u32[]{:S(2)}) %collective-permute-start.2) | collective-permute-done | bytes 122912 | tf_op jit(solution)/shard_map/ppermute | solution.py:590
  33.8 0.0 copy-start.8
  33.8 3.7 %collective-permute-done.3.y_high_in = f32[15,4,512]{2,1,0:T(4,128)S(1)} collective-permute-done((f32[15,4,512]{2,1,0:T(4,128)S(1)}, f32[15,4,512]{2,1,0:T(4,128)S(1)}, u32[]{:S(2)}, u32[]{:S(2)}) %collective-permute-start.3) | collective-permute-done | bytes 122912 | tf_op jit(solution)/shard_map/ppermute | solution.py:591
  37.5 0.0 copy-done.5
  37.5 0.0 copy-done.8
  37.5 0.0 copy-start.9
  37.5 0.7 copy-done.9
  38.2 8.1 %shard_map.137.near_in = f32[1152,640]{1,0:T(8,128)} custom-call(s32[4]{0:T(128)} %pad_add_fusion.place, f32[8,64,512]{2,1,0:T(8,128)} %charge_in.1, f32[8,64,512]{2,1,0:T(8,128)} %copy-done.6, f32[8,64,512]{2,1,0:T(8,128)} %copy-done.5, f32[15,4,512]{2,1,0:T(4,128)} %copy-done.8, f32[15,4,512]{2,1,0:T(4,128)} %copy-done.9, ...), custom_call_target="tpu_custom_call" | custom-call | flops 2000000000 | bytes 16000000 | tf_op jit(solution)/shard_map/pallas_call | solution.py:545
  46.4 0.0 all-to-all-done
  46.4 0.0 copy-done
  46.4 0.0 copy-done.1
  46.4 0.0 copy-done.2
  46.4 0.0 copy-done.3
  46.4 0.0 copy-done.4
  46.4 2.4 %shard_map.138 = f32[512,128]{1,0:T(8,128)} custom-call(s32[4]{0:T(128)S(1)} %copy-done.4, f32[512,128]{1,0:T(8,128)S(1)} %bitcast.8, bf16[4,128,384]{2,1,0:T(8,128)(2,1)S(1)} %copy-done, bf16[4,128,384]{2,1,0:T(8,128)(2,1)S(1)} %copy-done.1, bf16[320,384]{1,0:T(8,128)(2,1)S(1)} %copy-done.2, bf16[320,384]{1,0:T(8,128)(2,1)S(1)} %copy-done.3), custom_call_target="tpu_custom_call" | custom-call | flops 200000000 | bytes 2000000 | tf_op jit(solution)/shard_map/pallas_call | solution.py:545
  48.9 11.0 %all-to-all-start.1 = ((f32[64,8,128]{2,1,0:T(8,128)}), f32[64,8,128]{2,1,0:T(8,128)S(1)}, u32[]{:S(2)}, u32[]{:S(2)}) async-start(f32[64,8,128]{2,1,0:T(8,128)} %bitcast.6), calls=%async_computation.1 | async-start | bytes 524288 | tf_op jit(solution)/shard_map/all_to_all | solution.py:630
  59.9 15.3 %shard_map.139.near_in = f32[4,16384]{1,0:T(4,128)} custom-call(s32[128]{0:T(128)} %cell.3, s32[128]{0:T(128)} %count.3, f32[1152,640]{1,0:T(8,128)} %shard_map.137.near_in, f32[3,16384]{1,0:T(4,128)} %offset_in.3), custom_call_target="tpu_custom_call" | custom-call | flops 10000000000 | bytes 8000000 | tf_op jit(solution)/shard_map/pallas_call | solution.py:545
  75.2 0.0 all-to-all-done.1
  75.2 0.0 copy-start.7
  75.2 0.7 copy-done.7
  75.9 9.8 %shard_map.140 = f32[4,16384]{1,0:T(4,128)} custom-call(s32[4]{0:T(128)} %pad_add_fusion.place, s32[128]{0:T(128)} %cell.3, s32[128]{0:T(128)} %count.3, f32[512,128]{1,0:T(8,128)} %bitcast.10, bf16[1024,512]{1,0:T(8,128)(2,1)} %constant.46.clone.along_x_in, bf16[4,512,128]{2,1,0:T(8,128)(2,1)} %constant.47.clone.along_y_in, ...), custom_call_target="tpu_custom_call" | custom-call | flops 1000000000 | bytes 8000000 | tf_op jit(solution)/shard_map/pallas_call | solution.py:545
  (4 shorter events, 0.1 us)
Async XLA Ops:
  0.0 26.6 %collective-permute-start.1 = (f32[8,64,512]{2,1,0:T(8,128)}, f32[8,64,512]{2,1,0:T(8,128)S(1)}, u32[]{:S(2)}, u32[]{:S(2)}) collective-permute-start(f32[8,64,512]{2,1,0:T(8,128)} %charge_in.1), channel_id=1, source_target_pairs={{4,0},{8,4},{12,8},{16,12},{20,16},{24,20},{28,24},{32,28},{36,32}... | collective-permute-start | bytes 3145736 | tf_op jit(solution)/shard_map/ppermute | solution.py:568
  5.1 21.5 %collective-permute-start = (f32[8,64,512]{2,1,0:T(8,128)}, f32[8,64,512]{2,1,0:T(8,128)S(1)}, u32[]{:S(2)}, u32[]{:S(2)}) collective-permute-start(f32[8,64,512]{2,1,0:T(8,128)} %charge_in.1), channel_id=1, source_target_pairs={{0,4},{4,8},{8,12},{12,16},{16,20},{20,24},{24,28},{28,32},{32,36}... | collective-permute-start | bytes 3145736 | tf_op jit(solution)/shard_map/ppermute | solution.py:567
  11.2 35.1 %all-to-all-start = ((f32[256,2,128]{2,1,0:T(2,128)}), f32[256,2,128]{2,1,0:T(2,128)S(1)}, u32[]{:S(2)}, u32[]{:S(2)}) async-start(f32[256,2,128]{2,1,0:T(2,128)} %bitcast.9), calls=%async_computation | async-start | bytes 524288 | tf_op jit(solution)/shard_map/all_to_all | solution.py:585
  26.6 10.9 %copy-start.5 = (f32[8,64,512]{2,1,0:T(8,128)}, f32[8,64,512]{2,1,0:T(8,128)S(1)}, u32[]{:S(2)}) copy-start(f32[8,64,512]{2,1,0:T(8,128)S(1)} %collective-permute-done.1.z_high_in) | copy-start | bytes 3145732
  26.7 3.4 %copy-start.6 = (f32[8,64,512]{2,1,0:T(8,128)}, f32[8,64,512]{2,1,0:T(8,128)S(1)}, u32[]{:S(2)}) copy-start(f32[8,64,512]{2,1,0:T(8,128)S(1)} %collective-permute-done.z_low_in) | copy-start | bytes 3145732
  26.7 7.0 %collective-permute-start.2 = (f32[15,4,512]{2,1,0:T(4,128)S(1)}, f32[15,4,512]{2,1,0:T(4,128)S(1)}, u32[]{:S(2)}, u32[]{:S(2)}) collective-permute-start(f32[15,4,512]{2,1,0:T(4,128)S(1)} %pad_maximum_fusion), channel_id=1, source_target_pairs={{0,1},{1,2},{2,3},{4,5},{5,6},{6,7},{8,9},{9,10},{10,11},{12,13},{... | collective-permute-start | bytes 368648 | tf_op jit(solution)/shard_map/ppermute | solution.py:590
  30.1 16.3 %copy-start = (bf16[4,128,384]{2,1,0:T(8,128)(2,1)S(1)}, bf16[4,128,384]{2,1,0:T(8,128)(2,1)}, u32[]{:S(2)}) copy-start(bf16[4,128,384]{2,1,0:T(8,128)(2,1)} %constant.42.clone.y_high) | copy-start | bytes 1179652
  30.1 16.3 %copy-start.1 = (bf16[4,128,384]{2,1,0:T(8,128)(2,1)S(1)}, bf16[4,128,384]{2,1,0:T(8,128)(2,1)}, u32[]{:S(2)}) copy-start(bf16[4,128,384]{2,1,0:T(8,128)(2,1)} %constant.43.clone.y_low) | copy-start | bytes 1179652
  30.1 16.3 %copy-start.2 = (bf16[320,384]{1,0:T(8,128)(2,1)S(1)}, bf16[320,384]{1,0:T(8,128)(2,1)}, u32[]{:S(2)}) copy-start(bf16[320,384]{1,0:T(8,128)(2,1)} %constant.44.clone.z_high) | copy-start | bytes 737284
  30.1 16.3 %copy-start.3 = (bf16[320,384]{1,0:T(8,128)(2,1)S(1)}, bf16[320,384]{1,0:T(8,128)(2,1)}, u32[]{:S(2)}) copy-start(bf16[320,384]{1,0:T(8,128)(2,1)} %constant.45.clone.z_low) | copy-start | bytes 737284
  30.1 16.3 %copy-start.4 = (s32[4]{0:T(128)S(1)}, s32[4]{0:T(128)}, u32[]{:S(2)}) copy-start(s32[4]{0:T(128)} %pad_add_fusion.place) | copy-start | bytes 52
  30.2 7.4 %collective-permute-start.3 = (f32[15,4,512]{2,1,0:T(4,128)S(1)}, f32[15,4,512]{2,1,0:T(4,128)S(1)}, u32[]{:S(2)}, u32[]{:S(2)}) collective-permute-start(f32[15,4,512]{2,1,0:T(4,128)S(1)} %pad_maximum_fusion.1), channel_id=1, source_target_pairs={{1,0},{2,1},{3,2},{5,4},{6,5},{7,6},{9,8},{10,9},{11,10},{13,12},{... | collective-permute-start | bytes 368648 | tf_op jit(solution)/shard_map/ppermute | solution.py:591
  33.8 3.7 %copy-start.8 = (f32[15,4,512]{2,1,0:T(4,128)}, f32[15,4,512]{2,1,0:T(4,128)S(1)}, u32[]{:S(2)}) copy-start(f32[15,4,512]{2,1,0:T(4,128)S(1)} %collective-permute-done.2.y_low_in) | copy-start | bytes 368644
  37.5 0.7 copy-start.9
  48.9 26.3 %all-to-all-start.1 = ((f32[64,8,128]{2,1,0:T(8,128)}), f32[64,8,128]{2,1,0:T(8,128)S(1)}, u32[]{:S(2)}, u32[]{:S(2)}) async-start(f32[64,8,128]{2,1,0:T(8,128)} %bitcast.6), calls=%async_computation.1 | async-start | bytes 524288 | tf_op jit(solution)/shard_map/all_to_all | solution.py:630
  75.2 0.7 copy-start.7

commit v6 on v4

--- a/solution.py
+++ b/solution.py
@@ -26,6 +26,7 @@
 TILES = 16
 ROWS = 384
 STEP = 8
+PIECES = 8
 
 F32, BF16 = jnp.float32, jnp.bfloat16
 
@@ -223,7 +224,7 @@
     out_sems,
 ):
     copies = fetch(
-        (charge_in, z_low_in.at[pl.ds(CZ - 3, 3)], z_high_in.at[pl.ds(0, 4)], y_low_in, y_high_in, along_x_in),
+        (charge_in, z_low_in, z_high_in, y_low_in, y_high_in, along_x_in),
         (charge, z_low, z_high, y_low, y_high, along_x),
         sems,
     )
@@ -311,15 +312,12 @@
     in_sems,
     sems,
 ):
+    chunks = [pl.ds(ROWS * i, ROWS) for i in range(FY * FZ // ROWS)]
     copies = fetch(
-        (
-            along_x_in,
-            along_y_in.at[place[1]],
-            along_z_in.at[place[2]],
-            near_in,
-            offset_in,
-        ),
-        (along_x, along_y, along_z, near, offset),
+        [along_x_in, along_y_in.at[place[1]], along_z_in.at[place[2]]]
+        + [near_in.at[at] for at in chunks]
+        + [offset_in],
+        [along_x, along_y, along_z] + [near.at[at] for at in chunks] + [offset],
         in_sems,
     )
     top_high, top_low = split(arrived[...].T)
@@ -327,19 +325,12 @@
     top = dot3(top_high, top_low, along_x[0:512], along_x[512:1024])
     high, low = split(top)
     twice = jnp.concatenate([high, high], axis=0)
-    for copy in copies[1:]:
-        copy.wait()
+    copies[1].wait()
+    copies[2].wait()
     z_weight = jnp.concatenate([along_z[...].astype(F32)] * (ROWS // 128), axis=0)
-    for i in range(FY * FZ // ROWS):
-        at = pl.ds(ROWS * i, ROWS)
-        weight_high, weight_low = split(along_y[at, :].astype(F32) * z_weight)
-        both = jnp.concatenate([weight_high, weight_low], axis=1)
-        grid[at, :] = near[at, :] + (dot(both, twice) + dot(weight_high, low))
-
-    lane = lax.broadcasted_iota(jnp.int32, (32, 128), 1)
-
-    def build(i, carry):
-        at = pl.ds(pl.multiple_of(32 * i, 32), 32)
+    lane = lax.broadcasted_iota(jnp.int32, (16, 128), 1)
+
+    def pieces(at):
         values = grid[at, :]
         fine_high = values.astype(BF16).astype(F32)
         fine_low = values - fine_high
@@ -356,9 +347,21 @@
                 place_in = (lane + (128 - 32 * j)) & 127
                 row = jnp.where(place_in < TILE, one, jnp.where(place_in < 2 * TILE, two, three))
                 table[4 * c + j, at, :] = row.astype(BF16)
+
+    def build(i, carry):
+        for k in range(PIECES):
+            pieces(pl.ds(pl.multiple_of(16 * (PIECES * i + k), 16), 16))
         return carry
 
-    lax.fori_loop(0, (CY + 3) * FZ // 32 + 1, build, 0)
+    for i, at in enumerate(chunks):
+        weight_high, weight_low = split(along_y[at, :].astype(F32) * z_weight)
+        both = jnp.concatenate([weight_high, weight_low], axis=1)
+        far = dot(both, twice) + dot(weight_high, low)
+        copies[3 + i].wait()
+        grid[at, :] = near[at, :] + far
+        per = ROWS // (16 * PIECES)
+        lax.fori_loop(per * i, per * (i + 1), build, 0)
+    copies[-1].wait()
 
     row16 = lax.broadcasted_iota(jnp.int32, (16, 128), 0).astype(F32) - 1.0
     row40 = lax.broadcasted_iota(jnp.int32, (TILE, 128), 0).astype(F32) - 1.0
@@ -381,10 +384,10 @@
         first = pl.multiple_of(128 * brick_y, 128)
         patch = table[tile, pl.ds(first, 11 * FZ), :]
         weights = weights.astype(BF16)
-        turned[k, 0:128] = weights
-        turned[k, 128:256] = weights
-        turn = pl.multiple_of(128 - 32 * (tile & 3), 32)
-        product = dot(patch, turned[k, pl.ds(turn, 128), :])
+        for i in range(4):
+            turn = pl.multiple_of(32 * ((tile + i) & 3), 32)
+            turned[k, pl.ds(turn, 32), :] = weights[32 * i : 32 * i + 32]
+        product = dot(patch, turned[k])
         base = along = cross = None
         for j in range(11):
             v = product[FZ * j : FZ * (j + 1), :128]
@@ -451,13 +454,13 @@
     kind = jnp.where(p == 0, 0, jnp.where(p == SLABS - 1, 2, 1))
     place = jnp.stack([p, q, kind, kind * SUBS + q]).astype(jnp.int32)
 
-    up = [(i, i + 1) for i in range(SLABS - 1)]
-    down = [(b, a) for a, b in up]
     up_sub = [(i, i + 1) for i in range(SUBS - 1)]
     down_sub = [(b, a) for a, b in up_sub]
 
-    below = lax.ppermute(charge_grid, "slab", up)
-    above = lax.ppermute(charge_grid, "slab", down)
+    inner = [(i, i ^ 1) for i in range(SLABS)]
+    outer = [(i, i + 1 if i % 2 else i - 1) for i in range(1, SLABS - 1)]
+    twin = lax.ppermute(charge_grid, "slab", inner)
+    other = lax.ppermute(charge_grid, "slab", outer)
     partial = pl.pallas_call(
         restrict_kernel,
         grid_spec=pltpu.PrefetchScalarGridSpec(
@@ -476,7 +479,10 @@
     )(place, charge_grid, consts["restrict_x"], consts["restrict_zy"])
     pencil = lax.all_to_all(partial, ("slab", "sub"), 0, 0, tiled=True)
 
-    planes = (below[CZ - 3 :], charge_grid, above[:4])
+    odd = p % 2 == 1
+    below = jnp.where(odd, twin[CZ - 3 :], other[CZ - 3 :])
+    above = jnp.where(odd, other[:4], twin[:4])
+    planes = (below, charge_grid, above)
     left = jnp.concatenate([plane[:, CY - 4 :] for plane in planes], axis=0)
     right = jnp.concatenate([plane[:, :4] for plane in planes], axis=0)
     left = lax.ppermute(left, "sub", up_sub)
@@ -536,9 +542,9 @@
             pltpu.VMEM((3, BLOCKS * SLOT), F32),
             pltpu.VMEM((TILES, FY * FZ, 128), BF16),
             pltpu.VMEM((FY * FZ, FX), F32),
-            pltpu.VMEM((STEP, 256, 256), BF16),
+            pltpu.VMEM((STEP, 128, 256), BF16),
             pltpu.VMEM((4, BLOCKS * SLOT), F32),
-            pltpu.SemaphoreType.DMA((5,)),
+            pltpu.SemaphoreType.DMA((4 + FY * FZ // ROWS,)),
             pltpu.SemaphoreType.DMA((BLOCKS // STEP,)),
         ],
         60,

time: 82.1 us -> 78.9 us (0.961)
  Pallas kernels: 31.2 us -> 29.2 us
  waiting for transfers between devices: 12.9 us -> 11.4 us
  other arithmetic: 0.73 us -> 2.04 us
  starting transfers between devices: 33.9 us -> 32.8 us
    ppermute x2, starting transfers between devices: 7.06 us -> 5.02 us  [the longest x1 4.93 us: on_device(): other = lax.ppermute(charge_grid, 'slab', outer)]
    pallas_call x3, Pallas kernels: 27.6 us -> 25.6 us  [call(): pl.pallas_call(kernel, in_specs=[IN_SMEM] * len(scalars) + [IN_VMEM] * le...]
    all_to_all x1, starting transfers between devices: 7.9 us -> 9.42 us  [on_device(): arrived = lax.all_to_all(folded, 'slab', 0, 0, tiled=True)]
    all_to_all x1, waiting for transfers between devices: 9.02 us -> 7.51 us  [on_device(): pencil = lax.all_to_all(partial, ('slab', 'sub'), 0, 0, tiled=True)]
    select_n x0 -> x2, other arithmetic: none -> 1.36 us  [the longest x1 1.28 us: on_device(): below = jnp.where(odd, twin[CZ - 3:], other[CZ - 3:])]
    unnamed x18 -> x22, local copies, waits for them, and re-layouts: 0.73 us -> 1.73 us
    slice x3, local copies, waits for them, and re-layouts: 1.96 us -> 1.02 us  [on_device(): right = jnp.concatenate([plane[:, :4] for plane in planes], axis=0)]
  transfers between devices with their start and end apart: 6 -> 6, of which waited for: 2 -> 2; matrix products, arithmetic and copies ran while one was open for 3% -> 4% of each run, Pallas kernels for 14% -> 15%
where the time goes in v6:
time: 78.9 us; the launch traced here: 78.6 us
  starting transfers between devices  32.8 us (42%)
  Pallas kernels  29.2 us (37%)
  waiting for transfers between devices  11.4 us (14%)
  local copies, waits for them, and re-layouts  2.75 us (3%)
  other arithmetic  2.04 us (3%)
    pallas_call x3, Pallas kernels, call(): pl.pallas_call(kernel, in_specs=[IN_SMEM] * len(scalars) + [IN_VMEM] * le...  25.6 us
    all_to_all x1, starting transfers between devices, on_device(): pencil = lax.all_to_all(partial, ('slab', 'sub'), 0, 0, tiled=True)  13.7 us
    all_to_all x1, starting transfers between devices, on_device(): arrived = lax.all_to_all(folded, 'slab', 0, 0, tiled=True)  9.42 us
    all_to_all x1, waiting for transfers between devices, on_device(): pencil = lax.all_to_all(partial, ('slab', 'sub'), 0, 0, tiled=True)  7.51 us
    ppermute x1, starting transfers between devices, on_device(): other = lax.ppermute(charge_grid, 'slab', outer)  4.93 us
    all_to_all x1, waiting for transfers between devices, on_device(): arrived = lax.all_to_all(folded, 'slab', 0, 0, tiled=True)  3.84 us
    pallas_call x1, Pallas kernels, on_device(): pl.pallas_call(restrict_kernel, grid_spec=pltpu.PrefetchScalarGridSpec(nu...  3.57 us
    ppermute x1, starting transfers between devices, on_device(): left = lax.ppermute(left, 'sub', up_sub)  3.3 us
  transfers between devices with their start and end apart: 6, of which 2 were waited for; matrix products, arithmetic and copies ran while one was open for 4% of the time, Pallas kernels for 15%

profile of v6, /device:TPU:1, one launch (start us, length us, event | category | flops | bytes accessed | tf_op | source)
XLA Modules:
  0.0 78.6 jit_solution(1999708603807485505)
XLA Ops:
  0.0 4.9 %collective-permute-start.1 = (f32[8,64,512]{2,1,0:T(8,128)}, f32[8,64,512]{2,1,0:T(8,128)S(1)}, u32[]{:S(2)}, u32[]{:S(2)}) collective-permute-start(f32[8,64,512]{2,1,0:T(8,128)} %charge_in.1), channel_id=1, source_target_pairs={{4,8},{8,4},{12,16},{16,12},{20,24},{24,20},{28,32},{32,28},{36,40... | collective-permute-start | bytes 3145736 | tf_op jit(solution)/shard_map/ppermute | solution.py:463
  4.9 0.1 collective-permute-start
  5.1 0.6 pad_add_fusion.place
  5.7 3.6 %shard_map.136 = f32[512,128]{1,0:T(8,128)} custom-call(s32[4]{0:T(128)} %pad_add_fusion.place, f32[8,64,512]{2,1,0:T(8,128)} %charge_in.1, bf16[512,128]{1,0:T(8,128)(2,1)} %constant.48.clone.along_x, f32[12,512,128]{2,1,0:T(8,128)} %constant.49.clone.along_zy), custom_call_target="tpu_custom_call" | custom-call | flops 100000000 | bytes 1000000 | tf_op jit(solution)/shard_map/pallas_call | solution.py:464
  9.2 13.7 %all-to-all-start = ((f32[256,2,128]{2,1,0:T(2,128)}), f32[256,2,128]{2,1,0:T(2,128)S(1)}, u32[]{:S(2)}, u32[]{:S(2)}) async-start(f32[256,2,128]{2,1,0:T(2,128)} %bitcast.9), calls=%async_computation | async-start | bytes 524288 | tf_op jit(solution)/shard_map/all_to_all | solution.py:480
  23.0 1.0 %fusion = (f32[8,4,512]{2,1,0:T(4,128)S(1)}, f32[8,4,512]{2,1,0:T(4,128)S(1)}) fusion(f32[8,64,512]{2,1,0:T(8,128)} %charge_in.1), kind=kLoop, calls=%fused_computation.5 | loop fusion | bytes 262144 | tf_op jit(solution)/shard_map/slice | solution.py:487
  24.0 0.0 collective-permute-done.1
  24.0 0.0 collective-permute-done
  24.0 0.0 copy-start.6
  24.0 1.0 %copy-done.6 = f32[8,64,512]{2,1,0:T(8,128)} copy-done((f32[8,64,512]{2,1,0:T(8,128)}, f32[8,64,512]{2,1,0:T(8,128)S(1)}, u32[]{:S(2)}) %copy-start.6) | copy-done | bytes 1048600
  25.0 0.1 slice_select_fusion.z_high_in
  25.1 0.0 copy-start.7
  25.1 0.0 copy-start
  25.1 0.0 copy-start.1
  25.1 0.0 copy-start.2
  25.1 0.0 copy-start.3
  25.1 0.0 copy-start.4
  25.2 1.3 %slice_select_fusion.1.z_low_in = f32[3,64,512]{2,1,0:T(8,128)S(1)} fusion(f32[8,64,512]{2,1,0:T(8,128)S(1)} %collective-permute-done.1, f32[8,64,512]{2,1,0:T(8,128)} %copy-done.6, pred[]{:T(512)S(6)} %eq.13), kind=kLoop, calls=%fused_computation.1 | loop fusion | flops 98304 | bytes 1179649 | tf_op jit(solution)/shard_map/jit(_where)/select_n | solution.py:483
  26.5 0.0 copy-start.8
  26.5 3.3 %collective-permute-start.2 = (f32[15,4,512]{2,1,0:T(4,128)S(1)}, f32[15,4,512]{2,1,0:T(4,128)S(1)}, u32[]{:S(2)}, u32[]{:S(2)}) collective-permute-start(f32[15,4,512]{2,1,0:T(4,128)S(1)} %pad_maximum_fusion), channel_id=1, source_target_pairs={{0,1},{1,2},{2,3},{4,5},{5,6},{6,7},{8,9},{9,10},{10,11},{12,13},{... | collective-permute-start | bytes 368648 | tf_op jit(solution)/shard_map/ppermute | solution.py:488
  29.9 1.3 %collective-permute-start.3 = (f32[15,4,512]{2,1,0:T(4,128)S(1)}, f32[15,4,512]{2,1,0:T(4,128)S(1)}, u32[]{:S(2)}, u32[]{:S(2)}) collective-permute-start(f32[15,4,512]{2,1,0:T(4,128)S(1)} %pad_maximum_fusion.1), channel_id=1, source_target_pairs={{1,0},{2,1},{3,2},{5,4},{6,5},{7,6},{9,8},{10,9},{11,10},{13,12},{... | collective-permute-start | bytes 368648 | tf_op jit(solution)/shard_map/ppermute | solution.py:489
  31.2 7.5 %all-to-all-done = f32[256,2,128]{2,1,0:T(2,128)S(1)} async-done(((f32[256,2,128]{2,1,0:T(2,128)}), f32[256,2,128]{2,1,0:T(2,128)S(1)}, u32[]{:S(2)}, u32[]{:S(2)}) %all-to-all-start) | async-done | bytes 262176 | tf_op jit(solution)/shard_map/all_to_all | solution.py:480
  38.7 0.0 collective-permute-done.2.y_low_in
  38.7 0.0 copy-start.9
  38.7 0.0 collective-permute-done.3.y_high_in
  38.7 0.0 copy-start.10
  38.7 0.0 copy-done
  38.7 0.0 copy-done.1
  38.7 0.0 copy-done.2
  38.7 0.0 copy-done.3
  38.8 0.0 copy-done.4
  38.8 2.4 %shard_map.137 = f32[512,128]{1,0:T(8,128)} custom-call(s32[4]{0:T(128)S(1)} %copy-done.4, f32[512,128]{1,0:T(8,128)S(1)} %bitcast.8, bf16[4,128,384]{2,1,0:T(8,128)(2,1)S(1)} %copy-done.1, bf16[4,128,384]{2,1,0:T(8,128)(2,1)S(1)} %copy-done, bf16[320,384]{1,0:T(8,128)(2,1)S(1)} %copy-done.3, bf16[320,384]{1,0:T(8,128)(2,1)S(1)} %copy-done.2), custom_call_target="tpu_custom_call" | custom-call | flops 200000000 | bytes 2000000 | tf_op jit(solution)/shard_map/pallas_call | solution.py:440
  41.2 0.0 copy-done.7
  41.2 0.0 copy-done.8
  41.2 9.4 %all-to-all-start.1 = ((f32[64,8,128]{2,1,0:T(8,128)}), f32[64,8,128]{2,1,0:T(8,128)S(1)}, u32[]{:S(2)}, u32[]{:S(2)}) async-start(f32[64,8,128]{2,1,0:T(8,128)} %bitcast.6), calls=%async_computation.1 | async-start | bytes 524288 | tf_op jit(solution)/shard_map/all_to_all | solution.py:504
  50.6 0.0 copy-done.9
  50.7 0.0 copy-done.10
  50.7 8.1 %shard_map.138.near_in = f32[1152,640]{1,0:T(8,128)} custom-call(s32[4]{0:T(128)} %pad_add_fusion.place, f32[8,64,512]{2,1,0:T(8,128)} %charge_in.1, f32[3,64,512]{2,1,0:T(8,128)} %copy-done.8, f32[4,64,512]{2,1,0:T(8,128)} %copy-done.7, f32[15,4,512]{2,1,0:T(4,128)} %copy-done.9, f32[15,4,512]{2,1,0:T(4,128)} %copy-done.10, ...), custom_call_target="tpu_custom_call" | custom-call | flops 2000000000 | bytes 16000000 | tf_op jit(solution)/shard_map/pallas_call | solution.py:440
  58.8 3.8 %all-to-all-done.1 = f32[64,8,128]{2,1,0:T(8,128)S(1)} async-done(((f32[64,8,128]{2,1,0:T(8,128)}), f32[64,8,128]{2,1,0:T(8,128)S(1)}, u32[]{:S(2)}, u32[]{:S(2)}) %all-to-all-start.1) | async-done | bytes 262176 | tf_op jit(solution)/shard_map/all_to_all | solution.py:504
  62.6 0.0 copy-start.5
  62.6 0.7 copy-done.5
  63.3 15.1 %shard_map.139 = f32[4,16384]{1,0:T(4,128)} custom-call(s32[4]{0:T(128)} %pad_add_fusion.place, s32[128]{0:T(128)} %cell.1, s32[128]{0:T(128)} %count.1, f32[512,128]{1,0:T(8,128)} %bitcast.10, f32[1152,640]{1,0:T(8,128)} %shard_map.138.near_in, bf16[1024,640]{1,0:T(8,128)(2,1)} %constant.55.clone.along_x_in, ...), custom_call_target="tpu_custom_call" | custom-call | flops 1000000000 | bytes 8000000 | tf_op jit(solution)/shard_map/pallas_call | solution.py:440
  (4 shorter events, 0.1 us)
Async XLA Ops:
  0.0 24.0 %collective-permute-start.1 = (f32[8,64,512]{2,1,0:T(8,128)}, f32[8,64,512]{2,1,0:T(8,128)S(1)}, u32[]{:S(2)}, u32[]{:S(2)}) collective-permute-start(f32[8,64,512]{2,1,0:T(8,128)} %charge_in.1), channel_id=1, source_target_pairs={{4,8},{8,4},{12,16},{16,12},{20,24},{24,20},{28,32},{32,28},{36,40... | collective-permute-start | bytes 3145736 | tf_op jit(solution)/shard_map/ppermute | solution.py:463
  4.9 19.1 %collective-permute-start = (f32[8,64,512]{2,1,0:T(8,128)}, f32[8,64,512]{2,1,0:T(8,128)S(1)}, u32[]{:S(2)}, u32[]{:S(2)}) collective-permute-start(f32[8,64,512]{2,1,0:T(8,128)} %charge_in.1), channel_id=1, source_target_pairs={{0,4},{4,0},{8,12},{12,8},{16,20},{20,16},{24,28},{28,24},{32,36},... | collective-permute-start | bytes 3145736 | tf_op jit(solution)/shard_map/ppermute | solution.py:462
  9.2 29.5 %all-to-all-start = ((f32[256,2,128]{2,1,0:T(2,128)}), f32[256,2,128]{2,1,0:T(2,128)S(1)}, u32[]{:S(2)}, u32[]{:S(2)}) async-start(f32[256,2,128]{2,1,0:T(2,128)} %bitcast.9), calls=%async_computation | async-start | bytes 524288 | tf_op jit(solution)/shard_map/all_to_all | solution.py:480
  24.0 1.0 %copy-start.6 = (f32[8,64,512]{2,1,0:T(8,128)}, f32[8,64,512]{2,1,0:T(8,128)S(1)}, u32[]{:S(2)}) copy-start(f32[8,64,512]{2,1,0:T(8,128)S(1)} %collective-permute-done) | copy-start | bytes 3145732
  25.1 16.1 %copy-start.7 = (f32[4,64,512]{2,1,0:T(8,128)}, f32[4,64,512]{2,1,0:T(8,128)S(1)}, u32[]{:S(2)}) copy-start(f32[4,64,512]{2,1,0:T(8,128)S(1)} %slice_select_fusion.z_high_in) | copy-start | bytes 1572868
  25.1 13.6 %copy-start = (bf16[4,128,384]{2,1,0:T(8,128)(2,1)S(1)}, bf16[4,128,384]{2,1,0:T(8,128)(2,1)}, u32[]{:S(2)}) copy-start(bf16[4,128,384]{2,1,0:T(8,128)(2,1)} %constant.51.clone.y_low) | copy-start | bytes 1179652
  25.1 13.6 %copy-start.1 = (bf16[4,128,384]{2,1,0:T(8,128)(2,1)S(1)}, bf16[4,128,384]{2,1,0:T(8,128)(2,1)}, u32[]{:S(2)}) copy-start(bf16[4,128,384]{2,1,0:T(8,128)(2,1)} %constant.50.clone.y_high) | copy-start | bytes 1179652
  25.1 13.6 %copy-start.2 = (bf16[320,384]{1,0:T(8,128)(2,1)S(1)}, bf16[320,384]{1,0:T(8,128)(2,1)}, u32[]{:S(2)}) copy-start(bf16[320,384]{1,0:T(8,128)(2,1)} %constant.53.clone.z_low) | copy-start | bytes 737284
  25.1 13.6 %copy-start.3 = (bf16[320,384]{1,0:T(8,128)(2,1)S(1)}, bf16[320,384]{1,0:T(8,128)(2,1)}, u32[]{:S(2)}) copy-start(bf16[320,384]{1,0:T(8,128)(2,1)} %constant.52.clone.z_high) | copy-start | bytes 737284
  25.1 13.6 %copy-start.4 = (s32[4]{0:T(128)S(1)}, s32[4]{0:T(128)}, u32[]{:S(2)}) copy-start(s32[4]{0:T(128)} %pad_add_fusion.place) | copy-start | bytes 52
  26.5 14.7 %copy-start.8 = (f32[3,64,512]{2,1,0:T(8,128)}, f32[3,64,512]{2,1,0:T(8,128)S(1)}, u32[]{:S(2)}) copy-start(f32[3,64,512]{2,1,0:T(8,128)S(1)} %slice_select_fusion.1.z_low_in) | copy-start | bytes 1179652
  26.5 12.2 %collective-permute-start.2 = (f32[15,4,512]{2,1,0:T(4,128)S(1)}, f32[15,4,512]{2,1,0:T(4,128)S(1)}, u32[]{:S(2)}, u32[]{:S(2)}) collective-permute-start(f32[15,4,512]{2,1,0:T(4,128)S(1)} %pad_maximum_fusion), channel_id=1, source_target_pairs={{0,1},{1,2},{2,3},{4,5},{5,6},{6,7},{8,9},{9,10},{10,11},{12,13},{... | collective-permute-start | bytes 368648 | tf_op jit(solution)/shard_map/ppermute | solution.py:488
  29.9 8.8 %collective-permute-start.3 = (f32[15,4,512]{2,1,0:T(4,128)S(1)}, f32[15,4,512]{2,1,0:T(4,128)S(1)}, u32[]{:S(2)}, u32[]{:S(2)}) collective-permute-start(f32[15,4,512]{2,1,0:T(4,128)S(1)} %pad_maximum_fusion.1), channel_id=1, source_target_pairs={{1,0},{2,1},{3,2},{5,4},{6,5},{7,6},{9,8},{10,9},{11,10},{13,12},{... | collective-permute-start | bytes 368648 | tf_op jit(solution)/shard_map/ppermute | solution.py:489
  38.7 11.9 %copy-start.9 = (f32[15,4,512]{2,1,0:T(4,128)}, f32[15,4,512]{2,1,0:T(4,128)S(1)}, u32[]{:S(2)}) copy-start(f32[15,4,512]{2,1,0:T(4,128)S(1)} %collective-permute-done.2.y_low_in) | copy-start | bytes 368644
  38.7 11.9 %copy-start.10 = (f32[15,4,512]{2,1,0:T(4,128)}, f32[15,4,512]{2,1,0:T(4,128)S(1)}, u32[]{:S(2)}) copy-start(f32[15,4,512]{2,1,0:T(4,128)S(1)} %collective-permute-done.3.y_high_in) | copy-start | bytes 368644
  41.2 21.4 %all-to-all-start.1 = ((f32[64,8,128]{2,1,0:T(8,128)}), f32[64,8,128]{2,1,0:T(8,128)S(1)}, u32[]{:S(2)}, u32[]{:S(2)}) async-start(f32[64,8,128]{2,1,0:T(8,128)} %bitcast.6), calls=%async_computation.1 | async-start | bytes 524288 | tf_op jit(solution)/shard_map/all_to_all | solution.py:504
  62.6 0.7 copy-start.5

commit v7 on v6

--- a/solution.py
+++ b/solution.py
@@ -26,7 +26,7 @@
 TILES = 16
 ROWS = 384
 STEP = 8
-PIECES = 8
+PIECES = 24
 
 F32, BF16 = jnp.float32, jnp.bfloat16
 
@@ -148,12 +148,29 @@
 CONSTANTS = make_constants()
 
 
-def restrict_kernel(place, charge, along_x, along_zy, out):
-    values = charge[...].reshape(CZ * CY, NX)
-    high, low = split(values)
-    narrow = dot(high, along_x[...]) + dot(low, along_x[...])
-    narrow_high, narrow_low = split(narrow.T)
-    zy_high, zy_low = split(along_zy[0])
+def slab_kind(p):
+    return jnp.where(p == 0, 0, jnp.where(p == SLABS - 1, 2, 1))
+
+
+def restrict_kernel(charge_in, along_x_in, along_zy_in, out, charge, along_x, along_zy, sems):
+    mine = slab_kind(lax.axis_index("slab")) * SUBS + lax.axis_index("sub")
+    half = CZ // 2
+    first, second = pl.ds(0, half), pl.ds(half, half)
+    copies = fetch(
+        (along_x_in, charge_in.at[first], along_zy_in.at[mine], charge_in.at[second]),
+        (along_x, charge.at[first], along_zy, charge.at[second]),
+        sems,
+    )
+    copies[0].wait()
+    narrow = []
+    for part, copy in enumerate((copies[1], copies[3])):
+        copy.wait()
+        values = charge[half * part : half * (part + 1)].reshape(half * CY, NX)
+        high, low = split(values)
+        narrow.append((dot(high, along_x[...]) + dot(low, along_x[...])).T)
+    copies[2].wait()
+    narrow_high, narrow_low = split(jnp.concatenate(narrow, axis=1))
+    zy_high, zy_low = split(along_zy[...])
     partial = dot3(narrow_high, narrow_low, zy_high, zy_low)
     for x in range(2):
         for q in range(SUBS):
@@ -427,10 +444,6 @@
         copy(i).wait()
 
 
-def whole(shape):
-    return pl.BlockSpec(shape, lambda i, *_: (0,) * len(shape))
-
-
 IN_VMEM = pl.BlockSpec(memory_space=pltpu.VMEM)
 IN_SMEM = pl.BlockSpec(memory_space=pltpu.SMEM)
 ANYWHERE = pl.BlockSpec(memory_space=pl.ANY)
@@ -451,7 +464,7 @@
 def on_device(charge_grid, atom_offset, block_cell, block_count):
     consts = CONSTANTS
     p, q = lax.axis_index("slab"), lax.axis_index("sub")
-    kind = jnp.where(p == 0, 0, jnp.where(p == SLABS - 1, 2, 1))
+    kind = slab_kind(p)
     place = jnp.stack([p, q, kind, kind * SUBS + q]).astype(jnp.int32)
 
     up_sub = [(i, i + 1) for i in range(SUBS - 1)]
@@ -461,22 +474,23 @@
     outer = [(i, i + 1 if i % 2 else i - 1) for i in range(1, SLABS - 1)]
     twin = lax.ppermute(charge_grid, "slab", inner)
     other = lax.ppermute(charge_grid, "slab", outer)
-    partial = pl.pallas_call(
+    partial = call(
         restrict_kernel,
-        grid_spec=pltpu.PrefetchScalarGridSpec(
-            num_scalar_prefetch=1,
-            grid=(1,),
-            in_specs=[
-                whole((CZ, CY, NX)),
-                whole((NX, 128)),
-                pl.BlockSpec((1, CZ * CY, 128), lambda i, place: (place[3], 0, 0)),
-            ],
-            out_specs=whole((512, 128)),
-        ),
-        out_shape=jax.ShapeDtypeStruct((512, 128), F32),
-        compiler_params=pltpu.CompilerParams(vmem_limit_bytes=60 * 2**20),
-        cost_estimate=pl.CostEstimate(flops=10**8, bytes_accessed=10**6, transcendentals=0),
-    )(place, charge_grid, consts["restrict_x"], consts["restrict_zy"])
+        [],
+        [],
+        [charge_grid, consts["restrict_x"], consts["restrict_zy"]],
+        (512, 128),
+        IN_VMEM,
+        [
+            pltpu.VMEM((CZ, CY, NX), F32),
+            pltpu.VMEM((NX, 128), BF16),
+            pltpu.VMEM((CZ * CY, 128), F32),
+            pltpu.SemaphoreType.DMA((4,)),
+        ],
+        60,
+        10**8,
+        10**6,
+    )
     pencil = lax.all_to_all(partial, ("slab", "sub"), 0, 0, tiled=True)
 
     odd = p % 2 == 1

time: 78.9 us -> 76.4 us (0.968)
  Pallas kernels: 29.2 us -> 27.3 us
    pallas_call x1 -> x0, Pallas kernels: 3.57 us -> none  [on_device(): pl.pallas_call(restrict_kernel, grid_spec=pltpu.PrefetchScalarGridSpec(nu...]
    pallas_call x3 -> x4, Pallas kernels: 25.6 us -> 27.3 us  [call(): pl.pallas_call(kernel, in_specs=[IN_SMEM] * len(scalars) + [IN_VMEM] * le...]
  transfers between devices with their start and end apart: 6 -> 6, of which waited for: 2 -> 2; matrix products, arithmetic and copies ran while one was open for 4% -> 3% of each run, Pallas kernels for 15% -> 14%
where the time goes in v7:
time: 76.4 us; the launch traced here: 76 us
  starting transfers between devices  32.8 us (43%)
  Pallas kernels  27.3 us (36%)
  waiting for transfers between devices  11.3 us (15%)
  local copies, waits for them, and re-layouts  2.75 us (4%)
  other arithmetic  1.49 us (2%)
    pallas_call x4, Pallas kernels, call(): pl.pallas_call(kernel, in_specs=[IN_SMEM] * len(scalars) + [IN_VMEM] * le...  27.3 us
    all_to_all x1, starting transfers between devices, on_device(): pencil = lax.all_to_all(partial, ('slab', 'sub'), 0, 0, tiled=True)  13.8 us
    all_to_all x1, starting transfers between devices, on_device(): arrived = lax.all_to_all(folded, 'slab', 0, 0, tiled=True)  9.41 us
    all_to_all x1, waiting for transfers between devices, on_device(): pencil = lax.all_to_all(partial, ('slab', 'sub'), 0, 0, tiled=True)  7.43 us
    ppermute x1, starting transfers between devices, on_device(): other = lax.ppermute(charge_grid, 'slab', outer)  4.93 us
    all_to_all x1, waiting for transfers between devices, on_device(): arrived = lax.all_to_all(folded, 'slab', 0, 0, tiled=True)  3.84 us
    ppermute x1, starting transfers between devices, on_device(): left = lax.ppermute(left, 'sub', up_sub)  3.3 us
    unnamed x22, local copies, waits for them, and re-layouts  1.73 us
  transfers between devices with their start and end apart: 6, of which 2 were waited for; matrix products, arithmetic and copies ran while one was open for 3% of the time, Pallas kernels for 14%

profile of v7, /device:TPU:1, one launch (start us, length us, event | category | flops | bytes accessed | tf_op | source)
XLA Modules:
  0.0 76.0 jit_solution(7143372810679342680)
XLA Ops:
  0.0 4.9 %collective-permute-start.1 = (f32[8,64,512]{2,1,0:T(8,128)}, f32[8,64,512]{2,1,0:T(8,128)S(1)}, u32[]{:S(2)}, u32[]{:S(2)}) collective-permute-start(f32[8,64,512]{2,1,0:T(8,128)} %charge_in.3), channel_id=1, source_target_pairs={{4,8},{8,4},{12,16},{16,12},{20,24},{24,20},{28,32},{32,28},{36,40... | collective-permute-start | bytes 3145736 | tf_op jit(solution)/shard_map/ppermute | solution.py:476
  4.9 0.1 collective-permute-start
  5.0 2.9 %shard_map.136 = f32[512,128]{1,0:T(8,128)} custom-call(f32[8,64,512]{2,1,0:T(8,128)} %charge_in.3, bf16[512,128]{1,0:T(8,128)(2,1)} %constant.48.clone.along_x_in, f32[12,512,128]{2,1,0:T(8,128)} %constant.49.clone.along_zy_in), custom_call_target="tpu_custom_call" | custom-call | flops 100000000 | bytes 1000000 | tf_op jit(solution)/shard_map/pallas_call | solution.py:453
  7.9 13.8 %all-to-all-start = ((f32[256,2,128]{2,1,0:T(2,128)}), f32[256,2,128]{2,1,0:T(2,128)S(1)}, u32[]{:S(2)}, u32[]{:S(2)}) async-start(f32[256,2,128]{2,1,0:T(2,128)} %bitcast.9), calls=%async_computation | async-start | bytes 524288 | tf_op jit(solution)/shard_map/all_to_all | solution.py:494
  21.7 1.0 %fusion = (f32[8,4,512]{2,1,0:T(4,128)S(1)}, f32[8,4,512]{2,1,0:T(4,128)S(1)}) fusion(f32[8,64,512]{2,1,0:T(8,128)} %charge_in.3), kind=kLoop, calls=%fused_computation.5 | loop fusion | bytes 262144 | tf_op jit(solution)/shard_map/slice | solution.py:501
  22.7 0.0 collective-permute-done.1
  22.7 0.0 collective-permute-done
  22.7 0.0 copy-start.6
  22.7 1.0 %copy-done.6 = f32[8,64,512]{2,1,0:T(8,128)} copy-done((f32[8,64,512]{2,1,0:T(8,128)}, f32[8,64,512]{2,1,0:T(8,128)S(1)}, u32[]{:S(2)}) %copy-start.6) | copy-done | bytes 1048600
  23.7 0.1 slice_select_fusion.z_high_in
  23.8 0.0 copy-start.7
  23.8 0.0 copy-start
  23.8 0.0 copy-start.1
  23.8 0.0 copy-start.2
  23.8 0.0 copy-start.3
  23.9 1.3 %slice_select_fusion.1.z_low_in = f32[3,64,512]{2,1,0:T(8,128)S(1)} fusion(f32[8,64,512]{2,1,0:T(8,128)S(1)} %collective-permute-done.1, f32[8,64,512]{2,1,0:T(8,128)} %copy-done.6, pred[]{:T(512)S(6)} %eq.13), kind=kLoop, calls=%fused_computation.1 | loop fusion | flops 98304 | bytes 1179649 | tf_op jit(solution)/shard_map/jit(_where)/select_n | solution.py:497
  25.1 0.0 copy-start.8
  25.2 3.3 %collective-permute-start.2 = (f32[15,4,512]{2,1,0:T(4,128)S(1)}, f32[15,4,512]{2,1,0:T(4,128)S(1)}, u32[]{:S(2)}, u32[]{:S(2)}) collective-permute-start(f32[15,4,512]{2,1,0:T(4,128)S(1)} %pad_maximum_fusion), channel_id=1, source_target_pairs={{0,1},{1,2},{2,3},{4,5},{5,6},{6,7},{8,9},{9,10},{10,11},{12,13},{... | collective-permute-start | bytes 368648 | tf_op jit(solution)/shard_map/ppermute | solution.py:502
  28.6 1.3 %collective-permute-start.3 = (f32[15,4,512]{2,1,0:T(4,128)S(1)}, f32[15,4,512]{2,1,0:T(4,128)S(1)}, u32[]{:S(2)}, u32[]{:S(2)}) collective-permute-start(f32[15,4,512]{2,1,0:T(4,128)S(1)} %pad_maximum_fusion.1), channel_id=1, source_target_pairs={{1,0},{2,1},{3,2},{5,4},{6,5},{7,6},{9,8},{10,9},{11,10},{13,12},{... | collective-permute-start | bytes 368648 | tf_op jit(solution)/shard_map/ppermute | solution.py:503
  29.9 0.1 pad_add_fusion.place
  29.9 0.0 copy-start.4
  29.9 7.4 %all-to-all-done = f32[256,2,128]{2,1,0:T(2,128)S(1)} async-done(((f32[256,2,128]{2,1,0:T(2,128)}), f32[256,2,128]{2,1,0:T(2,128)S(1)}, u32[]{:S(2)}, u32[]{:S(2)}) %all-to-all-start) | async-done | bytes 262176 | tf_op jit(solution)/shard_map/all_to_all | solution.py:494
  37.4 0.0 collective-permute-done.2.y_low_in
  37.4 0.0 copy-start.9
  37.4 0.0 collective-permute-done.3.y_high_in
  37.4 0.0 copy-start.10
  37.4 0.0 copy-done
  37.4 0.0 copy-done.1
  37.4 0.0 copy-done.2
  37.4 0.0 copy-done.3
  37.4 2.4 %shard_map.137 = f32[512,128]{1,0:T(8,128)} custom-call(s32[4]{0:T(128)S(1)} %pad_add_fusion.place, f32[512,128]{1,0:T(8,128)S(1)} %bitcast.8, bf16[4,128,384]{2,1,0:T(8,128)(2,1)S(1)} %copy-done.1, bf16[4,128,384]{2,1,0:T(8,128)(2,1)S(1)} %copy-done, bf16[320,384]{1,0:T(8,128)(2,1)S(1)} %copy-done.3, bf16[320,384]{1,0:T(8,128)(2,1)S(1)} %copy-done.2), custom_call_target="tpu_custom_call" | custom-call | flops 200000000 | bytes 2000000 | tf_op jit(solution)/shard_map/pallas_call | solution.py:453
  39.9 0.0 copy-done.7
  39.9 0.0 copy-done.8
  39.9 9.4 %all-to-all-start.1 = ((f32[64,8,128]{2,1,0:T(8,128)}), f32[64,8,128]{2,1,0:T(8,128)S(1)}, u32[]{:S(2)}, u32[]{:S(2)}) async-start(f32[64,8,128]{2,1,0:T(8,128)} %bitcast.6), calls=%async_computation.1 | async-start | bytes 524288 | tf_op jit(solution)/shard_map/all_to_all | solution.py:518
  49.3 0.0 copy-done.4
  49.3 0.0 copy-done.9
  49.3 0.0 copy-done.10
  49.3 8.1 %shard_map.138.near_in = f32[1152,640]{1,0:T(8,128)} custom-call(s32[4]{0:T(128)} %copy-done.4, f32[8,64,512]{2,1,0:T(8,128)} %charge_in.3, f32[3,64,512]{2,1,0:T(8,128)} %copy-done.8, f32[4,64,512]{2,1,0:T(8,128)} %copy-done.7, f32[15,4,512]{2,1,0:T(4,128)} %copy-done.9, f32[15,4,512]{2,1,0:T(4,128)} %copy-done.10, bf16[1024,640]{1,0:T(8,128)(2,1)} %constant.54.clone.along_x_in), custom_call_target="tpu_custom_call" | custom-call | flops 2000000000 | bytes 16000000 | tf_op jit(solution)/shard_map/pallas_call | solution.py:453
  57.5 3.8 %all-to-all-done.1 = f32[64,8,128]{2,1,0:T(8,128)S(1)} async-done(((f32[64,8,128]{2,1,0:T(8,128)}), f32[64,8,128]{2,1,0:T(8,128)S(1)}, u32[]{:S(2)}, u32[]{:S(2)}) %all-to-all-start.1) | async-done | bytes 262176 | tf_op jit(solution)/shard_map/all_to_all | solution.py:518
  61.3 0.0 copy-start.5
  61.3 0.7 copy-done.5
  62.0 13.9 %shard_map.139 = f32[4,16384]{1,0:T(4,128)} custom-call(s32[4]{0:T(128)} %copy-done.4, s32[128]{0:T(128)} %cell.1, s32[128]{0:T(128)} %count.1, f32[512,128]{1,0:T(8,128)} %bitcast.10, f32[1152,640]{1,0:T(8,128)} %shard_map.138.near_in, bf16[1024,640]{1,0:T(8,128)(2,1)} %constant.55.clone.along_x_in, bf16[4,1152,128]{2,1,0:T(8,128)(2,1)} %constant.56.clone.along_y_in, ...), custom_call_target="tpu_custom_call" | custom-call | flops 1000000000 | bytes 8000000 | tf_op jit(solution)/shard_map/pallas_call | solution.py:453
  (4 shorter events, 0.1 us)
Async XLA Ops:
  0.0 22.7 %collective-permute-start.1 = (f32[8,64,512]{2,1,0:T(8,128)}, f32[8,64,512]{2,1,0:T(8,128)S(1)}, u32[]{:S(2)}, u32[]{:S(2)}) collective-permute-start(f32[8,64,512]{2,1,0:T(8,128)} %charge_in.3), channel_id=1, source_target_pairs={{4,8},{8,4},{12,16},{16,12},{20,24},{24,20},{28,32},{32,28},{36,40... | collective-permute-start | bytes 3145736 | tf_op jit(solution)/shard_map/ppermute | solution.py:476
  4.9 17.8 %collective-permute-start = (f32[8,64,512]{2,1,0:T(8,128)}, f32[8,64,512]{2,1,0:T(8,128)S(1)}, u32[]{:S(2)}, u32[]{:S(2)}) collective-permute-start(f32[8,64,512]{2,1,0:T(8,128)} %charge_in.3), channel_id=1, source_target_pairs={{0,4},{4,0},{8,12},{12,8},{16,20},{20,16},{24,28},{28,24},{32,36},... | collective-permute-start | bytes 3145736 | tf_op jit(solution)/shard_map/ppermute | solution.py:475
  7.9 29.5 %all-to-all-start = ((f32[256,2,128]{2,1,0:T(2,128)}), f32[256,2,128]{2,1,0:T(2,128)S(1)}, u32[]{:S(2)}, u32[]{:S(2)}) async-start(f32[256,2,128]{2,1,0:T(2,128)} %bitcast.9), calls=%async_computation | async-start | bytes 524288 | tf_op jit(solution)/shard_map/all_to_all | solution.py:494
  22.7 1.0 %copy-start.6 = (f32[8,64,512]{2,1,0:T(8,128)}, f32[8,64,512]{2,1,0:T(8,128)S(1)}, u32[]{:S(2)}) copy-start(f32[8,64,512]{2,1,0:T(8,128)S(1)} %collective-permute-done) | copy-start | bytes 3145732
  23.8 16.1 %copy-start.7 = (f32[4,64,512]{2,1,0:T(8,128)}, f32[4,64,512]{2,1,0:T(8,128)S(1)}, u32[]{:S(2)}) copy-start(f32[4,64,512]{2,1,0:T(8,128)S(1)} %slice_select_fusion.z_high_in) | copy-start | bytes 1572868
  23.8 13.6 %copy-start = (bf16[4,128,384]{2,1,0:T(8,128)(2,1)S(1)}, bf16[4,128,384]{2,1,0:T(8,128)(2,1)}, u32[]{:S(2)}) copy-start(bf16[4,128,384]{2,1,0:T(8,128)(2,1)} %constant.51.clone.y_low) | copy-start | bytes 1179652
  23.8 13.6 %copy-start.1 = (bf16[4,128,384]{2,1,0:T(8,128)(2,1)S(1)}, bf16[4,128,384]{2,1,0:T(8,128)(2,1)}, u32[]{:S(2)}) copy-start(bf16[4,128,384]{2,1,0:T(8,128)(2,1)} %constant.50.clone.y_high) | copy-start | bytes 1179652
  23.8 13.6 %copy-start.2 = (bf16[320,384]{1,0:T(8,128)(2,1)S(1)}, bf16[320,384]{1,0:T(8,128)(2,1)}, u32[]{:S(2)}) copy-start(bf16[320,384]{1,0:T(8,128)(2,1)} %constant.53.clone.z_low) | copy-start | bytes 737284
  23.8 13.6 %copy-start.3 = (bf16[320,384]{1,0:T(8,128)(2,1)S(1)}, bf16[320,384]{1,0:T(8,128)(2,1)}, u32[]{:S(2)}) copy-start(bf16[320,384]{1,0:T(8,128)(2,1)} %constant.52.clone.z_high) | copy-start | bytes 737284
  25.1 14.7 %copy-start.8 = (f32[3,64,512]{2,1,0:T(8,128)}, f32[3,64,512]{2,1,0:T(8,128)S(1)}, u32[]{:S(2)}) copy-start(f32[3,64,512]{2,1,0:T(8,128)S(1)} %slice_select_fusion.1.z_low_in) | copy-start | bytes 1179652
  25.2 12.2 %collective-permute-start.2 = (f32[15,4,512]{2,1,0:T(4,128)S(1)}, f32[15,4,512]{2,1,0:T(4,128)S(1)}, u32[]{:S(2)}, u32[]{:S(2)}) collective-permute-start(f32[15,4,512]{2,1,0:T(4,128)S(1)} %pad_maximum_fusion), channel_id=1, source_target_pairs={{0,1},{1,2},{2,3},{4,5},{5,6},{6,7},{8,9},{9,10},{10,11},{12,13},{... | collective-permute-start | bytes 368648 | tf_op jit(solution)/shard_map/ppermute | solution.py:502
  28.6 8.8 %collective-permute-start.3 = (f32[15,4,512]{2,1,0:T(4,128)S(1)}, f32[15,4,512]{2,1,0:T(4,128)S(1)}, u32[]{:S(2)}, u32[]{:S(2)}) collective-permute-start(f32[15,4,512]{2,1,0:T(4,128)S(1)} %pad_maximum_fusion.1), channel_id=1, source_target_pairs={{1,0},{2,1},{3,2},{5,4},{6,5},{7,6},{9,8},{10,9},{11,10},{13,12},{... | collective-permute-start | bytes 368648 | tf_op jit(solution)/shard_map/ppermute | solution.py:503
  29.9 19.4 %copy-start.4 = (s32[4]{0:T(128)}, s32[4]{0:T(128)S(1)}, u32[]{:S(2)}) copy-start(s32[4]{0:T(128)S(1)} %pad_add_fusion.place) | copy-start | bytes 52
  37.4 11.9 %copy-start.9 = (f32[15,4,512]{2,1,0:T(4,128)}, f32[15,4,512]{2,1,0:T(4,128)S(1)}, u32[]{:S(2)}) copy-start(f32[15,4,512]{2,1,0:T(4,128)S(1)} %collective-permute-done.2.y_low_in) | copy-start | bytes 368644
  37.4 11.9 %copy-start.10 = (f32[15,4,512]{2,1,0:T(4,128)}, f32[15,4,512]{2,1,0:T(4,128)S(1)}, u32[]{:S(2)}) copy-start(f32[15,4,512]{2,1,0:T(4,128)S(1)} %collective-permute-done.3.y_high_in) | copy-start | bytes 368644
  39.9 21.4 %all-to-all-start.1 = ((f32[64,8,128]{2,1,0:T(8,128)}), f32[64,8,128]{2,1,0:T(8,128)S(1)}, u32[]{:S(2)}, u32[]{:S(2)}) async-start(f32[64,8,128]{2,1,0:T(8,128)} %bitcast.6), calls=%async_computation.1 | async-start | bytes 524288 | tf_op jit(solution)/shard_map/all_to_all | solution.py:518
  61.3 0.7 copy-start.5
